TPU v7x, 512 devices: a whole 4x4x16 slice. The times are simulated.
512 devices in a mesh: group: 2 (over core), ep: 128 (over z_lo, x, y), tp: 2 (over z_hi).
Axes of the slice: x: 4, y: 4, z: 16 (z_hi: 2, z_lo: 8; z = z_hi * 8 + z_lo), core: 2. Of those that a mesh axis runs over, the one named last changes fastest.
Arguments:
- queries: bfloat16 [512, 4, 128, 576], P(('group', 'ep'), None, 'tp'), may hold values from -60 to 60, as said below
- step_rows: bfloat16 [512, 4, 576], P(('group', 'ep')), may hold values from -6 to 6
- cache: bfloat16 [256, 512, 576], P(('group', 'ep')), may hold values from -6 to 6
- lengths: int32 [256], P(('group', 'ep')), may hold values from 2 to 512, as said below
- outgoing: bfloat16 [65536, 576], P(('group', 'ep')), may hold values from -6 to 6
- crossing: int32 [65536], P(('group', 'ep')), may hold values from 0 to 127, as said below
Outputs:
- attended: bfloat16 [512, 4, 128, 512], P(('group', 'ep'), None, 'tp')
Inputs may be any that keep to these rules, and one draw needn't show every extreme that they name: `queries`: query entries. `lengths`: some entry equals 512. `crossing`: split each device's 256 entries into 2 equal runs in order; each run names every decode device index exactly once.
All inputs are finite; a program needn't handle non-finite values.
Results may differ from a plain program's by a relative error of at most 0.0029.
Values may be sent and summed in bfloat16 or wider, within the bound.
No kernel may reach another device: no remote copies, remote signals or barrier semaphores. Data moves between devices by JAX's collectives and lax.ppermute only.
A program may use at most 64 MiB of HBM per device.

v0:
```python
import jax
import jax.numpy as jnp
from jax import lax
from jax.sharding import PartitionSpec as P

KV_RANK = 512


score_scale = 192.0 ** (-0.5)
masked_score = -1e30


def passed_along(value, axis, by):
    devices = lax.axis_size(axis)
    pairs = [(i, i + by) for i in range(devices) if 0 <= i + by < devices]
    return lax.ppermute(value, axis, pairs)


def bucket_rows(latent_rows, owners, peer_count):
    row_total = latent_rows.shape[0]
    per_peer = row_total // peer_count
    owner_table = (owners[:, None] == jnp.arange(peer_count, dtype=jnp.int32)[None, :]).astype(
        jnp.int32
    )
    owner_rank = jnp.sum((jnp.cumsum(owner_table, axis=0) - 1) * owner_table, axis=1)
    slot_index = owners * per_peer + owner_rank
    packed = jnp.zeros_like(latent_rows).at[slot_index].set(latent_rows)
    return packed.reshape(peer_count, per_peer, latent_rows.shape[1])


def tail_scores_of(flat_query, step_keys, head_count):
    scores = (
        jnp.einsum("qd,kd->qk", flat_query, step_keys, preferred_element_type=jnp.float32)
        * score_scale
    )
    query_step = jnp.arange(flat_query.shape[0], dtype=jnp.int32)[:, None] // head_count
    key_step = jnp.arange(step_keys.shape[0], dtype=jnp.int32)[None, :]
    return jnp.where(key_step <= query_step, scores, masked_score)


def softmax_mix(base_scores, tail_scores, base_keys, step_keys):
    peak = jnp.maximum(
        jnp.max(base_scores, axis=1, keepdims=True), jnp.max(tail_scores, axis=1, keepdims=True)
    )
    base_expo = jnp.exp(base_scores - peak)
    tail_expo = jnp.exp(tail_scores - peak)
    total = jnp.sum(base_expo, axis=1, keepdims=True) + jnp.sum(tail_expo, axis=1, keepdims=True)
    mixed = jnp.dot(
        base_expo.astype(jnp.bfloat16), base_keys[:, :KV_RANK], preferred_element_type=jnp.float32
    )
    mixed = mixed + jnp.dot(
        tail_expo.astype(jnp.bfloat16), step_keys[:, :KV_RANK], preferred_element_type=jnp.float32
    )
    return mixed / total


def base_scores_of(flat_query, base_keys, live_rows):
    scores = (
        jnp.einsum("qd,kd->qk", flat_query, base_keys, preferred_element_type=jnp.float32)
        * score_scale
    )
    return jnp.where(live_rows[None, :], scores, masked_score)


def shards(queries, step_rows, cache, lengths, outgoing, crossing):
    seq_count, steps_total, head_count, latent_width = queries.shape
    peer_count = lax.axis_size("ep")
    run_rows = outgoing.shape[0] // lax.axis_size("tp")
    run_start = lax.axis_index("tp") * run_rows
    run_latents = lax.dynamic_slice_in_dim(outgoing, run_start, run_rows, 0)
    run_owners = lax.dynamic_slice_in_dim(crossing, run_start, run_rows, 0)
    packed = bucket_rows(run_latents, run_owners, peer_count)
    moved = lax.all_to_all(packed, "ep", split_axis=0, concat_axis=0, tiled=True)
    landed = passed_along(moved, "group", 1)
    arrived = lax.all_gather(landed, "tp", axis=0, tiled=True)
    arrived = arrived.reshape(-1, latent_width)
    decode_flag = lax.axis_index("group") == 1
    resident_count = cache.shape[0]
    cache_len = cache.shape[1]
    positions = jnp.arange(cache_len, dtype=jnp.int32)
    results = []
    flat_query = queries[0].reshape(steps_total * head_count, latent_width)
    step_keys = step_rows[0]
    tail_scores = tail_scores_of(flat_query, step_keys, head_count)
    live_rows = positions < lengths[0]
    base_scores = base_scores_of(flat_query, cache[0], live_rows)
    mixed = softmax_mix(base_scores, tail_scores, cache[0], step_keys)
    results.append(mixed)
    flat_query = queries[resident_count].reshape(steps_total * head_count, latent_width)
    step_keys = step_rows[resident_count]
    tail_scores = tail_scores_of(flat_query, step_keys, head_count)
    arrive_live = jnp.broadcast_to(decode_flag, (arrived.shape[0],))
    base_scores = base_scores_of(flat_query, arrived, arrive_live)
    results.append(softmax_mix(base_scores, tail_scores, arrived, step_keys))
    shaped = [
        mixed_rows.astype(jnp.bfloat16).reshape(steps_total, head_count, KV_RANK)
        for mixed_rows in results
    ]
    return jnp.stack(shaped)


def solution(mesh):
    placed = (
        P(("group", "ep"), None, "tp", None),
        P(("group", "ep"), None, None),
        P(("group", "ep"), None, None),
        P(("group", "ep")),
        P(("group", "ep"), None),
        P(("group", "ep")),
    )
    return jax.shard_map(
        shards,
        mesh=mesh,
        in_specs=placed,
        out_specs=P(("group", "ep"), None, "tp", None),
        check_vma=False,
    )
```

profile of v0, /device:TPU:1, one launch (start us, length us, event | category | flops | bytes accessed | tf_op | source)
XLA Modules:
  0.0 72.2 jit_solution(9753416540142722765)
XLA Ops:
  0.0 0.0 copy-start
  0.0 0.0 copy-start.4
  0.0 0.7 %copy-done.4 = s32[256]{0:T(256)S(1)} copy-done((s32[256]{0:T(256)S(1)}, s32[256]{0:T(256)}, u32[]{:S(2)}) %copy-start.4) | copy-done | bytes 1048
  0.7 0.1 dynamic_slice.6
  0.8 0.1 fusion.21
  0.9 0.2 reduce_window_sum.11
  1.1 0.2 select_reduce_fusion
  1.2 0.1 compare_select_fusion
  1.3 0.0 copy-done
  1.3 0.2 copy.10
  1.5 0.0 copy-start.1
  1.5 1.1 %scatter_custom_fusion = bf16[128,576]{1,0:T(8,128)(2,1)S(1)} fusion(s32[128]{0:T(128)S(1)} %compare_select_fusion, bf16[128,576]{1,0:T(8,128)(2,1)S(1)} %copy.10, bf16[]{:T(256)} %constant.51.clone.1), kind=kCustom, calls=%fused_computation.27 | custom fusion | bytes 147458 | tf_op jit(solution)/shard_map/scatter | solution.py:27
  2.7 0.5 broadcast.71
  3.2 0.7 reduce.2
  3.9 0.9 %reshape.85 = bf16[128,2,288]{2,1,0:T(2,128)(2,1)} reshape(bf16[128,576]{1,0:T(8,128)(2,1)S(1)} %reduce.2) | data formatting | bytes 294912
  4.8 20.4 %all-to-all-start = ((bf16[128,2,288]{2,1,0:T(2,128)(2,1)}), bf16[128,2,288]{2,1,0:T(2,128)(2,1)S(1)}, u32[]{:S(2)}, u32[]{:S(2)}) async-start(bf16[128,2,288]{2,1,0:T(2,128)(2,1)} %reshape.85), calls=%async_computation | async-start | bytes 393216 | tf_op jit(solution)/shard_map/all_to_all | solution.py:73
  25.2 0.0 copy-start.3
  25.9 0.0 copy-done.3
  25.9 0.0 copy-done.1
  25.9 0.0 copy-start.2
  25.9 0.1 fusion.35
  26.0 0.2 fusion.39
  26.2 0.8 %copy-done.2 = bf16[1,512,576]{1,2,0:T(8,128)(2,1)S(1)} copy-done((bf16[1,512,576]{1,2,0:T(8,128)(2,1)S(1)}, bf16[1,512,576]{1,2,0:T(8,128)(2,1)}, u32[]{:S(2)}) %copy-start.2) | copy-done | bytes 589848
  27.0 0.4 fusion.38
  27.4 0.2 fusion.10
  27.7 0.4 fusion.8
  28.0 0.3 fusion.3
  28.3 11.4 %all-to-all-done = bf16[128,2,288]{2,1,0:T(2,128)(2,1)S(1)} async-done(((bf16[128,2,288]{2,1,0:T(2,128)(2,1)}), bf16[128,2,288]{2,1,0:T(2,128)(2,1)S(1)}, u32[]{:S(2)}, u32[]{:S(2)}) %all-to-all-start) | async-done | bytes 147488 | tf_op jit(solution)/shard_map/all_to_all | solution.py:73
  39.8 0.3 reshape.86
  40.0 0.2 copy.12
  40.2 1.3 %collective-permute-start = (bf16[128,1,576]{0,2,1:T(8,128)(2,1)S(1)}, bf16[128,1,576]{0,2,1:T(8,128)(2,1)S(1)}, u32[]{:S(2)}, u32[]{:S(2)}) collective-permute-start(bf16[128,1,576]{0,2,1:T(8,128)(2,1)S(1)} %copy.12), channel_id=1, source_target_pairs={{0,256},{1,257},{2,258},{3,259},{4,260},{5,261},{6,262},{7,263},{8... | collective-permute-start | bytes 442376 | tf_op jit(solution)/shard_map/ppermute | solution.py:16
  41.5 0.2 fusion.37
  41.8 5.1 %collective-permute-done = bf16[128,1,576]{0,2,1:T(8,128)(2,1)S(1)} collective-permute-done((bf16[128,1,576]{0,2,1:T(8,128)(2,1)S(1)}, bf16[128,1,576]{0,2,1:T(8,128)(2,1)S(1)}, u32[]{:S(2)}, u32[]{:S(2)}) %collective-permute-start) | collective-permute-done | bytes 147488 | tf_op jit(solution)/shard_map/ppermute | solution.py:16
  46.9 23.4 %all_gather.3 = bf16[256,1,576]{0,2,1:T(8,128)(2,1)S(1)} all-gather(bf16[128,1,576]{0,2,1:T(8,128)(2,1)S(1)} %collective-permute-done), channel_id=1, replica_groups=mesh['group'=2,'ep'=128,'tp'=2] {'tp'}, dimensions={0}, use_global_device_ids=true | all-gather | bytes 442368 | tf_op jit(solution)/shard_map/all_gather | solution.py:75
  70.3 0.3 fusion.36
  70.7 0.1 fusion.15
  70.7 0.3 fusion.22
  71.0 0.3 fusion.4
  71.3 0.8 %pad_maximum_fusion = bf16[2,4,64,512]{3,2,1,0:T(8,128)(2,1)} fusion(bf16[1,4,64,512]{3,2,1,0:T(8,128)(2,1)S(1)} %bitcast.40, bf16[1,4,64,512]{3,2,1,0:T(8,128)(2,1)S(1)} %bitcast.39), kind=kLoop, calls=%fused_computation.17 | loop fusion | flops 262144 | bytes 1048576 | tf_op jit(solution)/shard_map/stack | solution.py:99
  (10 shorter events, 0.1 us)
Async XLA Ops:
  0.0 1.3 %copy-start = (bf16[256,576]{0,1:T(8,128)(2,1)S(1)}, bf16[256,576]{0,1:T(8,128)(2,1)}, u32[]{:S(2)}) copy-start(bf16[256,576]{0,1:T(8,128)(2,1)} %param.10) | copy-start | bytes 884740
  0.0 0.7 %copy-start.4 = (s32[256]{0:T(256)S(1)}, s32[256]{0:T(256)}, u32[]{:S(2)}) copy-start(s32[256]{0:T(256)} %param.11) | copy-start | bytes 3076
  1.5 24.4 %copy-start.1 = (bf16[2,4,64,576]{3,2,1,0:T(8,128)(2,1)S(1)}, bf16[2,4,64,576]{3,2,1,0:T(8,128)(2,1)}, u32[]{:S(2)}) copy-start(bf16[2,4,64,576]{3,2,1,0:T(8,128)(2,1)} %param.6) | copy-start | bytes 1769476
  4.8 35.0 %all-to-all-start = ((bf16[128,2,288]{2,1,0:T(2,128)(2,1)}), bf16[128,2,288]{2,1,0:T(2,128)(2,1)S(1)}, u32[]{:S(2)}, u32[]{:S(2)}) async-start(bf16[128,2,288]{2,1,0:T(2,128)(2,1)} %reshape.85), calls=%async_computation | async-start | bytes 393216 | tf_op jit(solution)/shard_map/all_to_all | solution.py:73
  25.2 0.7 copy-start.3
  25.9 1.1 %copy-start.2 = (bf16[1,512,576]{1,2,0:T(8,128)(2,1)S(1)}, bf16[1,512,576]{1,2,0:T(8,128)(2,1)}, u32[]{:S(2)}) copy-start(bf16[1,512,576]{1,2,0:T(8,128)(2,1)} %param.8) | copy-start | bytes 1769476
  40.2 6.7 %collective-permute-start = (bf16[128,1,576]{0,2,1:T(8,128)(2,1)S(1)}, bf16[128,1,576]{0,2,1:T(8,128)(2,1)S(1)}, u32[]{:S(2)}, u32[]{:S(2)}) collective-permute-start(bf16[128,1,576]{0,2,1:T(8,128)(2,1)S(1)} %copy.12), channel_id=1, source_target_pairs={{0,256},{1,257},{2,258},{3,259},{4,260},{5,261},{6,262},{7,263},{8... | collective-permute-start | bytes 442376 | tf_op jit(solution)/shard_map/ppermute | solution.py:16
where the time goes:
time: 72.4 us; the launch traced here: 72.2 us
  blocking collectives  23.4 us (32%)
  starting transfers between devices  21.7 us (30%)
  waiting for transfers between devices  16.5 us (23%)
  local copies, waits for them, and re-layouts  4.87 us (7%)
  matrix products  2.44 us (3%)
  other arithmetic  2.41 us (3%)
  between operations  0.84 us (1%)
    all_gather x1, blocking collectives, shards(): arrived = lax.all_gather(landed, 'tp', axis=0, tiled=True)  23.4 us
    all_to_all x1, starting transfers between devices, shards(): lax.all_to_all(packed, 'ep', split_axis=0, concat_axis=0, tiled=True)  20.4 us
    all_to_all x1, waiting for transfers between devices, shards(): lax.all_to_all(packed, 'ep', split_axis=0, concat_axis=0, tiled=True)  11.4 us
    ppermute x1, waiting for transfers between devices, passed_along(): return lax.ppermute(value, axis, pairs)  5.14 us
    unnamed x12, local copies, waits for them, and re-layouts  2.67 us
  transfers between devices with their start and end apart: 2, of which 2 were waited for; matrix products, arithmetic and copies ran while one was open for 3% of the time, Pallas kernels for 0%

commit v1 on v0

v1 whole, which is shorter than its diff:
```python
import jax
import jax.numpy as jnp
from jax import lax
from jax.experimental import pallas as pl
from jax.experimental.pallas import tpu as pltpu
from jax.sharding import Mesh, PartitionSpec as P

KV_RANK = 512
PLANE = 16
LINE = 8

score_scale = 192.0 ** (-0.5)
masked_score = -1e30


def product(left, right, dims):
    return lax.dot_general(left, right, (dims, ((), ())), preferred_element_type=jnp.float32)


def picked(where_one, rows, dims):
    selector = jnp.where(where_one, 1.0, 0.0).astype(jnp.bfloat16)
    return product(selector, rows, dims).astype(jnp.bfloat16)


def pack_kernel(slot_ref, latent_ref, packed_ref):
    count = slot_ref.shape[1]
    rows = lax.broadcasted_iota(jnp.int32, (count, count), 0)
    packed_ref[...] = picked(rows == slot_ref[...], latent_ref[...], ((1,), (1,)))


def attend(query, step_keys, first_step, base_scores, base_mix):
    head_count = query.shape[1]
    query = query.reshape(query.shape[0] * head_count, query.shape[2])
    scores = product(query, step_keys, ((1,), (1,))) * score_scale
    query_step = first_step + lax.broadcasted_iota(jnp.int32, scores.shape, 0) // head_count
    key_step = lax.broadcasted_iota(jnp.int32, scores.shape, 1)
    tail_scores = jnp.where(key_step <= query_step, scores, masked_score)
    base_scores = base_scores(query)
    peak = jnp.maximum(
        jnp.max(base_scores, axis=1, keepdims=True), jnp.max(tail_scores, axis=1, keepdims=True)
    )
    base_expo = jnp.exp(base_scores - peak)
    tail_expo = jnp.exp(tail_scores - peak)
    total = jnp.sum(base_expo, axis=1, keepdims=True) + jnp.sum(tail_expo, axis=1, keepdims=True)
    mixed = base_mix(base_expo.astype(jnp.bfloat16)) + product(
        tail_expo.astype(jnp.bfloat16), step_keys[:, :KV_RANK], ((1,), (0,))
    )
    return (mixed * (1.0 / total)).astype(jnp.bfloat16).reshape(-1, head_count, KV_RANK)


def resident(length, query, step_keys, keys):
    def base_scores(flat_query):
        scores = product(flat_query, keys, ((1,), (0,))) * score_scale
        position = lax.broadcasted_iota(jnp.int32, scores.shape, 1)
        return jnp.where(position < length, scores, masked_score)

    return attend(
        query, step_keys, 0, base_scores, lambda weights: product(weights, keys[:KV_RANK], ((1,), (1,)))
    )


def middle_kernel(length_ref, query_ref, step_ref, cache_ref, moved_ref, first_ref, *part_refs):
    decode = lax.axis_index("group") == 1

    @pl.when(decode)
    def _():
        first_ref[...] = resident(length_ref[0], query_ref[0], step_ref[0], cache_ref[0])

    @pl.when(jnp.logical_not(decode))
    def _():
        count = moved_ref.shape[0]
        rows = lax.broadcasted_iota(jnp.int32, (count, count), 0)
        cols = lax.broadcasted_iota(jnp.int32, (count, count), 1)
        run, plane, ahead = rows % 2, (rows // 2) % PLANE, rows // (2 * PLANE)
        source = (plane * LINE + ahead) * 2 + run
        turned = picked(cols == source, moved_ref[...], ((1,), (0,)))
        step = count // LINE
        for part, part_ref in enumerate(part_refs):
            part_ref[...] = turned[part * step : (part + 1) * step]


def last_kernel(length_ref, query_ref, step_ref, cache_ref, first_ref, *refs):
    part_refs, (out_ref, result, sems) = refs[:LINE], refs[LINE:]
    decode = lax.axis_index("group") == 1

    @pl.when(decode)
    def _():
        pltpu.make_async_copy(first_ref, out_ref.at[0], sems.at[0]).start()

    @pl.when(jnp.logical_not(decode))
    def _():
        result[0] = resident(length_ref[0], query_ref[0], step_ref[0], cache_ref[0])
        pltpu.make_async_copy(result.at[0], out_ref.at[0], sems.at[0]).start()

    keys = jnp.concatenate([ref[...] for ref in part_refs], axis=0)

    def base_scores(flat_query):
        scores = product(flat_query, keys, ((1,), (1,))) * score_scale
        return jnp.where(decode, scores, masked_score)

    half = query_ref.shape[1] // 2
    copies = []
    for part in range(2):
        steps = pl.ds(part * half, half)
        result[1, steps] = attend(
            query_ref[1, steps],
            step_ref[1],
            part * half,
            base_scores,
            lambda weights: product(weights, keys[:, :KV_RANK], ((1,), (0,))),
        )
        copy = pltpu.make_async_copy(
            result.at[1, steps], out_ref.at[1, steps], sems.at[1 + part]
        )
        copy.start()
        copies.append(copy)
    pltpu.make_async_copy(result.at[0], out_ref.at[0], sems.at[0]).wait()
    for copy in copies:
        copy.wait()


vmem = pl.BlockSpec(memory_space=pltpu.VMEM)
smem = pl.BlockSpec(memory_space=pltpu.SMEM)
anywhere = pl.BlockSpec(memory_space=pl.ANY)
params = pltpu.CompilerParams(vmem_limit_bytes=16 << 20)


def step_of(place, ahead):
    if ahead == LINE // 2:
        down = place % LINE >= LINE // 2 or place % 2 == 1
        return -ahead if down else ahead
    return ahead if ahead < LINE // 2 else ahead - LINE


def up_line(rows, ahead):
    line_total, ring = PLANE * LINE * 2, LINE * 2
    pairs = []
    for place in range(ring):
        there = (place + step_of(place, ahead)) % ring
        for plane in range(PLANE):
            source = ((place % LINE) * PLANE + plane) * 2 + place // LINE
            target = ((there % LINE) * PLANE + plane) * 2 + there // LINE
            pairs.append((source, line_total + target))
    return lax.ppermute(rows, ("group", "z", "x", "y", "tp"), pairs)


def shards(queries, step_rows, cache, lengths, outgoing, crossing):
    seq_count, steps_total, head_count, latent_width = queries.shape
    row_total = outgoing.shape[0]
    first_shape = jax.ShapeDtypeStruct((steps_total, head_count, KV_RANK), jnp.bfloat16)
    keys = cache.transpose(0, 2, 1)

    run = jnp.arange(row_total, dtype=jnp.int32) // (row_total // 2)
    ahead = (crossing // PLANE - lax.axis_index("z") + LINE) % LINE
    slots = ((crossing % PLANE) * LINE + ahead) * 2 + run
    packed = pl.pallas_call(
        pack_kernel,
        out_shape=jax.ShapeDtypeStruct((row_total, latent_width), jnp.bfloat16),
        in_specs=[vmem] * 2,
        out_specs=vmem,
        compiler_params=params,
    )(slots.reshape(1, row_total), outgoing.T)
    moved = lax.cond(
        lax.axis_index("group") == 0,
        lambda rows: lax.all_to_all(rows, ("x", "y"), 0, 0, tiled=True),
        lambda rows: rows,
        packed.reshape(PLANE, row_total // PLANE, latent_width),
    )
    first, *parts = pl.pallas_call(
        middle_kernel,
        out_shape=[first_shape]
        + [jax.ShapeDtypeStruct((row_total // LINE, latent_width), jnp.bfloat16)] * LINE,
        in_specs=[smem] + [vmem] * 4,
        out_specs=[vmem] * (1 + LINE),
        compiler_params=params,
    )(lengths, queries, step_rows, keys, moved.reshape(row_total, latent_width))
    arrived = [up_line(parts[ahead], ahead) for ahead in (4, 5, 1, 2, 3, 7, 6, 0)]
    return pl.pallas_call(
        last_kernel,
        out_shape=jax.ShapeDtypeStruct((seq_count,) + first_shape.shape, jnp.bfloat16),
        in_specs=[smem] + [vmem] * (4 + LINE),
        out_specs=anywhere,
        scratch_shapes=[
            pltpu.VMEM((seq_count,) + first_shape.shape, jnp.bfloat16),
            pltpu.SemaphoreType.DMA((3,)),
        ],
        compiler_params=params,
    )(lengths, queries, step_rows, keys, first, *arrived)


def solution(mesh):
    parted = Mesh(mesh.devices.reshape(2, LINE, 4, 4, 2), ("group", "z", "x", "y", "tp"))
    own = ("group", "z", "x", "y")
    placed = (
        P(own, None, "tp", None),
        P(own, None, None),
        P(own, None, None),
        P(own),
        P(own, None),
        P(own),
    )
    return jax.shard_map(
        shards,
        mesh=parted,
        in_specs=placed,
        out_specs=P(own, None, "tp", None),
        check_vma=False,
    )
```

time: 72.4 us -> 43.1 us (0.60)
  blocking collectives: 23.4 us -> 0 us
  starting transfers between devices: 21.7 us -> 10.3 us
  waiting for transfers between devices: 16.5 us -> 26.3 us
  Pallas kernels: 0 us -> 3.2 us
  local copies, waits for them, and re-layouts: 4.87 us -> 2.2 us
  matrix products: 2.44 us -> 0 us
  other arithmetic: 2.41 us -> 0.02 us
    all_gather x1 -> x0, blocking collectives: 23.4 us -> none  [shards(): arrived = lax.all_gather(landed, 'tp', axis=0, tiled=True)]
    ppermute x1 -> x8, waiting for transfers between devices: 5.14 us -> 26.3 us  [up_line(): return lax.ppermute(rows, ('group', 'z', 'x', 'y', 'tp'), pairs)]
    all_to_all x1 -> x0, starting transfers between devices: 20.4 us -> none  [shards(): lax.all_to_all(packed, 'ep', split_axis=0, concat_axis=0, tiled=True)]
    all_to_all x1 -> x0, waiting for transfers between devices: 11.4 us -> none  [shards(): lax.all_to_all(packed, 'ep', split_axis=0, concat_axis=0, tiled=True)]
    ppermute x1 -> x8, starting transfers between devices: 1.29 us -> 10.3 us  [up_line(): return lax.ppermute(rows, ('group', 'z', 'x', 'y', 'tp'), pairs)]
    pallas_call x0 -> x3, Pallas kernels: none -> 3.2 us  [the longest x1 1.72 us: shards(): pl.pallas_call(last_kernel, out_shape=jax.ShapeDtypeStruct((seq_count,) +...]
    dot_general x8 -> x0, matrix products: 2.44 us -> none  [the longest x2 0.78 us: base_scores_of(): jnp.einsum('qd,kd->qk', flat_query, base_keys, preferred_element_type=jnp...]
    scatter x1 -> x0, local copies, waits for them, and re-layouts: 1.15 us -> none  [bucket_rows(): packed = jnp.zeros_like(latent_rows).at[slot_index].set(latent_rows)]
  transfers between devices with their start and end apart: 2 -> 8, of which waited for: 2 -> 5; matrix products, arithmetic and copies ran while one was open for 3% -> 0% of each run, Pallas kernels for 0% -> 0%
where the time goes in v1:
time: 43.1 us; the launch traced here: 42.8 us
  waiting for transfers between devices  26.3 us (61%)
  starting transfers between devices  10.3 us (24%)
  Pallas kernels  3.2 us (7%)
  local copies, waits for them, and re-layouts  2.2 us (5%)
  between operations  0.8 us (2%)
    ppermute x8, waiting for transfers between devices, up_line(): return lax.ppermute(rows, ('group', 'z', 'x', 'y', 'tp'), pairs)  26.3 us
    ppermute x8, starting transfers between devices, up_line(): return lax.ppermute(rows, ('group', 'z', 'x', 'y', 'tp'), pairs)  10.3 us
    unnamed x10, local copies, waits for them, and re-layouts  2.2 us
    pallas_call x1, Pallas kernels, shards(): pl.pallas_call(last_kernel, out_shape=jax.ShapeDtypeStruct((seq_count,) +...  1.72 us
    pallas_call x1, Pallas kernels, shards(): pl.pallas_call(middle_kernel, out_shape=[first_shape] + [jax.ShapeDtypeSt...  1.19 us
  transfers between devices with their start and end apart: 8, of which 5 were waited for; matrix products, arithmetic and copies ran while one was open for 0% of the time, Pallas kernels for 0%

profile of v1, /device:TPU:1, one launch (start us, length us, event | category | flops | bytes accessed | tf_op | source)
XLA Modules:
  0.0 42.8 jit_solution(1086184540770326734)
XLA Ops:
  0.0 0.0 copy-start.4
  0.7 0.0 copy-done.4
  0.7 0.0 copy-start.2
  0.7 1.0 %copy-done.2 = bf16[256,576]{0,1:T(8,128)(2,1)S(1)} copy-done((bf16[256,576]{0,1:T(8,128)(2,1)S(1)}, bf16[256,576]{0,1:T(8,128)(2,1)}, u32[]{:S(2)}) %copy-start.2) | copy-done | bytes 294936
  1.7 0.3 shard_map.64
  2.0 0.0 copy-start
  2.0 0.0 copy-start.1
  2.0 0.0 copy-start.3
  2.0 1.0 %copy-done = bf16[2,4,64,576]{3,2,1,0:T(8,128)(2,1)S(1)} copy-done((bf16[2,4,64,576]{3,2,1,0:T(8,128)(2,1)S(1)}, bf16[2,4,64,576]{3,2,1,0:T(8,128)(2,1)}, u32[]{:S(2)}) %copy-start) | copy-done | bytes 589848
  3.1 0.2 copy-done.1
  3.2 0.0 copy-done.3
  3.2 1.2 %shard_map.65 = (bf16[4,64,512]{2,1,0:T(8,128)(2,1)S(1)}, bf16[32,576]{1,0:T(8,128)(2,1)S(1)}, bf16[32,576]{1,0:T(8,128)(2,1)S(1)}, bf16[32,576]{1,0:T(8,128)(2,...) custom-call(s32[1]{0:T(128)S(6)} %copy.9.length_ref, ...), custom_call_target="tpu_custom_call" | custom-call | tf_op jit(solution)/shard_map/pallas_call | solution.py:169
  4.4 1.3 %collective-permute-start = (bf16[32,576]{1,0:T(8,128)(2,1)S(1)}, bf16[32,576]{1,0:T(8,128)(2,1)S(1)}, u32[]{:S(2)}, u32[]{:S(2)}) collective-permute-start(bf16[32,576]{1,0:T(8,128)(2,1)S(1)} %get-tuple-element.24), channel_id=1, source_target_pairs={{0,384},{2,386},{4,388},{6,390},{8,392},{10,394},{12,396},{14,398}... | collective-permute-start | bytes 110600 | tf_op jit(solution)/shard_map/ppermute | solution.py:144
  5.7 1.3 %collective-permute-start.1 = (bf16[32,576]{1,0:T(8,128)(2,1)S(1)}, bf16[32,576]{1,0:T(8,128)(2,1)S(1)}, u32[]{:S(2)}, u32[]{:S(2)}) collective-permute-start(bf16[32,576]{1,0:T(8,128)(2,1)S(1)} %get-tuple-element.25), channel_id=1, source_target_pairs={{0,417},{2,419},{4,421},{6,423},{8,425},{10,427},{12,429},{14,431}... | collective-permute-start | bytes 110600 | tf_op jit(solution)/shard_map/ppermute | solution.py:144
  7.0 1.3 %collective-permute-start.2 = (bf16[32,576]{1,0:T(8,128)(2,1)S(1)}, bf16[32,576]{1,0:T(8,128)(2,1)S(1)}, u32[]{:S(2)}, u32[]{:S(2)}) collective-permute-start(bf16[32,576]{1,0:T(8,128)(2,1)S(1)} %get-tuple-element.26), channel_id=1, source_target_pairs={{0,288},{2,290},{4,292},{6,294},{8,296},{10,298},{12,300},{14,302}... | collective-permute-start | bytes 110600 | tf_op jit(solution)/shard_map/ppermute | solution.py:144
  8.3 1.3 %collective-permute-start.3 = (bf16[32,576]{1,0:T(8,128)(2,1)S(1)}, bf16[32,576]{1,0:T(8,128)(2,1)S(1)}, u32[]{:S(2)}, u32[]{:S(2)}) collective-permute-start(bf16[32,576]{1,0:T(8,128)(2,1)S(1)} %get-tuple-element.27), channel_id=1, source_target_pairs={{0,320},{2,322},{4,324},{6,326},{8,328},{10,330},{12,332},{14,334}... | collective-permute-start | bytes 110600 | tf_op jit(solution)/shard_map/ppermute | solution.py:144
  9.6 1.3 %collective-permute-start.4 = (bf16[32,576]{1,0:T(8,128)(2,1)S(1)}, bf16[32,576]{1,0:T(8,128)(2,1)S(1)}, u32[]{:S(2)}, u32[]{:S(2)}) collective-permute-start(bf16[32,576]{1,0:T(8,128)(2,1)S(1)} %get-tuple-element.28), channel_id=1, source_target_pairs={{0,352},{2,354},{4,356},{6,358},{8,360},{10,362},{12,364},{14,366}... | collective-permute-start | bytes 110600 | tf_op jit(solution)/shard_map/ppermute | solution.py:144
  10.9 18.5 %collective-permute-done.refs_0_ = bf16[32,576]{1,0:T(8,128)(2,1)S(1)} collective-permute-done((bf16[32,576]{1,0:T(8,128)(2,1)S(1)}, bf16[32,576]{1,0:T(8,128)(2,1)S(1)}, u32[]{:S(2)}, u32[]{:S(2)}) %collective-permute-start) | collective-permute-done | bytes 36896 | tf_op jit(solution)/shard_map/ppermute | solution.py:144
  29.4 1.3 %collective-permute-start.5 = (bf16[32,576]{1,0:T(8,128)(2,1)S(1)}, bf16[32,576]{1,0:T(8,128)(2,1)S(1)}, u32[]{:S(2)}, u32[]{:S(2)}) collective-permute-start(bf16[32,576]{1,0:T(8,128)(2,1)S(1)} %get-tuple-element.29), channel_id=1, source_target_pairs={{0,481},{2,483},{4,485},{6,487},{8,489},{10,491},{12,493},{14,495}... | collective-permute-start | bytes 110600 | tf_op jit(solution)/shard_map/ppermute | solution.py:144
  30.7 0.0 collective-permute-done.1.refs_1_
  30.7 1.3 %collective-permute-start.6 = (bf16[32,576]{1,0:T(8,128)(2,1)S(1)}, bf16[32,576]{1,0:T(8,128)(2,1)S(1)}, u32[]{:S(2)}, u32[]{:S(2)}) collective-permute-start(bf16[32,576]{1,0:T(8,128)(2,1)S(1)} %get-tuple-element.30), channel_id=1, source_target_pairs={{0,449},{2,451},{4,453},{6,455},{8,457},{10,459},{12,461},{14,463}... | collective-permute-start | bytes 110600 | tf_op jit(solution)/shard_map/ppermute | solution.py:144
  32.0 2.3 %collective-permute-done.2.refs_2_ = bf16[32,576]{1,0:T(8,128)(2,1)S(1)} collective-permute-done((bf16[32,576]{1,0:T(8,128)(2,1)S(1)}, bf16[32,576]{1,0:T(8,128)(2,1)S(1)}, u32[]{:S(2)}, u32[]{:S(2)}) %collective-permute-start.2) | collective-permute-done | bytes 36896 | tf_op jit(solution)/shard_map/ppermute | solution.py:144
  34.3 1.3 %collective-permute-start.7 = (bf16[32,576]{1,0:T(8,128)(2,1)S(1)}, bf16[32,576]{1,0:T(8,128)(2,1)S(1)}, u32[]{:S(2)}, u32[]{:S(2)}) collective-permute-start(bf16[32,576]{1,0:T(8,128)(2,1)S(1)} %get-tuple-element.31), channel_id=1, source_target_pairs={{0,256},{2,258},{4,260},{6,262},{8,264},{10,266},{12,268},{14,270}... | collective-permute-start | bytes 110600 | tf_op jit(solution)/shard_map/ppermute | solution.py:144
  35.6 0.5 %collective-permute-done.3.refs_3_ = bf16[32,576]{1,0:T(8,128)(2,1)S(1)} collective-permute-done((bf16[32,576]{1,0:T(8,128)(2,1)S(1)}, bf16[32,576]{1,0:T(8,128)(2,1)S(1)}, u32[]{:S(2)}, u32[]{:S(2)}) %collective-permute-start.3) | collective-permute-done | bytes 36896 | tf_op jit(solution)/shard_map/ppermute | solution.py:144
  36.1 1.7 %collective-permute-done.4.refs_4_ = bf16[32,576]{1,0:T(8,128)(2,1)S(1)} collective-permute-done((bf16[32,576]{1,0:T(8,128)(2,1)S(1)}, bf16[32,576]{1,0:T(8,128)(2,1)S(1)}, u32[]{:S(2)}, u32[]{:S(2)}) %collective-permute-start.4) | collective-permute-done | bytes 36896 | tf_op jit(solution)/shard_map/ppermute | solution.py:144
  37.8 0.0 collective-permute-done.5.refs_5_
  37.8 0.0 collective-permute-done.6.refs_6_
  37.8 3.3 %collective-permute-done.7.refs_7_ = bf16[32,576]{1,0:T(8,128)(2,1)S(1)} collective-permute-done((bf16[32,576]{1,0:T(8,128)(2,1)S(1)}, bf16[32,576]{1,0:T(8,128)(2,1)S(1)}, u32[]{:S(2)}, u32[]{:S(2)}) %collective-permute-start.7) | collective-permute-done | bytes 36896 | tf_op jit(solution)/shard_map/ppermute | solution.py:144
  41.1 1.7 %shard_map.66 = bf16[2,4,64,512]{3,2,1,0:T(8,128)(2,1)} custom-call(s32[1]{0:T(128)S(6)} %copy.9.length_ref, bf16[2,4,64,576]{3,2,1,0:T(8,128)(2,1)S(1)} %copy-done, bf16[2,4,576]{2,1,0:T(4,128)(2,1)S(1)} %copy-done.3, bf16[1,576,512]{2,1,0:T(8,128)(2,1)S(1)} %bitcast.6, bf16[4,64,512]{2,1,0:T(8,128)(2,1)S(1)} %get-tuple-element.23.first_ref, ...), custom_call_target="tpu_custom_call" | custom-call | tf_op jit(solution)/shard_map/pallas_call | solution.py:178
  (2 shorter events, 0.0 us)
Async XLA Ops:
  0.0 0.7 %copy-start.4 = (s32[256]{0:T(256)S(1)}, s32[256]{0:T(256)}, u32[]{:S(2)}) copy-start(s32[256]{0:T(256)} %param.13) | copy-start | bytes 3076
  0.7 1.0 %copy-start.2 = (bf16[256,576]{0,1:T(8,128)(2,1)S(1)}, bf16[256,576]{0,1:T(8,128)(2,1)}, u32[]{:S(2)}) copy-start(bf16[256,576]{0,1:T(8,128)(2,1)} %param.12) | copy-start | bytes 884740
  2.0 1.1 %copy-start = (bf16[2,4,64,576]{3,2,1,0:T(8,128)(2,1)S(1)}, bf16[2,4,64,576]{3,2,1,0:T(8,128)(2,1)}, u32[]{:S(2)}) copy-start(bf16[2,4,64,576]{3,2,1,0:T(8,128)(2,1)} %query_ref.3) | copy-start | bytes 1769476
  2.0 1.3 %copy-start.1 = (bf16[1,512,576]{1,2,0:T(8,128)(2,1)S(1)}, bf16[1,512,576]{1,2,0:T(8,128)(2,1)}, u32[]{:S(2)}) copy-start(bf16[1,512,576]{1,2,0:T(8,128)(2,1)} %param.10) | copy-start | bytes 1769476
  2.0 1.2 %copy-start.3 = (bf16[2,4,576]{2,1,0:T(4,128)(2,1)S(1)}, bf16[2,4,576]{2,1,0:T(4,128)(2,1)}, u32[]{:S(2)}) copy-start(bf16[2,4,576]{2,1,0:T(4,128)(2,1)} %step_ref.3) | copy-start | bytes 27652
  4.4 25.0 %collective-permute-start = (bf16[32,576]{1,0:T(8,128)(2,1)S(1)}, bf16[32,576]{1,0:T(8,128)(2,1)S(1)}, u32[]{:S(2)}, u32[]{:S(2)}) collective-permute-start(bf16[32,576]{1,0:T(8,128)(2,1)S(1)} %get-tuple-element.24), channel_id=1, source_target_pairs={{0,384},{2,386},{4,388},{6,390},{8,392},{10,394},{12,396},{14,398}... | collective-permute-start | bytes 110600 | tf_op jit(solution)/shard_map/ppermute | solution.py:144
  5.7 25.0 %collective-permute-start.1 = (bf16[32,576]{1,0:T(8,128)(2,1)S(1)}, bf16[32,576]{1,0:T(8,128)(2,1)S(1)}, u32[]{:S(2)}, u32[]{:S(2)}) collective-permute-start(bf16[32,576]{1,0:T(8,128)(2,1)S(1)} %get-tuple-element.25), channel_id=1, source_target_pairs={{0,417},{2,419},{4,421},{6,423},{8,425},{10,427},{12,429},{14,431}... | collective-permute-start | bytes 110600 | tf_op jit(solution)/shard_map/ppermute | solution.py:144
  7.0 27.3 %collective-permute-start.2 = (bf16[32,576]{1,0:T(8,128)(2,1)S(1)}, bf16[32,576]{1,0:T(8,128)(2,1)S(1)}, u32[]{:S(2)}, u32[]{:S(2)}) collective-permute-start(bf16[32,576]{1,0:T(8,128)(2,1)S(1)} %get-tuple-element.26), channel_id=1, source_target_pairs={{0,288},{2,290},{4,292},{6,294},{8,296},{10,298},{12,300},{14,302}... | collective-permute-start | bytes 110600 | tf_op jit(solution)/shard_map/ppermute | solution.py:144
  8.3 27.7 %collective-permute-start.3 = (bf16[32,576]{1,0:T(8,128)(2,1)S(1)}, bf16[32,576]{1,0:T(8,128)(2,1)S(1)}, u32[]{:S(2)}, u32[]{:S(2)}) collective-permute-start(bf16[32,576]{1,0:T(8,128)(2,1)S(1)} %get-tuple-element.27), channel_id=1, source_target_pairs={{0,320},{2,322},{4,324},{6,326},{8,328},{10,330},{12,332},{14,334}... | collective-permute-start | bytes 110600 | tf_op jit(solution)/shard_map/ppermute | solution.py:144
  9.6 28.2 %collective-permute-start.4 = (bf16[32,576]{1,0:T(8,128)(2,1)S(1)}, bf16[32,576]{1,0:T(8,128)(2,1)S(1)}, u32[]{:S(2)}, u32[]{:S(2)}) collective-permute-start(bf16[32,576]{1,0:T(8,128)(2,1)S(1)} %get-tuple-element.28), channel_id=1, source_target_pairs={{0,352},{2,354},{4,356},{6,358},{8,360},{10,362},{12,364},{14,366}... | collective-permute-start | bytes 110600 | tf_op jit(solution)/shard_map/ppermute | solution.py:144
  29.4 8.4 %collective-permute-start.5 = (bf16[32,576]{1,0:T(8,128)(2,1)S(1)}, bf16[32,576]{1,0:T(8,128)(2,1)S(1)}, u32[]{:S(2)}, u32[]{:S(2)}) collective-permute-start(bf16[32,576]{1,0:T(8,128)(2,1)S(1)} %get-tuple-element.29), channel_id=1, source_target_pairs={{0,481},{2,483},{4,485},{6,487},{8,489},{10,491},{12,493},{14,495}... | collective-permute-start | bytes 110600 | tf_op jit(solution)/shard_map/ppermute | solution.py:144
  30.7 7.1 %collective-permute-start.6 = (bf16[32,576]{1,0:T(8,128)(2,1)S(1)}, bf16[32,576]{1,0:T(8,128)(2,1)S(1)}, u32[]{:S(2)}, u32[]{:S(2)}) collective-permute-start(bf16[32,576]{1,0:T(8,128)(2,1)S(1)} %get-tuple-element.30), channel_id=1, source_target_pairs={{0,449},{2,451},{4,453},{6,455},{8,457},{10,459},{12,461},{14,463}... | collective-permute-start | bytes 110600 | tf_op jit(solution)/shard_map/ppermute | solution.py:144
  34.3 6.8 %collective-permute-start.7 = (bf16[32,576]{1,0:T(8,128)(2,1)S(1)}, bf16[32,576]{1,0:T(8,128)(2,1)S(1)}, u32[]{:S(2)}, u32[]{:S(2)}) collective-permute-start(bf16[32,576]{1,0:T(8,128)(2,1)S(1)} %get-tuple-element.31), channel_id=1, source_target_pairs={{0,256},{2,258},{4,260},{6,262},{8,264},{10,266},{12,268},{14,270}... | collective-permute-start | bytes 110600 | tf_op jit(solution)/shard_map/ppermute | solution.py:144

commit v2 on v1

--- a/solution.py
+++ b/solution.py
@@ -6,8 +6,8 @@
 from jax.sharding import Mesh, PartitionSpec as P
 
 KV_RANK = 512
-PLANE = 16
-LINE = 8
+PEERS = 32
+LINE = 4
 
 score_scale = 192.0 ** (-0.5)
 masked_score = -1e30
@@ -71,8 +71,8 @@
         count = moved_ref.shape[0]
         rows = lax.broadcasted_iota(jnp.int32, (count, count), 0)
         cols = lax.broadcasted_iota(jnp.int32, (count, count), 1)
-        run, plane, ahead = rows % 2, (rows // 2) % PLANE, rows // (2 * PLANE)
-        source = (plane * LINE + ahead) * 2 + run
+        run, peer, ahead = rows % 2, (rows // 2) % PEERS, rows // (2 * PEERS)
+        source = (peer * LINE + ahead) * 2 + run
         turned = picked(cols == source, moved_ref[...], ((1,), (0,)))
         step = count // LINE
         for part, part_ref in enumerate(part_refs):
@@ -133,15 +133,15 @@
 
 
 def up_line(rows, ahead):
-    line_total, ring = PLANE * LINE * 2, LINE * 2
+    line_total, ring = PEERS * LINE * 2, LINE * 2
     pairs = []
     for place in range(ring):
         there = (place + step_of(place, ahead)) % ring
-        for plane in range(PLANE):
-            source = ((place % LINE) * PLANE + plane) * 2 + place // LINE
-            target = ((there % LINE) * PLANE + plane) * 2 + there // LINE
+        for peer in range(PEERS):
+            source = ((place % LINE) * PEERS + peer) * 2 + place // LINE
+            target = ((there % LINE) * PEERS + peer) * 2 + there // LINE
             pairs.append((source, line_total + target))
-    return lax.ppermute(rows, ("group", "z", "x", "y", "tp"), pairs)
+    return lax.ppermute(rows, ("group", "pair", "z", "x", "y", "tp"), pairs)
 
 
 def shards(queries, step_rows, cache, lengths, outgoing, crossing):
@@ -151,8 +151,8 @@
     keys = cache.transpose(0, 2, 1)
 
     run = jnp.arange(row_total, dtype=jnp.int32) // (row_total // 2)
-    ahead = (crossing // PLANE - lax.axis_index("z") + LINE) % LINE
-    slots = ((crossing % PLANE) * LINE + ahead) * 2 + run
+    ahead = (crossing // PEERS - lax.axis_index("pair") + LINE) % LINE
+    slots = ((crossing % PEERS) * LINE + ahead) * 2 + run
     packed = pl.pallas_call(
         pack_kernel,
         out_shape=jax.ShapeDtypeStruct((row_total, latent_width), jnp.bfloat16),
@@ -162,9 +162,9 @@
     )(slots.reshape(1, row_total), outgoing.T)
     moved = lax.cond(
         lax.axis_index("group") == 0,
-        lambda rows: lax.all_to_all(rows, ("x", "y"), 0, 0, tiled=True),
+        lambda rows: lax.all_to_all(rows, ("z", "x", "y"), 0, 0, tiled=True),
         lambda rows: rows,
-        packed.reshape(PLANE, row_total // PLANE, latent_width),
+        packed.reshape(PEERS, row_total // PEERS, latent_width),
     )
     first, *parts = pl.pallas_call(
         middle_kernel,
@@ -174,7 +174,7 @@
         out_specs=[vmem] * (1 + LINE),
         compiler_params=params,
     )(lengths, queries, step_rows, keys, moved.reshape(row_total, latent_width))
-    arrived = [up_line(parts[ahead], ahead) for ahead in (4, 5, 1, 2, 3, 7, 6, 0)]
+    arrived = [up_line(parts[ahead], ahead) for ahead in (1, 2, 3, 0)]
     return pl.pallas_call(
         last_kernel,
         out_shape=jax.ShapeDtypeStruct((seq_count,) + first_shape.shape, jnp.bfloat16),
@@ -189,8 +189,9 @@
 
 
 def solution(mesh):
-    parted = Mesh(mesh.devices.reshape(2, LINE, 4, 4, 2), ("group", "z", "x", "y", "tp"))
-    own = ("group", "z", "x", "y")
+    axes = ("group", "pair", "z", "x", "y", "tp")
+    parted = Mesh(mesh.devices.reshape(2, LINE, 2, 4, 4, 2), axes)
+    own = axes[:-1]
     placed = (
         P(own, None, "tp", None),
         P(own, None, None),

time: 43.1 us -> 37.1 us (0.86)
  starting transfers between devices: 10.3 us -> 5.17 us
  waiting for transfers between devices: 26.3 us -> 25.5 us
    ppermute x8 -> x4, starting transfers between devices: 10.3 us -> 5.17 us  [up_line(): return lax.ppermute(rows, ('group', 'pair', 'z', 'x', 'y', 'tp'), pairs)]
    ppermute x8 -> x4, waiting for transfers between devices: 26.3 us -> 25.5 us  [up_line(): return lax.ppermute(rows, ('group', 'pair', 'z', 'x', 'y', 'tp'), pairs)]
  transfers between devices with their start and end apart: 8 -> 4, of which waited for: 5 -> 2; matrix products, arithmetic and copies ran while one was open for 0% -> 0% of each run, Pallas kernels for 0% -> 0%
where the time goes in v2:
time: 37.1 us; the launch traced here: 36.8 us
  waiting for transfers between devices  25.5 us (69%)
  starting transfers between devices  5.17 us (14%)
  Pallas kernels  3.19 us (9%)
  local copies, waits for them, and re-layouts  2.2 us (6%)
  between operations  0.76 us (2%)
    ppermute x4, waiting for transfers between devices, up_line(): return lax.ppermute(rows, ('group', 'pair', 'z', 'x', 'y', 'tp'), pairs)  25.5 us
    ppermute x4, starting transfers between devices, up_line(): return lax.ppermute(rows, ('group', 'pair', 'z', 'x', 'y', 'tp'), pairs)  5.17 us
    unnamed x10, local copies, waits for them, and re-layouts  2.2 us
    pallas_call x1, Pallas kernels, shards(): pl.pallas_call(last_kernel, out_shape=jax.ShapeDtypeStruct((seq_count,) +...  1.71 us
    pallas_call x1, Pallas kernels, shards(): pl.pallas_call(middle_kernel, out_shape=[first_shape] + [jax.ShapeDtypeSt...  1.19 us
  transfers between devices with their start and end apart: 4, of which 2 were waited for; matrix products, arithmetic and copies ran while one was open for 0% of the time, Pallas kernels for 0%

profile of v2, /device:TPU:1, one launch (start us, length us, event | category | flops | bytes accessed | tf_op | source)
XLA Modules:
  0.0 36.8 jit_solution(10265581848302199056)
XLA Ops:
  0.0 0.0 copy-start.4
  0.7 0.0 copy-done.4
  0.7 0.0 copy-start.2
  0.7 1.0 %copy-done.2 = bf16[256,576]{0,1:T(8,128)(2,1)S(1)} copy-done((bf16[256,576]{0,1:T(8,128)(2,1)S(1)}, bf16[256,576]{0,1:T(8,128)(2,1)}, u32[]{:S(2)}) %copy-start.2) | copy-done | bytes 294936
  1.7 0.3 shard_map.64
  2.0 0.0 copy-start
  2.0 0.0 copy-start.1
  2.0 0.0 copy-start.3
  2.0 1.0 %copy-done = bf16[2,4,64,576]{3,2,1,0:T(8,128)(2,1)S(1)} copy-done((bf16[2,4,64,576]{3,2,1,0:T(8,128)(2,1)S(1)}, bf16[2,4,64,576]{3,2,1,0:T(8,128)(2,1)}, u32[]{:S(2)}) %copy-start) | copy-done | bytes 589848
  3.1 0.2 copy-done.1
  3.2 0.0 copy-done.3
  3.2 1.2 %shard_map.65 = (bf16[4,64,512]{2,1,0:T(8,128)(2,1)S(1)}, bf16[64,576]{1,0:T(8,128)(2,1)S(1)}, bf16[64,576]{1,0:T(8,128)(2,1)S(1)}, bf16[64,576]{1,0:T(8,128)(2,1)S(1)}, bf16[64,576]{1,0:T(8,128)(2,1)S(1)}) custom-call(s32[1]{0:T(128)S(6)} %copy.9.length_ref, bf16[2,4,64,576]{3,2,1,0:T(8,128)(2,1)S(1)} %copy-done, bf16[2,4,576]{2,1,0:T(4,128)(2,1)S(1)} %copy-done.3, ...), custom_call_target="tpu_custom_call" | custom-call | tf_op jit(solution)/shard_map/pallas_call | solution.py:169
  4.4 1.3 %collective-permute-start = (bf16[64,576]{1,0:T(8,128)(2,1)S(1)}, bf16[64,576]{1,0:T(8,128)(2,1)S(1)}, u32[]{:S(2)}, u32[]{:S(2)}) collective-permute-start(bf16[64,576]{1,0:T(8,128)(2,1)S(1)} %get-tuple-element.20), channel_id=1, source_target_pairs={{0,320},{2,322},{4,324},{6,326},{8,328},{10,330},{12,332},{14,334}... | collective-permute-start | bytes 221192 | tf_op jit(solution)/shard_map/ppermute | solution.py:144
  5.7 1.3 %collective-permute-start.1 = (bf16[64,576]{1,0:T(8,128)(2,1)S(1)}, bf16[64,576]{1,0:T(8,128)(2,1)S(1)}, u32[]{:S(2)}, u32[]{:S(2)}) collective-permute-start(bf16[64,576]{1,0:T(8,128)(2,1)S(1)} %get-tuple-element.21), channel_id=1, source_target_pairs={{0,384},{2,386},{4,388},{6,390},{8,392},{10,394},{12,396},{14,398}... | collective-permute-start | bytes 221192 | tf_op jit(solution)/shard_map/ppermute | solution.py:144
  7.0 1.3 %collective-permute-start.2 = (bf16[64,576]{1,0:T(8,128)(2,1)S(1)}, bf16[64,576]{1,0:T(8,128)(2,1)S(1)}, u32[]{:S(2)}, u32[]{:S(2)}) collective-permute-start(bf16[64,576]{1,0:T(8,128)(2,1)S(1)} %get-tuple-element.22), channel_id=1, source_target_pairs={{0,449},{2,451},{4,453},{6,455},{8,457},{10,459},{12,461},{14,463}... | collective-permute-start | bytes 221192 | tf_op jit(solution)/shard_map/ppermute | solution.py:144
  8.3 1.3 %collective-permute-start.3 = (bf16[64,576]{1,0:T(8,128)(2,1)S(1)}, bf16[64,576]{1,0:T(8,128)(2,1)S(1)}, u32[]{:S(2)}, u32[]{:S(2)}) collective-permute-start(bf16[64,576]{1,0:T(8,128)(2,1)S(1)} %get-tuple-element.23), channel_id=1, source_target_pairs={{0,256},{2,258},{4,260},{6,262},{8,264},{10,266},{12,268},{14,270}... | collective-permute-start | bytes 221192 | tf_op jit(solution)/shard_map/ppermute | solution.py:144
  9.6 25.0 %collective-permute-done.refs_0_ = bf16[64,576]{1,0:T(8,128)(2,1)S(1)} collective-permute-done((bf16[64,576]{1,0:T(8,128)(2,1)S(1)}, bf16[64,576]{1,0:T(8,128)(2,1)S(1)}, u32[]{:S(2)}, u32[]{:S(2)}) %collective-permute-start) | collective-permute-done | bytes 73760 | tf_op jit(solution)/shard_map/ppermute | solution.py:144
  34.6 0.5 %collective-permute-done.1.refs_1_ = bf16[64,576]{1,0:T(8,128)(2,1)S(1)} collective-permute-done((bf16[64,576]{1,0:T(8,128)(2,1)S(1)}, bf16[64,576]{1,0:T(8,128)(2,1)S(1)}, u32[]{:S(2)}, u32[]{:S(2)}) %collective-permute-start.1) | collective-permute-done | bytes 73760 | tf_op jit(solution)/shard_map/ppermute | solution.py:144
  35.1 0.0 collective-permute-done.2.refs_2_
  35.1 0.0 collective-permute-done.3.refs_3_
  35.1 1.7 %shard_map.66 = bf16[2,4,64,512]{3,2,1,0:T(8,128)(2,1)} custom-call(s32[1]{0:T(128)S(6)} %copy.9.length_ref, bf16[2,4,64,576]{3,2,1,0:T(8,128)(2,1)S(1)} %copy-done, bf16[2,4,576]{2,1,0:T(4,128)(2,1)S(1)} %copy-done.3, bf16[1,576,512]{2,1,0:T(8,128)(2,1)S(1)} %bitcast.6, bf16[4,64,512]{2,1,0:T(8,128)(2,1)S(1)} %get-tuple-element.19.first_ref, ...), custom_call_target="tpu_custom_call" | custom-call | tf_op jit(solution)/shard_map/pallas_call | solution.py:178
  (2 shorter events, 0.0 us)
Async XLA Ops:
  0.0 0.7 %copy-start.4 = (s32[256]{0:T(256)S(1)}, s32[256]{0:T(256)}, u32[]{:S(2)}) copy-start(s32[256]{0:T(256)} %param.13) | copy-start | bytes 3076
  0.7 1.0 %copy-start.2 = (bf16[256,576]{0,1:T(8,128)(2,1)S(1)}, bf16[256,576]{0,1:T(8,128)(2,1)}, u32[]{:S(2)}) copy-start(bf16[256,576]{0,1:T(8,128)(2,1)} %param.12) | copy-start | bytes 884740
  2.0 1.1 %copy-start = (bf16[2,4,64,576]{3,2,1,0:T(8,128)(2,1)S(1)}, bf16[2,4,64,576]{3,2,1,0:T(8,128)(2,1)}, u32[]{:S(2)}) copy-start(bf16[2,4,64,576]{3,2,1,0:T(8,128)(2,1)} %query_ref.3) | copy-start | bytes 1769476
  2.0 1.3 %copy-start.1 = (bf16[1,512,576]{1,2,0:T(8,128)(2,1)S(1)}, bf16[1,512,576]{1,2,0:T(8,128)(2,1)}, u32[]{:S(2)}) copy-start(bf16[1,512,576]{1,2,0:T(8,128)(2,1)} %param.10) | copy-start | bytes 1769476
  2.0 1.2 %copy-start.3 = (bf16[2,4,576]{2,1,0:T(4,128)(2,1)S(1)}, bf16[2,4,576]{2,1,0:T(4,128)(2,1)}, u32[]{:S(2)}) copy-start(bf16[2,4,576]{2,1,0:T(4,128)(2,1)} %step_ref.3) | copy-start | bytes 27652
  4.4 30.2 %collective-permute-start = (bf16[64,576]{1,0:T(8,128)(2,1)S(1)}, bf16[64,576]{1,0:T(8,128)(2,1)S(1)}, u32[]{:S(2)}, u32[]{:S(2)}) collective-permute-start(bf16[64,576]{1,0:T(8,128)(2,1)S(1)} %get-tuple-element.20), channel_id=1, source_target_pairs={{0,320},{2,322},{4,324},{6,326},{8,328},{10,330},{12,332},{14,334}... | collective-permute-start | bytes 221192 | tf_op jit(solution)/shard_map/ppermute | solution.py:144
  5.7 29.4 %collective-permute-start.1 = (bf16[64,576]{1,0:T(8,128)(2,1)S(1)}, bf16[64,576]{1,0:T(8,128)(2,1)S(1)}, u32[]{:S(2)}, u32[]{:S(2)}) collective-permute-start(bf16[64,576]{1,0:T(8,128)(2,1)S(1)} %get-tuple-element.21), channel_id=1, source_target_pairs={{0,384},{2,386},{4,388},{6,390},{8,392},{10,394},{12,396},{14,398}... | collective-permute-start | bytes 221192 | tf_op jit(solution)/shard_map/ppermute | solution.py:144
  7.0 28.1 %collective-permute-start.2 = (bf16[64,576]{1,0:T(8,128)(2,1)S(1)}, bf16[64,576]{1,0:T(8,128)(2,1)S(1)}, u32[]{:S(2)}, u32[]{:S(2)}) collective-permute-start(bf16[64,576]{1,0:T(8,128)(2,1)S(1)} %get-tuple-element.22), channel_id=1, source_target_pairs={{0,449},{2,451},{4,453},{6,455},{8,457},{10,459},{12,461},{14,463}... | collective-permute-start | bytes 221192 | tf_op jit(solution)/shard_map/ppermute | solution.py:144
  8.3 26.8 %collective-permute-start.3 = (bf16[64,576]{1,0:T(8,128)(2,1)S(1)}, bf16[64,576]{1,0:T(8,128)(2,1)S(1)}, u32[]{:S(2)}, u32[]{:S(2)}) collective-permute-start(bf16[64,576]{1,0:T(8,128)(2,1)S(1)} %get-tuple-element.23), channel_id=1, source_target_pairs={{0,256},{2,258},{4,260},{6,262},{8,264},{10,266},{12,268},{14,270}... | collective-permute-start | bytes 221192 | tf_op jit(solution)/shard_map/ppermute | solution.py:144

commit v3 on v2

v3 whole, which is shorter than its diff:
```python
import jax
import jax.numpy as jnp
from jax import lax
from jax.experimental import pallas as pl
from jax.experimental.pallas import tpu as pltpu
from jax.sharding import Mesh, PartitionSpec as P

KV_RANK = 512
PEERS = 32
LINE = 4
AHEAD = (1, 0, 2, 3)

score_scale = 192.0 ** (-0.5)
masked_score = -1e30


def product(left, right, dims):
    return lax.dot_general(left, right, (dims, ((), ())), preferred_element_type=jnp.float32)


def picked(where_one, rows, dims):
    selector = jnp.where(where_one, 1.0, 0.0).astype(jnp.bfloat16)
    return product(selector, rows, dims).astype(jnp.bfloat16)


def pack_kernel(slot_ref, latent_ref, packed_ref):
    count = slot_ref.shape[1]
    rows = lax.broadcasted_iota(jnp.int32, (count, count), 0)
    packed_ref[...] = picked(rows == slot_ref[...], latent_ref[...], ((1,), (1,)))


def flat_rows(query_ref, seq):
    query = query_ref[seq]
    return query.reshape(query.shape[0] * query.shape[1], query.shape[2])


def step_scores(query, step_keys, head_count):
    scores = product(query, step_keys, ((1,), (1,))) * score_scale
    query_step = lax.broadcasted_iota(jnp.int32, scores.shape, 0) // head_count
    key_step = lax.broadcasted_iota(jnp.int32, scores.shape, 1)
    return jnp.where(key_step <= query_step, scores, masked_score)


def resident(length, query, step_keys, keys):
    head_count = query.shape[0] // step_keys.shape[0]
    scores = product(query, keys, ((1,), (0,))) * score_scale
    position = lax.broadcasted_iota(jnp.int32, scores.shape, 1)
    base_scores = jnp.where(position < length, scores, masked_score)
    tail_scores = step_scores(query, step_keys, head_count)
    peak = jnp.maximum(
        jnp.max(base_scores, axis=1, keepdims=True), jnp.max(tail_scores, axis=1, keepdims=True)
    )
    base_expo = jnp.exp(base_scores - peak)
    tail_expo = jnp.exp(tail_scores - peak)
    total = jnp.sum(base_expo, axis=1, keepdims=True) + jnp.sum(tail_expo, axis=1, keepdims=True)
    mixed = product(base_expo.astype(jnp.bfloat16), keys[:KV_RANK], ((1,), (1,))) + product(
        tail_expo.astype(jnp.bfloat16), step_keys[:, :KV_RANK], ((1,), (0,))
    )
    return (mixed * (1.0 / total)).astype(jnp.bfloat16).reshape(-1, head_count, KV_RANK)


def steps_only(query, step_keys):
    head_count = query.shape[0] // step_keys.shape[0]
    scores = step_scores(query, step_keys, head_count)
    expo = jnp.exp(scores - jnp.max(scores, axis=1, keepdims=True))
    total = jnp.sum(expo, axis=1, keepdims=True)
    mixed = product(expo.astype(jnp.bfloat16), step_keys[:, :KV_RANK], ((1,), (0,)))
    return (mixed * (1.0 / total)).astype(jnp.bfloat16).reshape(-1, head_count, KV_RANK)


def arrived_and_steps(query_t, keys, base_count, head_count):
    scores = product(keys, query_t, ((1,), (0,))) * score_scale
    step = lax.broadcasted_iota(jnp.int32, scores.shape, 0) - base_count
    query_step = lax.broadcasted_iota(jnp.int32, scores.shape, 1) // head_count
    scores = jnp.where(step <= query_step, scores, masked_score)
    expo = jnp.exp(scores - jnp.max(scores, axis=0, keepdims=True))
    total = jnp.sum(expo, axis=0, keepdims=True)
    mixed = product(expo.astype(jnp.bfloat16), keys[:, :KV_RANK], ((0,), (0,)))
    share = jnp.transpose(jnp.broadcast_to(1.0 / total, (8, total.shape[1])))[:, :1]
    return (mixed * share).astype(jnp.bfloat16).reshape(-1, head_count, KV_RANK)


def middle_kernel(
    length_ref, query_ref, step_ref, cache_ref, moved_ref, first_ref, query_t_ref, tail_ref, *part_refs
):
    decode = lax.axis_index("group") == 1

    @pl.when(decode)
    def _():
        first_ref[...] = resident(length_ref[0], flat_rows(query_ref, 0), step_ref[0], cache_ref[0])
        query_t_ref[...] = jnp.transpose(flat_rows(query_ref, 1))
        tail_ref[...] = jnp.zeros_like(tail_ref)
        tail_ref[: step_ref.shape[1]] = step_ref[1]

    @pl.when(jnp.logical_not(decode))
    def _():
        count = moved_ref.shape[0]
        rows = lax.broadcasted_iota(jnp.int32, (count, count), 0)
        cols = lax.broadcasted_iota(jnp.int32, (count, count), 1)
        run, peer, part = rows % 2, (rows // 2) % PEERS, rows // (2 * PEERS)
        ahead = jnp.zeros_like(part)
        for index, part_ahead in enumerate(AHEAD):
            ahead = jnp.where(part == index, part_ahead, ahead)
        source = (peer * LINE + ahead) * 2 + run
        turned = picked(cols == source, moved_ref[...], ((1,), (0,)))
        step = count // LINE
        for part, part_ref in enumerate(part_refs):
            part_ref[...] = turned[part * step : (part + 1) * step]


def last_kernel(
    length_ref, query_ref, step_ref, cache_ref, first_ref, query_t_ref, tail_ref, *refs
):
    part_refs, (out_ref, result, sems) = refs[:LINE], refs[LINE:]
    decode = lax.axis_index("group") == 1

    @pl.when(decode)
    def _():
        before = pltpu.make_async_copy(first_ref, out_ref.at[0], sems.at[0])
        before.start()
        keys = jnp.concatenate([ref[...] for ref in part_refs] + [tail_ref[...]], axis=0)
        base_count = keys.shape[0] - tail_ref.shape[0]
        result[1] = arrived_and_steps(query_t_ref[...], keys, base_count, query_ref.shape[2])
        after = pltpu.make_async_copy(result.at[1], out_ref.at[1], sems.at[1])
        after.start()
        before.wait()
        after.wait()

    @pl.when(jnp.logical_not(decode))
    def _():
        result[0] = resident(length_ref[0], flat_rows(query_ref, 0), step_ref[0], cache_ref[0])
        before = pltpu.make_async_copy(result.at[0], out_ref.at[0], sems.at[0])
        before.start()
        result[1] = steps_only(flat_rows(query_ref, 1), step_ref[1])
        after = pltpu.make_async_copy(result.at[1], out_ref.at[1], sems.at[1])
        after.start()
        before.wait()
        after.wait()


vmem = pl.BlockSpec(memory_space=pltpu.VMEM)
smem = pl.BlockSpec(memory_space=pltpu.SMEM)
anywhere = pl.BlockSpec(memory_space=pl.ANY)
params = pltpu.CompilerParams(vmem_limit_bytes=16 << 20)


def step_of(place, ahead):
    if ahead == LINE // 2:
        down = place % LINE >= LINE // 2 or place % 2 == 1
        return -ahead if down else ahead
    return ahead if ahead < LINE // 2 else ahead - LINE


def along_line(rows, ahead):
    line_total, ring = PEERS * LINE * 2, LINE * 2
    pairs = []
    for place in range(ring):
        there = (place + step_of(place, ahead)) % ring
        for peer in range(PEERS):
            source = ((place % LINE) * PEERS + peer) * 2 + place // LINE
            target = ((there % LINE) * PEERS + peer) * 2 + there // LINE
            pairs.append((source, line_total + target))
    return lax.ppermute(rows, ("group", "pair", "z", "x", "y", "tp"), pairs)


def shards(queries, step_rows, cache, lengths, outgoing, crossing):
    seq_count, steps_total, head_count, latent_width = queries.shape
    row_total = outgoing.shape[0]
    first_shape = jax.ShapeDtypeStruct((steps_total, head_count, KV_RANK), jnp.bfloat16)
    keys = cache.transpose(0, 2, 1)

    query_rows = steps_total * head_count
    run = jnp.arange(row_total, dtype=jnp.int32) // (row_total // 2)
    ahead = (crossing // PEERS - lax.axis_index("pair") + LINE) % LINE
    slots = ((crossing % PEERS) * LINE + ahead) * 2 + run
    mine = jnp.where(lax.axis_index("group") == 0, outgoing.T, jnp.zeros((), outgoing.dtype))
    packed = pl.pallas_call(
        pack_kernel,
        out_shape=jax.ShapeDtypeStruct((row_total, latent_width), jnp.bfloat16),
        in_specs=[vmem] * 2,
        out_specs=vmem,
        compiler_params=params,
    )(slots.reshape(1, row_total), mine)
    moved = lax.cond(
        lax.axis_index("group") == 0,
        lambda rows: lax.all_to_all(rows, ("z", "x", "y"), 0, 0, tiled=True),
        lambda rows: rows,
        packed.reshape(PEERS, row_total // PEERS, latent_width),
    )
    first, query_t, tail, *parts = pl.pallas_call(
        middle_kernel,
        out_shape=[
            first_shape,
            jax.ShapeDtypeStruct((latent_width, query_rows), jnp.bfloat16),
            jax.ShapeDtypeStruct((16, latent_width), jnp.bfloat16),
        ]
        + [jax.ShapeDtypeStruct((row_total // LINE, latent_width), jnp.bfloat16)] * LINE,
        in_specs=[smem] + [vmem] * 4,
        out_specs=[vmem] * (3 + LINE),
        compiler_params=params,
    )(lengths, queries, step_rows, keys, moved.reshape(row_total, latent_width))
    arrived = [along_line(part, ahead) for part, ahead in zip(parts, AHEAD)]
    return pl.pallas_call(
        last_kernel,
        out_shape=jax.ShapeDtypeStruct((seq_count,) + first_shape.shape, jnp.bfloat16),
        in_specs=[smem] + [vmem] * (6 + LINE),
        out_specs=anywhere,
        scratch_shapes=[
            pltpu.VMEM((seq_count,) + first_shape.shape, jnp.bfloat16),
            pltpu.SemaphoreType.DMA((2,)),
        ],
        compiler_params=params,
    )(lengths, queries, step_rows, keys, first, query_t, tail, *arrived)


def solution(mesh):
    axes = ("group", "pair", "z", "x", "y", "tp")
    parted = Mesh(mesh.devices.reshape(2, LINE, 2, 4, 4, 2), axes)
    own = axes[:-1]
    placed = (
        P(own, None, "tp", None),
        P(own, None, None),
        P(own, None, None),
        P(own),
        P(own, None),
        P(own),
    )
    return jax.shard_map(
        shards,
        mesh=parted,
        in_specs=placed,
        out_specs=P(own, None, "tp", None),
        check_vma=False,
    )
```

time: 37.1 us -> 38.3 us (1.032)
  waiting for transfers between devices: 25.5 us -> 27.1 us
    ppermute x4, waiting for transfers between devices: 25.5 us -> 27.1 us  [along_line(): return lax.ppermute(rows, ('group', 'pair', 'z', 'x', 'y', 'tp'), pairs)]
    unnamed x10 -> x8, local copies, waits for them, and re-layouts: 2.2 us -> 1.86 us
where the time goes in v3:
time: 38.3 us; the launch traced here: 38 us
  waiting for transfers between devices  27.1 us (71%)
  starting transfers between devices  5.17 us (13%)
  Pallas kernels  3.1 us (8%)
  local copies, waits for them, and re-layouts  1.86 us (5%)
  between operations  0.75 us (2%)
    ppermute x4, waiting for transfers between devices, along_line(): return lax.ppermute(rows, ('group', 'pair', 'z', 'x', 'y', 'tp'), pairs)  27.1 us
    ppermute x4, starting transfers between devices, along_line(): return lax.ppermute(rows, ('group', 'pair', 'z', 'x', 'y', 'tp'), pairs)  5.17 us
    unnamed x8, local copies, waits for them, and re-layouts  1.86 us
    pallas_call x1, Pallas kernels, shards(): pl.pallas_call(last_kernel, out_shape=jax.ShapeDtypeStruct((seq_count,) +...  1.61 us
    pallas_call x1, Pallas kernels, shards(): pl.pallas_call(middle_kernel, out_shape=[first_shape, jax.ShapeDtypeStruc...  1.2 us
  transfers between devices with their start and end apart: 4, of which 2 were waited for; matrix products, arithmetic and copies ran while one was open for 0% of the time, Pallas kernels for 0%

profile of v3, /device:TPU:1, one launch (start us, length us, event | category | flops | bytes accessed | tf_op | source)
XLA Modules:
  0.0 38.0 jit_solution(16458539104791881188)
XLA Ops:
  0.7 0.0 copy-start.3
  0.7 0.6 %copy-done.3 = s32[256]{0:T(256)S(1)} copy-done((s32[256]{0:T(256)S(1)}, s32[256]{0:T(256)}, u32[]{:S(2)}) %copy-start.3) | copy-done | bytes 1048
  1.4 0.3 shard_map.64
  1.7 0.0 copy-start
  1.7 0.0 copy-start.1
  1.7 0.0 copy-start.2
  1.7 1.0 %copy-done = bf16[2,4,64,576]{3,2,1,0:T(8,128)(2,1)S(1)} copy-done((bf16[2,4,64,576]{3,2,1,0:T(8,128)(2,1)S(1)}, bf16[2,4,64,576]{3,2,1,0:T(8,128)(2,1)}, u32[]{:S(2)}) %copy-start) | copy-done | bytes 589848
  2.7 0.2 copy-done.1
  2.9 0.0 copy-done.2
  2.9 1.2 %shard_map.65 = (bf16[4,64,512]{2,1,0:T(8,128)(2,1)S(1)}, bf16[576,256]{1,0:T(8,128)(2,1)S(1)}, bf16[16,576]{1,0:T(8,128)(2,1)S(1)}, bf16[64,576]{1,0:T(8,128)(2...) custom-call(s32[1]{0:T(128)S(6)} %copy.9.length_ref, ...), custom_call_target="tpu_custom_call" | custom-call | tf_op jit(solution)/shard_map/pallas_call | solution.py:190
  4.1 1.3 %collective-permute-start = (bf16[64,576]{1,0:T(8,128)(2,1)S(1)}, bf16[64,576]{1,0:T(8,128)(2,1)S(1)}, u32[]{:S(2)}, u32[]{:S(2)}) collective-permute-start(bf16[64,576]{1,0:T(8,128)(2,1)S(1)} %get-tuple-element.24), channel_id=1, source_target_pairs={{0,320},{2,322},{4,324},{6,326},{8,328},{10,330},{12,332},{14,334}... | collective-permute-start | bytes 221192 | tf_op jit(solution)/shard_map/ppermute | solution.py:163
  5.4 1.3 %collective-permute-start.1 = (bf16[64,576]{1,0:T(8,128)(2,1)S(1)}, bf16[64,576]{1,0:T(8,128)(2,1)S(1)}, u32[]{:S(2)}, u32[]{:S(2)}) collective-permute-start(bf16[64,576]{1,0:T(8,128)(2,1)S(1)} %get-tuple-element.25), channel_id=1, source_target_pairs={{0,256},{2,258},{4,260},{6,262},{8,264},{10,266},{12,268},{14,270}... | collective-permute-start | bytes 221192 | tf_op jit(solution)/shard_map/ppermute | solution.py:163
  6.7 1.3 %collective-permute-start.2 = (bf16[64,576]{1,0:T(8,128)(2,1)S(1)}, bf16[64,576]{1,0:T(8,128)(2,1)S(1)}, u32[]{:S(2)}, u32[]{:S(2)}) collective-permute-start(bf16[64,576]{1,0:T(8,128)(2,1)S(1)} %get-tuple-element.26), channel_id=1, source_target_pairs={{0,384},{2,386},{4,388},{6,390},{8,392},{10,394},{12,396},{14,398}... | collective-permute-start | bytes 221192 | tf_op jit(solution)/shard_map/ppermute | solution.py:163
  8.0 1.3 %collective-permute-start.3 = (bf16[64,576]{1,0:T(8,128)(2,1)S(1)}, bf16[64,576]{1,0:T(8,128)(2,1)S(1)}, u32[]{:S(2)}, u32[]{:S(2)}) collective-permute-start(bf16[64,576]{1,0:T(8,128)(2,1)S(1)} %get-tuple-element.27), channel_id=1, source_target_pairs={{0,449},{2,451},{4,453},{6,455},{8,457},{10,459},{12,461},{14,463}... | collective-permute-start | bytes 221192 | tf_op jit(solution)/shard_map/ppermute | solution.py:163
  9.3 25.3 %collective-permute-done.refs_0_ = bf16[64,576]{1,0:T(8,128)(2,1)S(1)} collective-permute-done((bf16[64,576]{1,0:T(8,128)(2,1)S(1)}, bf16[64,576]{1,0:T(8,128)(2,1)S(1)}, u32[]{:S(2)}, u32[]{:S(2)}) %collective-permute-start) | collective-permute-done | bytes 73760 | tf_op jit(solution)/shard_map/ppermute | solution.py:163
  34.6 0.0 collective-permute-done.1.refs_1_
  34.6 1.8 %collective-permute-done.2.refs_2_ = bf16[64,576]{1,0:T(8,128)(2,1)S(1)} collective-permute-done((bf16[64,576]{1,0:T(8,128)(2,1)S(1)}, bf16[64,576]{1,0:T(8,128)(2,1)S(1)}, u32[]{:S(2)}, u32[]{:S(2)}) %collective-permute-start.2) | collective-permute-done | bytes 73760 | tf_op jit(solution)/shard_map/ppermute | solution.py:163
  36.4 0.0 collective-permute-done.3.refs_3_
  36.4 1.6 %shard_map.66 = bf16[2,4,64,512]{3,2,1,0:T(8,128)(2,1)} custom-call(s32[1]{0:T(128)S(6)} %copy.9.length_ref, bf16[2,4,64,576]{3,2,1,0:T(8,128)(2,1)S(1)} %copy-done, bf16[2,4,576]{2,1,0:T(4,128)(2,1)S(1)} %copy-done.2, bf16[1,576,512]{2,1,0:T(8,128)(2,1)S(1)} %bitcast.7, bf16[4,64,512]{2,1,0:T(8,128)(2,1)S(1)} %get-tuple-element.21.first_ref, ...), custom_call_target="tpu_custom_call" | custom-call | tf_op jit(solution)/shard_map/pallas_call | solution.py:203
  (3 shorter events, 0.1 us)
Async XLA Ops:
  0.7 0.7 %copy-start.3 = (s32[256]{0:T(256)S(1)}, s32[256]{0:T(256)}, u32[]{:S(2)}) copy-start(s32[256]{0:T(256)} %param.13) | copy-start | bytes 3076
  1.7 1.1 %copy-start = (bf16[2,4,64,576]{3,2,1,0:T(8,128)(2,1)S(1)}, bf16[2,4,64,576]{3,2,1,0:T(8,128)(2,1)}, u32[]{:S(2)}) copy-start(bf16[2,4,64,576]{3,2,1,0:T(8,128)(2,1)} %query_ref.3) | copy-start | bytes 1769476
  1.7 1.3 %copy-start.1 = (bf16[1,512,576]{1,2,0:T(8,128)(2,1)S(1)}, bf16[1,512,576]{1,2,0:T(8,128)(2,1)}, u32[]{:S(2)}) copy-start(bf16[1,512,576]{1,2,0:T(8,128)(2,1)} %param.10) | copy-start | bytes 1769476
  1.7 1.2 %copy-start.2 = (bf16[2,4,576]{2,1,0:T(4,128)(2,1)S(1)}, bf16[2,4,576]{2,1,0:T(4,128)(2,1)}, u32[]{:S(2)}) copy-start(bf16[2,4,576]{2,1,0:T(4,128)(2,1)} %step_ref.3) | copy-start | bytes 27652
  4.1 30.5 %collective-permute-start = (bf16[64,576]{1,0:T(8,128)(2,1)S(1)}, bf16[64,576]{1,0:T(8,128)(2,1)S(1)}, u32[]{:S(2)}, u32[]{:S(2)}) collective-permute-start(bf16[64,576]{1,0:T(8,128)(2,1)S(1)} %get-tuple-element.24), channel_id=1, source_target_pairs={{0,320},{2,322},{4,324},{6,326},{8,328},{10,330},{12,332},{14,334}... | collective-permute-start | bytes 221192 | tf_op jit(solution)/shard_map/ppermute | solution.py:163
  5.4 29.2 %collective-permute-start.1 = (bf16[64,576]{1,0:T(8,128)(2,1)S(1)}, bf16[64,576]{1,0:T(8,128)(2,1)S(1)}, u32[]{:S(2)}, u32[]{:S(2)}) collective-permute-start(bf16[64,576]{1,0:T(8,128)(2,1)S(1)} %get-tuple-element.25), channel_id=1, source_target_pairs={{0,256},{2,258},{4,260},{6,262},{8,264},{10,266},{12,268},{14,270}... | collective-permute-start | bytes 221192 | tf_op jit(solution)/shard_map/ppermute | solution.py:163
  6.7 29.7 %collective-permute-start.2 = (bf16[64,576]{1,0:T(8,128)(2,1)S(1)}, bf16[64,576]{1,0:T(8,128)(2,1)S(1)}, u32[]{:S(2)}, u32[]{:S(2)}) collective-permute-start(bf16[64,576]{1,0:T(8,128)(2,1)S(1)} %get-tuple-element.26), channel_id=1, source_target_pairs={{0,384},{2,386},{4,388},{6,390},{8,392},{10,394},{12,396},{14,398}... | collective-permute-start | bytes 221192 | tf_op jit(solution)/shard_map/ppermute | solution.py:163
  8.0 28.4 %collective-permute-start.3 = (bf16[64,576]{1,0:T(8,128)(2,1)S(1)}, bf16[64,576]{1,0:T(8,128)(2,1)S(1)}, u32[]{:S(2)}, u32[]{:S(2)}) collective-permute-start(bf16[64,576]{1,0:T(8,128)(2,1)S(1)} %get-tuple-element.27), channel_id=1, source_target_pairs={{0,449},{2,451},{4,453},{6,455},{8,457},{10,459},{12,461},{14,463}... | collective-permute-start | bytes 221192 | tf_op jit(solution)/shard_map/ppermute | solution.py:163

commit v4 on v3

--- a/solution.py
+++ b/solution.py
@@ -8,7 +8,7 @@
 KV_RANK = 512
 PEERS = 32
 LINE = 4
-AHEAD = (1, 0, 2, 3)
+AHEAD = (1, 2, 3, 0)
 
 score_scale = 192.0 ** (-0.5)
 masked_score = -1e30
@@ -75,9 +75,13 @@
     scores = jnp.where(step <= query_step, scores, masked_score)
     expo = jnp.exp(scores - jnp.max(scores, axis=0, keepdims=True))
     total = jnp.sum(expo, axis=0, keepdims=True)
-    mixed = product(expo.astype(jnp.bfloat16), keys[:, :KV_RANK], ((0,), (0,)))
     share = jnp.transpose(jnp.broadcast_to(1.0 / total, (8, total.shape[1])))[:, :1]
-    return (mixed * share).astype(jnp.bfloat16).reshape(-1, head_count, KV_RANK)
+    weights = expo.astype(jnp.bfloat16)
+    width = 2 * head_count
+    for start in range(0, weights.shape[1], width):
+        mixed = product(weights[:, start : start + width], keys[:, :KV_RANK], ((0,), (0,)))
+        mixed = mixed * share[start : start + width]
+        yield mixed.astype(jnp.bfloat16).reshape(-1, head_count, KV_RANK)
 
 
 def middle_kernel(
@@ -87,7 +91,7 @@
 
     @pl.when(decode)
     def _():
-        first_ref[...] = resident(length_ref[0], flat_rows(query_ref, 0), step_ref[0], cache_ref[0])
+        first_ref[...] = resident(length_ref[...], flat_rows(query_ref, 0), step_ref[0], cache_ref[0])
         query_t_ref[...] = jnp.transpose(flat_rows(query_ref, 1))
         tail_ref[...] = jnp.zeros_like(tail_ref)
         tail_ref[: step_ref.shape[1]] = step_ref[1]
@@ -120,15 +124,22 @@
         before.start()
         keys = jnp.concatenate([ref[...] for ref in part_refs] + [tail_ref[...]], axis=0)
         base_count = keys.shape[0] - tail_ref.shape[0]
-        result[1] = arrived_and_steps(query_t_ref[...], keys, base_count, query_ref.shape[2])
-        after = pltpu.make_async_copy(result.at[1], out_ref.at[1], sems.at[1])
-        after.start()
-        before.wait()
-        after.wait()
+        copies = [before]
+        for part, attended in enumerate(
+            arrived_and_steps(query_t_ref[...], keys, base_count, query_ref.shape[2])
+        ):
+            steps = pl.ds(part * attended.shape[0], attended.shape[0])
+            result[1, steps] = attended
+            copies.append(
+                pltpu.make_async_copy(result.at[1, steps], out_ref.at[1, steps], sems.at[1 + part])
+            )
+            copies[-1].start()
+        for copy in copies:
+            copy.wait()
 
     @pl.when(jnp.logical_not(decode))
     def _():
-        result[0] = resident(length_ref[0], flat_rows(query_ref, 0), step_ref[0], cache_ref[0])
+        result[0] = resident(length_ref[...], flat_rows(query_ref, 0), step_ref[0], cache_ref[0])
         before = pltpu.make_async_copy(result.at[0], out_ref.at[0], sems.at[0])
         before.start()
         result[1] = steps_only(flat_rows(query_ref, 1), step_ref[1])
@@ -139,7 +150,6 @@
 
 
 vmem = pl.BlockSpec(memory_space=pltpu.VMEM)
-smem = pl.BlockSpec(memory_space=pltpu.SMEM)
 anywhere = pl.BlockSpec(memory_space=pl.ANY)
 params = pltpu.CompilerParams(vmem_limit_bytes=16 << 20)
 
@@ -168,6 +178,7 @@
     row_total = outgoing.shape[0]
     first_shape = jax.ShapeDtypeStruct((steps_total, head_count, KV_RANK), jnp.bfloat16)
     keys = cache.transpose(0, 2, 1)
+    length = lengths.reshape(1, 1)
 
     query_rows = steps_total * head_count
     run = jnp.arange(row_total, dtype=jnp.int32) // (row_total // 2)
@@ -195,22 +206,22 @@
             jax.ShapeDtypeStruct((16, latent_width), jnp.bfloat16),
         ]
         + [jax.ShapeDtypeStruct((row_total // LINE, latent_width), jnp.bfloat16)] * LINE,
-        in_specs=[smem] + [vmem] * 4,
+        in_specs=[vmem] * 5,
         out_specs=[vmem] * (3 + LINE),
         compiler_params=params,
-    )(lengths, queries, step_rows, keys, moved.reshape(row_total, latent_width))
+    )(length, queries, step_rows, keys, moved.reshape(row_total, latent_width))
     arrived = [along_line(part, ahead) for part, ahead in zip(parts, AHEAD)]
     return pl.pallas_call(
         last_kernel,
         out_shape=jax.ShapeDtypeStruct((seq_count,) + first_shape.shape, jnp.bfloat16),
-        in_specs=[smem] + [vmem] * (6 + LINE),
+        in_specs=[vmem] * (7 + LINE),
         out_specs=anywhere,
         scratch_shapes=[
             pltpu.VMEM((seq_count,) + first_shape.shape, jnp.bfloat16),
-            pltpu.SemaphoreType.DMA((2,)),
+            pltpu.SemaphoreType.DMA((3,)),
         ],
         compiler_params=params,
-    )(lengths, queries, step_rows, keys, first, query_t, tail, *arrived)
+    )(length, queries, step_rows, keys, first, query_t, tail, *arrived)
 
 
 def solution(mesh):

time: 38.3 us -> 36.9 us (0.963)
  waiting for transfers between devices: 27.1 us -> 25.8 us
    ppermute x4, waiting for transfers between devices: 27.1 us -> 25.8 us  [along_line(): return lax.ppermute(rows, ('group', 'pair', 'z', 'x', 'y', 'tp'), pairs)]
where the time goes in v4:
time: 36.9 us; the launch traced here: 36.7 us
  waiting for transfers between devices  25.8 us (70%)
  starting transfers between devices  5.17 us (14%)
  Pallas kernels  3.06 us (8%)
  local copies, waits for them, and re-layouts  1.86 us (5%)
  between operations  0.75 us (2%)
    ppermute x4, waiting for transfers between devices, along_line(): return lax.ppermute(rows, ('group', 'pair', 'z', 'x', 'y', 'tp'), pairs)  25.8 us
    ppermute x4, starting transfers between devices, along_line(): return lax.ppermute(rows, ('group', 'pair', 'z', 'x', 'y', 'tp'), pairs)  5.17 us
    unnamed x8, local copies, waits for them, and re-layouts  1.86 us
    pallas_call x1, Pallas kernels, shards(): pl.pallas_call(last_kernel, out_shape=jax.ShapeDtypeStruct((seq_count,) +...  1.57 us
    pallas_call x1, Pallas kernels, shards(): pl.pallas_call(middle_kernel, out_shape=[first_shape, jax.ShapeDtypeStruc...  1.2 us
  transfers between devices with their start and end apart: 4, of which 2 were waited for; matrix products, arithmetic and copies ran while one was open for 0% of the time, Pallas kernels for 0%

profile of v4, /device:TPU:1, one launch (start us, length us, event | category | flops | bytes accessed | tf_op | source)
XLA Modules:
  0.0 36.7 jit_solution(3854848474940369427)
XLA Ops:
  0.7 0.0 copy-start.3
  0.7 0.6 %copy-done.3 = s32[256]{0:T(256)S(1)} copy-done((s32[256]{0:T(256)S(1)}, s32[256]{0:T(256)}, u32[]{:S(2)}) %copy-start.3) | copy-done | bytes 1048
  1.4 0.3 shard_map.64
  1.7 0.0 copy-start
  1.7 0.0 copy-start.1
  1.7 0.0 copy-start.2
  1.7 1.0 %copy-done = bf16[2,4,64,576]{3,2,1,0:T(8,128)(2,1)S(1)} copy-done((bf16[2,4,64,576]{3,2,1,0:T(8,128)(2,1)S(1)}, bf16[2,4,64,576]{3,2,1,0:T(8,128)(2,1)}, u32[]{:S(2)}) %copy-start) | copy-done | bytes 589848
  2.7 0.2 copy-done.1
  2.9 0.0 copy-done.2
  2.9 1.2 %shard_map.65 = (bf16[4,64,512]{2,1,0:T(8,128)(2,1)S(1)}, bf16[576,256]{1,0:T(8,128)(2,1)S(1)}, bf16[16,576]{1,0:T(8,128)(2,1)S(1)}, bf16[64,576]{1,0:T(8,128)(2...) custom-call(s32[1,1]{1,0:T(1,128)} %bitcast.7.length_ref, ...), custom_call_target="tpu_custom_call" | custom-call | tf_op jit(solution)/shard_map/pallas_call | solution.py:201
  4.1 1.3 %collective-permute-start = (bf16[64,576]{1,0:T(8,128)(2,1)S(1)}, bf16[64,576]{1,0:T(8,128)(2,1)S(1)}, u32[]{:S(2)}, u32[]{:S(2)}) collective-permute-start(bf16[64,576]{1,0:T(8,128)(2,1)S(1)} %get-tuple-element.24), channel_id=1, source_target_pairs={{0,320},{2,322},{4,324},{6,326},{8,328},{10,330},{12,332},{14,334}... | collective-permute-start | bytes 221192 | tf_op jit(solution)/shard_map/ppermute | solution.py:173
  5.4 1.3 %collective-permute-start.1 = (bf16[64,576]{1,0:T(8,128)(2,1)S(1)}, bf16[64,576]{1,0:T(8,128)(2,1)S(1)}, u32[]{:S(2)}, u32[]{:S(2)}) collective-permute-start(bf16[64,576]{1,0:T(8,128)(2,1)S(1)} %get-tuple-element.25), channel_id=1, source_target_pairs={{0,384},{2,386},{4,388},{6,390},{8,392},{10,394},{12,396},{14,398}... | collective-permute-start | bytes 221192 | tf_op jit(solution)/shard_map/ppermute | solution.py:173
  6.7 1.3 %collective-permute-start.2 = (bf16[64,576]{1,0:T(8,128)(2,1)S(1)}, bf16[64,576]{1,0:T(8,128)(2,1)S(1)}, u32[]{:S(2)}, u32[]{:S(2)}) collective-permute-start(bf16[64,576]{1,0:T(8,128)(2,1)S(1)} %get-tuple-element.26), channel_id=1, source_target_pairs={{0,449},{2,451},{4,453},{6,455},{8,457},{10,459},{12,461},{14,463}... | collective-permute-start | bytes 221192 | tf_op jit(solution)/shard_map/ppermute | solution.py:173
  8.0 1.3 %collective-permute-start.3 = (bf16[64,576]{1,0:T(8,128)(2,1)S(1)}, bf16[64,576]{1,0:T(8,128)(2,1)S(1)}, u32[]{:S(2)}, u32[]{:S(2)}) collective-permute-start(bf16[64,576]{1,0:T(8,128)(2,1)S(1)} %get-tuple-element.27), channel_id=1, source_target_pairs={{0,256},{2,258},{4,260},{6,262},{8,264},{10,266},{12,268},{14,270}... | collective-permute-start | bytes 221192 | tf_op jit(solution)/shard_map/ppermute | solution.py:173
  9.3 25.3 %collective-permute-done.refs_0_ = bf16[64,576]{1,0:T(8,128)(2,1)S(1)} collective-permute-done((bf16[64,576]{1,0:T(8,128)(2,1)S(1)}, bf16[64,576]{1,0:T(8,128)(2,1)S(1)}, u32[]{:S(2)}, u32[]{:S(2)}) %collective-permute-start) | collective-permute-done | bytes 73760 | tf_op jit(solution)/shard_map/ppermute | solution.py:173
  34.6 0.5 %collective-permute-done.1.refs_1_ = bf16[64,576]{1,0:T(8,128)(2,1)S(1)} collective-permute-done((bf16[64,576]{1,0:T(8,128)(2,1)S(1)}, bf16[64,576]{1,0:T(8,128)(2,1)S(1)}, u32[]{:S(2)}, u32[]{:S(2)}) %collective-permute-start.1) | collective-permute-done | bytes 73760 | tf_op jit(solution)/shard_map/ppermute | solution.py:173
  35.1 0.0 collective-permute-done.2.refs_2_
  35.1 0.0 collective-permute-done.3.refs_3_
  35.1 1.6 %shard_map.66 = bf16[2,4,64,512]{3,2,1,0:T(8,128)(2,1)} custom-call(s32[1,1]{1,0:T(1,128)} %bitcast.8.length_ref, bf16[2,4,64,576]{3,2,1,0:T(8,128)(2,1)S(1)} %copy-done, bf16[2,4,576]{2,1,0:T(4,128)(2,1)S(1)} %copy-done.2, bf16[1,576,512]{2,1,0:T(8,128)(2,1)S(1)} %bitcast.10, bf16[4,64,512]{2,1,0:T(8,128)(2,1)S(1)} %get-tuple-element.21.first_ref, ...), custom_call_target="tpu_custom_call" | custom-call | tf_op jit(solution)/shard_map/pallas_call | solution.py:214
  (3 shorter events, 0.1 us)
Async XLA Ops:
  0.7 0.7 %copy-start.3 = (s32[256]{0:T(256)S(1)}, s32[256]{0:T(256)}, u32[]{:S(2)}) copy-start(s32[256]{0:T(256)} %param.13) | copy-start | bytes 3076
  1.7 1.1 %copy-start = (bf16[2,4,64,576]{3,2,1,0:T(8,128)(2,1)S(1)}, bf16[2,4,64,576]{3,2,1,0:T(8,128)(2,1)}, u32[]{:S(2)}) copy-start(bf16[2,4,64,576]{3,2,1,0:T(8,128)(2,1)} %query_ref.3) | copy-start | bytes 1769476
  1.7 1.3 %copy-start.1 = (bf16[1,512,576]{1,2,0:T(8,128)(2,1)S(1)}, bf16[1,512,576]{1,2,0:T(8,128)(2,1)}, u32[]{:S(2)}) copy-start(bf16[1,512,576]{1,2,0:T(8,128)(2,1)} %param.10) | copy-start | bytes 1769476
  1.7 1.2 %copy-start.2 = (bf16[2,4,576]{2,1,0:T(4,128)(2,1)S(1)}, bf16[2,4,576]{2,1,0:T(4,128)(2,1)}, u32[]{:S(2)}) copy-start(bf16[2,4,576]{2,1,0:T(4,128)(2,1)} %step_ref.3) | copy-start | bytes 27652
  4.1 30.5 %collective-permute-start = (bf16[64,576]{1,0:T(8,128)(2,1)S(1)}, bf16[64,576]{1,0:T(8,128)(2,1)S(1)}, u32[]{:S(2)}, u32[]{:S(2)}) collective-permute-start(bf16[64,576]{1,0:T(8,128)(2,1)S(1)} %get-tuple-element.24), channel_id=1, source_target_pairs={{0,320},{2,322},{4,324},{6,326},{8,328},{10,330},{12,332},{14,334}... | collective-permute-start | bytes 221192 | tf_op jit(solution)/shard_map/ppermute | solution.py:173
  5.4 29.7 %collective-permute-start.1 = (bf16[64,576]{1,0:T(8,128)(2,1)S(1)}, bf16[64,576]{1,0:T(8,128)(2,1)S(1)}, u32[]{:S(2)}, u32[]{:S(2)}) collective-permute-start(bf16[64,576]{1,0:T(8,128)(2,1)S(1)} %get-tuple-element.25), channel_id=1, source_target_pairs={{0,384},{2,386},{4,388},{6,390},{8,392},{10,394},{12,396},{14,398}... | collective-permute-start | bytes 221192 | tf_op jit(solution)/shard_map/ppermute | solution.py:173
  6.7 28.4 %collective-permute-start.2 = (bf16[64,576]{1,0:T(8,128)(2,1)S(1)}, bf16[64,576]{1,0:T(8,128)(2,1)S(1)}, u32[]{:S(2)}, u32[]{:S(2)}) collective-permute-start(bf16[64,576]{1,0:T(8,128)(2,1)S(1)} %get-tuple-element.26), channel_id=1, source_target_pairs={{0,449},{2,451},{4,453},{6,455},{8,457},{10,459},{12,461},{14,463}... | collective-permute-start | bytes 221192 | tf_op jit(solution)/shard_map/ppermute | solution.py:173
  8.0 27.1 %collective-permute-start.3 = (bf16[64,576]{1,0:T(8,128)(2,1)S(1)}, bf16[64,576]{1,0:T(8,128)(2,1)S(1)}, u32[]{:S(2)}, u32[]{:S(2)}) collective-permute-start(bf16[64,576]{1,0:T(8,128)(2,1)S(1)} %get-tuple-element.27), channel_id=1, source_target_pairs={{0,256},{2,258},{4,260},{6,262},{8,264},{10,266},{12,268},{14,270}... | collective-permute-start | bytes 221192 | tf_op jit(solution)/shard_map/ppermute | solution.py:173

commit v5 on v4

--- a/solution.py
+++ b/solution.py
@@ -7,6 +7,7 @@
 
 KV_RANK = 512
 PEERS = 32
+lap = 64
 LINE = 4
 AHEAD = (1, 2, 3, 0)
 
@@ -24,9 +25,21 @@
 
 
 def pack_kernel(slot_ref, latent_ref, packed_ref):
-    count = slot_ref.shape[1]
-    rows = lax.broadcasted_iota(jnp.int32, (count, count), 0)
-    packed_ref[...] = picked(rows == slot_ref[...], latent_ref[...], ((1,), (1,)))
+    width, count = latent_ref.shape
+    each = count // 2
+    rows = lax.broadcasted_iota(jnp.int32, (each, each), 0)
+    blank = jnp.zeros((lap, each), latent_ref.dtype)
+    first = picked(
+        rows == slot_ref[:, :each], jnp.concatenate([latent_ref[:, :each], blank]), ((1,), (1,))
+    )
+    second = picked(
+        rows == slot_ref[:, each:], jnp.concatenate([blank, latent_ref[:, each:]]), ((1,), (1,))
+    )
+    inner = width - lap
+    both = jnp.concatenate(
+        [first[:, :inner], first[:, inner:] + second[:, : 2 * lap], second[:, 2 * lap :]], axis=1
+    )
+    packed_ref[...] = both.reshape(packed_ref.shape)
 
 
 def flat_rows(query_ref, seq):
@@ -91,25 +104,24 @@
 
     @pl.when(decode)
     def _():
-        first_ref[...] = resident(length_ref[...], flat_rows(query_ref, 0), step_ref[0], cache_ref[0])
+        first_ref[...] = resident(length_ref[0], flat_rows(query_ref, 0), step_ref[0], cache_ref[0])
         query_t_ref[...] = jnp.transpose(flat_rows(query_ref, 1))
         tail_ref[...] = jnp.zeros_like(tail_ref)
         tail_ref[: step_ref.shape[1]] = step_ref[1]
 
     @pl.when(jnp.logical_not(decode))
     def _():
-        count = moved_ref.shape[0]
+        count = moved_ref.shape[0] * moved_ref.shape[1]
         rows = lax.broadcasted_iota(jnp.int32, (count, count), 0)
         cols = lax.broadcasted_iota(jnp.int32, (count, count), 1)
-        run, peer, part = rows % 2, (rows // 2) % PEERS, rows // (2 * PEERS)
+        peer, part = rows % PEERS, rows // PEERS
         ahead = jnp.zeros_like(part)
         for index, part_ahead in enumerate(AHEAD):
             ahead = jnp.where(part == index, part_ahead, ahead)
-        source = (peer * LINE + ahead) * 2 + run
-        turned = picked(cols == source, moved_ref[...], ((1,), (0,)))
-        step = count // LINE
+        moved = moved_ref[...].reshape(count, moved_ref.shape[2])
+        turned = picked(cols == peer * LINE + ahead, moved, ((1,), (0,)))
         for part, part_ref in enumerate(part_refs):
-            part_ref[...] = turned[part * step : (part + 1) * step]
+            part_ref[...] = turned[part * PEERS : (part + 1) * PEERS]
 
 
 def last_kernel(
@@ -122,7 +134,9 @@
     def _():
         before = pltpu.make_async_copy(first_ref, out_ref.at[0], sems.at[0])
         before.start()
-        keys = jnp.concatenate([ref[...] for ref in part_refs] + [tail_ref[...]], axis=0)
+        both = jnp.concatenate([ref[...] for ref in part_refs], axis=0)
+        width = tail_ref.shape[1]
+        keys = jnp.concatenate([both[:, :width], both[:, width:], tail_ref[...]], axis=0)
         base_count = keys.shape[0] - tail_ref.shape[0]
         copies = [before]
         for part, attended in enumerate(
@@ -139,7 +153,7 @@
 
     @pl.when(jnp.logical_not(decode))
     def _():
-        result[0] = resident(length_ref[...], flat_rows(query_ref, 0), step_ref[0], cache_ref[0])
+        result[0] = resident(length_ref[0], flat_rows(query_ref, 0), step_ref[0], cache_ref[0])
         before = pltpu.make_async_copy(result.at[0], out_ref.at[0], sems.at[0])
         before.start()
         result[1] = steps_only(flat_rows(query_ref, 1), step_ref[1])
@@ -150,6 +164,7 @@
 
 
 vmem = pl.BlockSpec(memory_space=pltpu.VMEM)
+smem = pl.BlockSpec(memory_space=pltpu.SMEM)
 anywhere = pl.BlockSpec(memory_space=pl.ANY)
 params = pltpu.CompilerParams(vmem_limit_bytes=16 << 20)
 
@@ -178,16 +193,14 @@
     row_total = outgoing.shape[0]
     first_shape = jax.ShapeDtypeStruct((steps_total, head_count, KV_RANK), jnp.bfloat16)
     keys = cache.transpose(0, 2, 1)
-    length = lengths.reshape(1, 1)
 
     query_rows = steps_total * head_count
-    run = jnp.arange(row_total, dtype=jnp.int32) // (row_total // 2)
     ahead = (crossing // PEERS - lax.axis_index("pair") + LINE) % LINE
-    slots = ((crossing % PEERS) * LINE + ahead) * 2 + run
+    slots = (crossing % PEERS) * LINE + ahead
     mine = jnp.where(lax.axis_index("group") == 0, outgoing.T, jnp.zeros((), outgoing.dtype))
     packed = pl.pallas_call(
         pack_kernel,
-        out_shape=jax.ShapeDtypeStruct((row_total, latent_width), jnp.bfloat16),
+        out_shape=jax.ShapeDtypeStruct((PEERS, LINE, 2 * latent_width), jnp.bfloat16),
         in_specs=[vmem] * 2,
         out_specs=vmem,
         compiler_params=params,
@@ -196,7 +209,7 @@
         lax.axis_index("group") == 0,
         lambda rows: lax.all_to_all(rows, ("z", "x", "y"), 0, 0, tiled=True),
         lambda rows: rows,
-        packed.reshape(PEERS, row_total // PEERS, latent_width),
+        packed,
     )
     first, query_t, tail, *parts = pl.pallas_call(
         middle_kernel,
@@ -205,23 +218,23 @@
             jax.ShapeDtypeStruct((latent_width, query_rows), jnp.bfloat16),
             jax.ShapeDtypeStruct((16, latent_width), jnp.bfloat16),
         ]
-        + [jax.ShapeDtypeStruct((row_total // LINE, latent_width), jnp.bfloat16)] * LINE,
-        in_specs=[vmem] * 5,
+        + [jax.ShapeDtypeStruct((PEERS, 2 * latent_width), jnp.bfloat16)] * LINE,
+        in_specs=[smem] + [vmem] * 4,
         out_specs=[vmem] * (3 + LINE),
         compiler_params=params,
-    )(length, queries, step_rows, keys, moved.reshape(row_total, latent_width))
+    )(lengths, queries, step_rows, keys, moved)
     arrived = [along_line(part, ahead) for part, ahead in zip(parts, AHEAD)]
     return pl.pallas_call(
         last_kernel,
         out_shape=jax.ShapeDtypeStruct((seq_count,) + first_shape.shape, jnp.bfloat16),
-        in_specs=[vmem] * (7 + LINE),
+        in_specs=[smem] + [vmem] * (6 + LINE),
         out_specs=anywhere,
         scratch_shapes=[
             pltpu.VMEM((seq_count,) + first_shape.shape, jnp.bfloat16),
             pltpu.SemaphoreType.DMA((3,)),
         ],
         compiler_params=params,
-    )(length, queries, step_rows, keys, first, query_t, tail, *arrived)
+    )(lengths, queries, step_rows, keys, first, query_t, tail, *arrived)
 
 
 def solution(mesh):

time: 36.9 us -> 36.6 us (level)
  no operation moved by 1% of the time
where the time goes in v5:
time: 36.6 us; the launch traced here: 36.3 us
  waiting for transfers between devices  25.6 us (70%)
  starting transfers between devices  5.17 us (14%)
  Pallas kernels  3.04 us (8%)
  local copies, waits for them, and re-layouts  1.73 us (5%)
  between operations  0.75 us (2%)
    ppermute x4, waiting for transfers between devices, along_line(): return lax.ppermute(rows, ('group', 'pair', 'z', 'x', 'y', 'tp'), pairs)  25.6 us
    ppermute x4, starting transfers between devices, along_line(): return lax.ppermute(rows, ('group', 'pair', 'z', 'x', 'y', 'tp'), pairs)  5.17 us
    unnamed x8, local copies, waits for them, and re-layouts  1.73 us
    pallas_call x1, Pallas kernels, shards(): pl.pallas_call(last_kernel, out_shape=jax.ShapeDtypeStruct((seq_count,) +...  1.57 us
    pallas_call x1, Pallas kernels, shards(): pl.pallas_call(middle_kernel, out_shape=[first_shape, jax.ShapeDtypeStruc...  1.2 us
  transfers between devices with their start and end apart: 4, of which 2 were waited for; matrix products, arithmetic and copies ran while one was open for 0% of the time, Pallas kernels for 0%

profile of v5, /device:TPU:1, one launch (start us, length us, event | category | flops | bytes accessed | tf_op | source)
XLA Modules:
  0.0 36.3 jit_solution(15004628525393214088)
XLA Ops:
  0.7 0.0 copy-start.3
  0.7 0.6 %copy-done.3 = s32[256]{0:T(256)S(1)} copy-done((s32[256]{0:T(256)S(1)}, s32[256]{0:T(256)}, u32[]{:S(2)}) %copy-start.3) | copy-done | bytes 1048
  1.4 0.0 copy-start.1
  1.4 0.3 shard_map.64
  1.6 0.0 copy-start
  1.6 0.0 copy-start.2
  1.7 0.7 %copy-done.1 = bf16[1,512,576]{1,2,0:T(8,128)(2,1)S(1)} copy-done((bf16[1,512,576]{1,2,0:T(8,128)(2,1)S(1)}, bf16[1,512,576]{1,2,0:T(8,128)(2,1)}, u32[]{:S(2)}) %copy-start.1) | copy-done | bytes 589848
  2.4 0.3 copy-done
  2.8 0.0 copy-done.2
  2.8 1.2 %shard_map.65 = (bf16[4,64,512]{2,1,0:T(8,128)(2,1)S(1)}, bf16[576,256]{1,0:T(8,128)(2,1)S(1)}, bf16[16,576]{1,0:T(8,128)(2,1)S(1)}, bf16[32,1152]{1,0:T(8,128)(...) custom-call(s32[1]{0:T(128)S(6)} %copy.9.length_ref, ...), custom_call_target="tpu_custom_call" | custom-call | tf_op jit(solution)/shard_map/pallas_call | solution.py:214
  4.0 1.3 %collective-permute-start = (bf16[32,1152]{1,0:T(8,128)(2,1)S(1)}, bf16[32,1152]{1,0:T(8,128)(2,1)S(1)}, u32[]{:S(2)}, u32[]{:S(2)}) collective-permute-start(bf16[32,1152]{1,0:T(8,128)(2,1)S(1)} %get-tuple-element.20), channel_id=1, source_target_pairs={{0,320},{2,322},{4,324},{6,326},{8,328},{10,330},{12,332},{14,334}... | collective-permute-start | bytes 221192 | tf_op jit(solution)/shard_map/ppermute | solution.py:188
  5.3 1.3 %collective-permute-start.1 = (bf16[32,1152]{1,0:T(8,128)(2,1)S(1)}, bf16[32,1152]{1,0:T(8,128)(2,1)S(1)}, u32[]{:S(2)}, u32[]{:S(2)}) collective-permute-start(bf16[32,1152]{1,0:T(8,128)(2,1)S(1)} %get-tuple-element.21), channel_id=1, source_target_pairs={{0,384},{2,386},{4,388},{6,390},{8,392},{10,394},{12,396},{14,398}... | collective-permute-start | bytes 221192 | tf_op jit(solution)/shard_map/ppermute | solution.py:188
  6.6 1.3 %collective-permute-start.2 = (bf16[32,1152]{1,0:T(8,128)(2,1)S(1)}, bf16[32,1152]{1,0:T(8,128)(2,1)S(1)}, u32[]{:S(2)}, u32[]{:S(2)}) collective-permute-start(bf16[32,1152]{1,0:T(8,128)(2,1)S(1)} %get-tuple-element.22), channel_id=1, source_target_pairs={{0,449},{2,451},{4,453},{6,455},{8,457},{10,459},{12,461},{14,463}... | collective-permute-start | bytes 221192 | tf_op jit(solution)/shard_map/ppermute | solution.py:188
  7.9 1.3 %collective-permute-start.3 = (bf16[32,1152]{1,0:T(8,128)(2,1)S(1)}, bf16[32,1152]{1,0:T(8,128)(2,1)S(1)}, u32[]{:S(2)}, u32[]{:S(2)}) collective-permute-start(bf16[32,1152]{1,0:T(8,128)(2,1)S(1)} %get-tuple-element.23), channel_id=1, source_target_pairs={{0,256},{2,258},{4,260},{6,262},{8,264},{10,266},{12,268},{14,270}... | collective-permute-start | bytes 221192 | tf_op jit(solution)/shard_map/ppermute | solution.py:188
  9.2 25.3 %collective-permute-done.refs_0_ = bf16[32,1152]{1,0:T(8,128)(2,1)S(1)} collective-permute-done((bf16[32,1152]{1,0:T(8,128)(2,1)S(1)}, bf16[32,1152]{1,0:T(8,128)(2,1)S(1)}, u32[]{:S(2)}, u32[]{:S(2)}) %collective-permute-start) | collective-permute-done | bytes 73760 | tf_op jit(solution)/shard_map/ppermute | solution.py:188
  34.5 0.3 collective-permute-done.1.refs_1_
  34.7 0.0 collective-permute-done.2.refs_2_
  34.8 0.0 collective-permute-done.3.refs_3_
  34.8 1.6 %shard_map.66 = bf16[2,4,64,512]{3,2,1,0:T(8,128)(2,1)} custom-call(s32[1]{0:T(128)S(6)} %copy.9.length_ref, bf16[2,4,64,576]{3,2,1,0:T(8,128)(2,1)S(1)} %copy-done, bf16[2,4,576]{2,1,0:T(4,128)(2,1)S(1)} %copy-done.2, bf16[1,576,512]{2,1,0:T(8,128)(2,1)S(1)} %bitcast.5, bf16[4,64,512]{2,1,0:T(8,128)(2,1)S(1)} %get-tuple-element.17.first_ref, ...), custom_call_target="tpu_custom_call" | custom-call | tf_op jit(solution)/shard_map/pallas_call | solution.py:227
  (3 shorter events, 0.1 us)
Async XLA Ops:
  0.7 0.7 %copy-start.3 = (s32[256]{0:T(256)S(1)}, s32[256]{0:T(256)}, u32[]{:S(2)}) copy-start(s32[256]{0:T(256)} %param.13) | copy-start | bytes 3076
  1.4 1.1 %copy-start.1 = (bf16[1,512,576]{1,2,0:T(8,128)(2,1)S(1)}, bf16[1,512,576]{1,2,0:T(8,128)(2,1)}, u32[]{:S(2)}) copy-start(bf16[1,512,576]{1,2,0:T(8,128)(2,1)} %param.10) | copy-start | bytes 1769476
  1.6 1.1 %copy-start = (bf16[2,4,64,576]{3,2,1,0:T(8,128)(2,1)S(1)}, bf16[2,4,64,576]{3,2,1,0:T(8,128)(2,1)}, u32[]{:S(2)}) copy-start(bf16[2,4,64,576]{3,2,1,0:T(8,128)(2,1)} %query_ref.3) | copy-start | bytes 1769476
  1.6 1.1 %copy-start.2 = (bf16[2,4,576]{2,1,0:T(4,128)(2,1)S(1)}, bf16[2,4,576]{2,1,0:T(4,128)(2,1)}, u32[]{:S(2)}) copy-start(bf16[2,4,576]{2,1,0:T(4,128)(2,1)} %step_ref.3) | copy-start | bytes 27652
  4.0 30.5 %collective-permute-start = (bf16[32,1152]{1,0:T(8,128)(2,1)S(1)}, bf16[32,1152]{1,0:T(8,128)(2,1)S(1)}, u32[]{:S(2)}, u32[]{:S(2)}) collective-permute-start(bf16[32,1152]{1,0:T(8,128)(2,1)S(1)} %get-tuple-element.20), channel_id=1, source_target_pairs={{0,320},{2,322},{4,324},{6,326},{8,328},{10,330},{12,332},{14,334}... | collective-permute-start | bytes 221192 | tf_op jit(solution)/shard_map/ppermute | solution.py:188
  5.3 29.5 %collective-permute-start.1 = (bf16[32,1152]{1,0:T(8,128)(2,1)S(1)}, bf16[32,1152]{1,0:T(8,128)(2,1)S(1)}, u32[]{:S(2)}, u32[]{:S(2)}) collective-permute-start(bf16[32,1152]{1,0:T(8,128)(2,1)S(1)} %get-tuple-element.21), channel_id=1, source_target_pairs={{0,384},{2,386},{4,388},{6,390},{8,392},{10,394},{12,396},{14,398}... | collective-permute-start | bytes 221192 | tf_op jit(solution)/shard_map/ppermute | solution.py:188
  6.6 28.2 %collective-permute-start.2 = (bf16[32,1152]{1,0:T(8,128)(2,1)S(1)}, bf16[32,1152]{1,0:T(8,128)(2,1)S(1)}, u32[]{:S(2)}, u32[]{:S(2)}) collective-permute-start(bf16[32,1152]{1,0:T(8,128)(2,1)S(1)} %get-tuple-element.22), channel_id=1, source_target_pairs={{0,449},{2,451},{4,453},{6,455},{8,457},{10,459},{12,461},{14,463}... | collective-permute-start | bytes 221192 | tf_op jit(solution)/shard_map/ppermute | solution.py:188
  7.9 26.9 %collective-permute-start.3 = (bf16[32,1152]{1,0:T(8,128)(2,1)S(1)}, bf16[32,1152]{1,0:T(8,128)(2,1)S(1)}, u32[]{:S(2)}, u32[]{:S(2)}) collective-permute-start(bf16[32,1152]{1,0:T(8,128)(2,1)S(1)} %get-tuple-element.23), channel_id=1, source_target_pairs={{0,256},{2,258},{4,260},{6,262},{8,264},{10,266},{12,268},{14,270}... | collective-permute-start | bytes 221192 | tf_op jit(solution)/shard_map/ppermute | solution.py:188

commit v6 on v5

--- a/solution.py
+++ b/solution.py
@@ -97,14 +97,15 @@
         yield mixed.astype(jnp.bfloat16).reshape(-1, head_count, KV_RANK)
 
 
-def middle_kernel(
-    length_ref, query_ref, step_ref, cache_ref, moved_ref, first_ref, query_t_ref, tail_ref, *part_refs
-):
+def resident_kernel(length_ref, query_ref, step_ref, cache_ref, after_ref, first_ref):
+    first_ref[...] = resident(length_ref[0], flat_rows(query_ref, 0), step_ref[0], cache_ref[0])
+
+
+def middle_kernel(query_ref, step_ref, moved_ref, query_t_ref, tail_ref, *part_refs):
     decode = lax.axis_index("group") == 1
 
     @pl.when(decode)
     def _():
-        first_ref[...] = resident(length_ref[0], flat_rows(query_ref, 0), step_ref[0], cache_ref[0])
         query_t_ref[...] = jnp.transpose(flat_rows(query_ref, 1))
         tail_ref[...] = jnp.zeros_like(tail_ref)
         tail_ref[: step_ref.shape[1]] = step_ref[1]
@@ -124,28 +125,26 @@
             part_ref[...] = turned[part * PEERS : (part + 1) * PEERS]
 
 
-def last_kernel(
-    length_ref, query_ref, step_ref, cache_ref, first_ref, query_t_ref, tail_ref, *refs
-):
+def last_kernel(query_ref, step_ref, first_ref, query_t_ref, tail_ref, *refs):
     part_refs, (out_ref, result, sems) = refs[:LINE], refs[LINE:]
     decode = lax.axis_index("group") == 1
+    before = pltpu.make_async_copy(first_ref, out_ref.at[0], sems.at[0])
+    before.start()
 
     @pl.when(decode)
     def _():
-        before = pltpu.make_async_copy(first_ref, out_ref.at[0], sems.at[0])
-        before.start()
         both = jnp.concatenate([ref[...] for ref in part_refs], axis=0)
         width = tail_ref.shape[1]
         keys = jnp.concatenate([both[:, :width], both[:, width:], tail_ref[...]], axis=0)
         base_count = keys.shape[0] - tail_ref.shape[0]
-        copies = [before]
+        copies = []
         for part, attended in enumerate(
             arrived_and_steps(query_t_ref[...], keys, base_count, query_ref.shape[2])
         ):
             steps = pl.ds(part * attended.shape[0], attended.shape[0])
-            result[1, steps] = attended
+            result[steps] = attended
             copies.append(
-                pltpu.make_async_copy(result.at[1, steps], out_ref.at[1, steps], sems.at[1 + part])
+                pltpu.make_async_copy(result.at[steps], out_ref.at[1, steps], sems.at[1 + part])
             )
             copies[-1].start()
         for copy in copies:
@@ -153,14 +152,12 @@
 
     @pl.when(jnp.logical_not(decode))
     def _():
-        result[0] = resident(length_ref[0], flat_rows(query_ref, 0), step_ref[0], cache_ref[0])
-        before = pltpu.make_async_copy(result.at[0], out_ref.at[0], sems.at[0])
-        before.start()
-        result[1] = steps_only(flat_rows(query_ref, 1), step_ref[1])
-        after = pltpu.make_async_copy(result.at[1], out_ref.at[1], sems.at[1])
+        result[...] = steps_only(flat_rows(query_ref, 1), step_ref[1])
+        after = pltpu.make_async_copy(result, out_ref.at[1], sems.at[1])
         after.start()
-        before.wait()
         after.wait()
+
+    before.wait()
 
 
 vmem = pl.BlockSpec(memory_space=pltpu.VMEM)
@@ -211,30 +208,36 @@
         lambda rows: rows,
         packed,
     )
-    first, query_t, tail, *parts = pl.pallas_call(
+    query_t, tail, *parts = pl.pallas_call(
         middle_kernel,
         out_shape=[
-            first_shape,
             jax.ShapeDtypeStruct((latent_width, query_rows), jnp.bfloat16),
             jax.ShapeDtypeStruct((16, latent_width), jnp.bfloat16),
         ]
         + [jax.ShapeDtypeStruct((PEERS, 2 * latent_width), jnp.bfloat16)] * LINE,
-        in_specs=[smem] + [vmem] * 4,
-        out_specs=[vmem] * (3 + LINE),
-        compiler_params=params,
-    )(lengths, queries, step_rows, keys, moved)
+        in_specs=[vmem] * 3,
+        out_specs=[vmem] * (2 + LINE),
+        compiler_params=params,
+    )(queries, step_rows, moved)
     arrived = [along_line(part, ahead) for part, ahead in zip(parts, AHEAD)]
+    first = pl.pallas_call(
+        resident_kernel,
+        out_shape=first_shape,
+        in_specs=[smem] + [vmem] * 3 + [anywhere],
+        out_specs=vmem,
+        compiler_params=params,
+    )(lengths, queries, step_rows, keys, tail)
     return pl.pallas_call(
         last_kernel,
         out_shape=jax.ShapeDtypeStruct((seq_count,) + first_shape.shape, jnp.bfloat16),
-        in_specs=[smem] + [vmem] * (6 + LINE),
+        in_specs=[vmem] * (5 + LINE),
         out_specs=anywhere,
         scratch_shapes=[
-            pltpu.VMEM((seq_count,) + first_shape.shape, jnp.bfloat16),
+            pltpu.VMEM(first_shape.shape, jnp.bfloat16),
             pltpu.SemaphoreType.DMA((3,)),
         ],
         compiler_params=params,
-    )(lengths, queries, step_rows, keys, first, query_t, tail, *arrived)
+    )(queries, step_rows, first, query_t, tail, *arrived)
 
 
 def solution(mesh):

time: 36.6 us -> 35.9 us (0.981)
  waiting for transfers between devices: 25.6 us -> 24.8 us
    ppermute x4, waiting for transfers between devices: 25.6 us -> 24.8 us  [along_line(): return lax.ppermute(rows, ('group', 'pair', 'z', 'x', 'y', 'tp'), pairs)]
    pallas_call x1 -> x2, Pallas kernels: 1.2 us -> 1.33 us  [the longest x1 1.2 us: shards(): pl.pallas_call(resident_kernel, out_shape=first_shape, in_specs=[smem] +...]
  transfers between devices with their start and end apart: 4 -> 4, of which waited for: 2 -> 2; matrix products, arithmetic and copies ran while one was open for 0% -> 0% of each run, Pallas kernels for 0% -> 3%
where the time goes in v6:
time: 35.9 us; the launch traced here: 35.7 us
  waiting for transfers between devices  24.8 us (69%)
  starting transfers between devices  5.17 us (14%)
  Pallas kernels  3.17 us (9%)
  local copies, waits for them, and re-layouts  1.7 us (5%)
  between operations  0.75 us (2%)
    ppermute x4, waiting for transfers between devices, along_line(): return lax.ppermute(rows, ('group', 'pair', 'z', 'x', 'y', 'tp'), pairs)  24.8 us
    ppermute x4, starting transfers between devices, along_line(): return lax.ppermute(rows, ('group', 'pair', 'z', 'x', 'y', 'tp'), pairs)  5.17 us
    unnamed x8, local copies, waits for them, and re-layouts  1.7 us
    pallas_call x1, Pallas kernels, shards(): pl.pallas_call(last_kernel, out_shape=jax.ShapeDtypeStruct((seq_count,) +...  1.58 us
    pallas_call x1, Pallas kernels, shards(): pl.pallas_call(resident_kernel, out_shape=first_shape, in_specs=[smem] +...  1.2 us
  transfers between devices with their start and end apart: 4, of which 2 were waited for; matrix products, arithmetic and copies ran while one was open for 0% of the time, Pallas kernels for 3%

profile of v6, /device:TPU:1, one launch (start us, length us, event | category | flops | bytes accessed | tf_op | source)
XLA Modules:
  0.0 35.7 jit_solution(7322597228864194761)
XLA Ops:
  0.0 0.0 copy-start.3
  0.0 0.6 %copy-done.3 = s32[256]{0:T(256)S(1)} copy-done((s32[256]{0:T(256)S(1)}, s32[256]{0:T(256)}, u32[]{:S(2)}) %copy-start.3) | copy-done | bytes 1048
  0.7 0.3 shard_map.64
  1.0 0.0 copy-start
  1.0 0.0 copy-start.2
  1.0 0.0 copy-start.1
  1.0 1.0 %copy-done = bf16[2,4,64,576]{3,2,1,0:T(8,128)(2,1)S(1)} copy-done((bf16[2,4,64,576]{3,2,1,0:T(8,128)(2,1)S(1)}, bf16[2,4,64,576]{3,2,1,0:T(8,128)(2,1)}, u32[]{:S(2)}) %copy-start) | copy-done | bytes 589848
  2.1 0.0 copy-done.2
  2.1 0.1 shard_map.65
  2.2 1.3 %collective-permute-start = (bf16[32,1152]{1,0:T(8,128)(2,1)S(1)}, bf16[32,1152]{1,0:T(8,128)(2,1)S(1)}, u32[]{:S(2)}, u32[]{:S(2)}) collective-permute-start(bf16[32,1152]{1,0:T(8,128)(2,1)S(1)} %get-tuple-element.18), channel_id=1, source_target_pairs={{0,320},{2,322},{4,324},{6,326},{8,328},{10,330},{12,332},{14,334}... | collective-permute-start | bytes 221192 | tf_op jit(solution)/shard_map/ppermute | solution.py:185
  3.5 1.3 %collective-permute-start.1 = (bf16[32,1152]{1,0:T(8,128)(2,1)S(1)}, bf16[32,1152]{1,0:T(8,128)(2,1)S(1)}, u32[]{:S(2)}, u32[]{:S(2)}) collective-permute-start(bf16[32,1152]{1,0:T(8,128)(2,1)S(1)} %get-tuple-element.19), channel_id=1, source_target_pairs={{0,384},{2,386},{4,388},{6,390},{8,392},{10,394},{12,396},{14,398}... | collective-permute-start | bytes 221192 | tf_op jit(solution)/shard_map/ppermute | solution.py:185
  4.8 1.3 %collective-permute-start.2 = (bf16[32,1152]{1,0:T(8,128)(2,1)S(1)}, bf16[32,1152]{1,0:T(8,128)(2,1)S(1)}, u32[]{:S(2)}, u32[]{:S(2)}) collective-permute-start(bf16[32,1152]{1,0:T(8,128)(2,1)S(1)} %get-tuple-element.20), channel_id=1, source_target_pairs={{0,449},{2,451},{4,453},{6,455},{8,457},{10,459},{12,461},{14,463}... | collective-permute-start | bytes 221192 | tf_op jit(solution)/shard_map/ppermute | solution.py:185
  6.1 1.3 %collective-permute-start.3 = (bf16[32,1152]{1,0:T(8,128)(2,1)S(1)}, bf16[32,1152]{1,0:T(8,128)(2,1)S(1)}, u32[]{:S(2)}, u32[]{:S(2)}) collective-permute-start(bf16[32,1152]{1,0:T(8,128)(2,1)S(1)} %get-tuple-element.21), channel_id=1, source_target_pairs={{0,256},{2,258},{4,260},{6,262},{8,264},{10,266},{12,268},{14,270}... | collective-permute-start | bytes 221192 | tf_op jit(solution)/shard_map/ppermute | solution.py:185
  8.1 0.0 copy-done.1
  8.1 1.2 %shard_map.66.first_ref = bf16[4,64,512]{2,1,0:T(8,128)(2,1)S(1)} custom-call(s32[1]{0:T(128)S(6)} %copy.9.length_ref, bf16[2,4,64,576]{3,2,1,0:T(8,128)(2,1)S(1)} %copy-done, bf16[2,4,576]{2,1,0:T(4,128)(2,1)S(1)} %copy-done.2, bf16[1,576,512]{2,1,0:T(8,128)(2,1)S(1)} %bitcast.4, bf16[16,576]{1,0:T(8,128)(2,1)S(1)} %get-tuple-element.16.after_ref.tail_ref), custom_call_target="tpu_custom_call" | custom-call | tf_op jit(solution)/shard_map/pallas_call | solution.py:223
  9.3 24.5 %collective-permute-done.refs_0_ = bf16[32,1152]{1,0:T(8,128)(2,1)S(1)} collective-permute-done((bf16[32,1152]{1,0:T(8,128)(2,1)S(1)}, bf16[32,1152]{1,0:T(8,128)(2,1)S(1)}, u32[]{:S(2)}, u32[]{:S(2)}) %collective-permute-start) | collective-permute-done | bytes 73760 | tf_op jit(solution)/shard_map/ppermute | solution.py:185
  33.8 0.3 collective-permute-done.1.refs_1_
  34.1 0.0 collective-permute-done.2.refs_2_
  34.1 0.0 collective-permute-done.3.refs_3_
  34.1 1.6 %shard_map.67 = bf16[2,4,64,512]{3,2,1,0:T(8,128)(2,1)} custom-call(bf16[2,4,64,576]{3,2,1,0:T(8,128)(2,1)S(1)} %copy-done, bf16[2,4,576]{2,1,0:T(4,128)(2,1)S(1)} %copy-done.2, bf16[4,64,512]{2,1,0:T(8,128)(2,1)S(1)} %shard_map.66.first_ref, bf16[576,256]{1,0:T(8,128)(2,1)S(1)} %get-tuple-element.17.query_t_ref, ...), custom_call_target="tpu_custom_call" | custom-call | tf_op jit(solution)/shard_map/pallas_call | solution.py:230
  (3 shorter events, 0.1 us)
Async XLA Ops:
  0.0 0.7 %copy-start.3 = (s32[256]{0:T(256)S(1)}, s32[256]{0:T(256)}, u32[]{:S(2)}) copy-start(s32[256]{0:T(256)} %param.13) | copy-start | bytes 3076
  1.0 1.1 %copy-start = (bf16[2,4,64,576]{3,2,1,0:T(8,128)(2,1)S(1)}, bf16[2,4,64,576]{3,2,1,0:T(8,128)(2,1)}, u32[]{:S(2)}) copy-start(bf16[2,4,64,576]{3,2,1,0:T(8,128)(2,1)} %query_ref.5) | copy-start | bytes 1769476
  1.0 1.1 %copy-start.2 = (bf16[2,4,576]{2,1,0:T(4,128)(2,1)S(1)}, bf16[2,4,576]{2,1,0:T(4,128)(2,1)}, u32[]{:S(2)}) copy-start(bf16[2,4,576]{2,1,0:T(4,128)(2,1)} %step_ref.5) | copy-start | bytes 27652
  1.0 7.0 %copy-start.1 = (bf16[1,512,576]{1,2,0:T(8,128)(2,1)S(1)}, bf16[1,512,576]{1,2,0:T(8,128)(2,1)}, u32[]{:S(2)}) copy-start(bf16[1,512,576]{1,2,0:T(8,128)(2,1)} %param.10) | copy-start | bytes 1769476
  2.2 31.6 %collective-permute-start = (bf16[32,1152]{1,0:T(8,128)(2,1)S(1)}, bf16[32,1152]{1,0:T(8,128)(2,1)S(1)}, u32[]{:S(2)}, u32[]{:S(2)}) collective-permute-start(bf16[32,1152]{1,0:T(8,128)(2,1)S(1)} %get-tuple-element.18), channel_id=1, source_target_pairs={{0,320},{2,322},{4,324},{6,326},{8,328},{10,330},{12,332},{14,334}... | collective-permute-start | bytes 221192 | tf_op jit(solution)/shard_map/ppermute | solution.py:185
  3.5 30.6 %collective-permute-start.1 = (bf16[32,1152]{1,0:T(8,128)(2,1)S(1)}, bf16[32,1152]{1,0:T(8,128)(2,1)S(1)}, u32[]{:S(2)}, u32[]{:S(2)}) collective-permute-start(bf16[32,1152]{1,0:T(8,128)(2,1)S(1)} %get-tuple-element.19), channel_id=1, source_target_pairs={{0,384},{2,386},{4,388},{6,390},{8,392},{10,394},{12,396},{14,398}... | collective-permute-start | bytes 221192 | tf_op jit(solution)/shard_map/ppermute | solution.py:185
  4.8 29.3 %collective-permute-start.2 = (bf16[32,1152]{1,0:T(8,128)(2,1)S(1)}, bf16[32,1152]{1,0:T(8,128)(2,1)S(1)}, u32[]{:S(2)}, u32[]{:S(2)}) collective-permute-start(bf16[32,1152]{1,0:T(8,128)(2,1)S(1)} %get-tuple-element.20), channel_id=1, source_target_pairs={{0,449},{2,451},{4,453},{6,455},{8,457},{10,459},{12,461},{14,463}... | collective-permute-start | bytes 221192 | tf_op jit(solution)/shard_map/ppermute | solution.py:185
  6.1 28.0 %collective-permute-start.3 = (bf16[32,1152]{1,0:T(8,128)(2,1)S(1)}, bf16[32,1152]{1,0:T(8,128)(2,1)S(1)}, u32[]{:S(2)}, u32[]{:S(2)}) collective-permute-start(bf16[32,1152]{1,0:T(8,128)(2,1)S(1)} %get-tuple-element.21), channel_id=1, source_target_pairs={{0,256},{2,258},{4,260},{6,262},{8,264},{10,266},{12,268},{14,270}... | collective-permute-start | bytes 221192 | tf_op jit(solution)/shard_map/ppermute | solution.py:185

commit v7 on v6

--- a/solution.py
+++ b/solution.py
@@ -9,7 +9,7 @@
 PEERS = 32
 lap = 64
 LINE = 4
-AHEAD = (1, 2, 3, 0)
+AHEAD = ((1, 2), (2, 1), (3, 3), (0, 0))
 
 score_scale = 192.0 ** (-0.5)
 masked_score = -1e30
@@ -117,8 +117,9 @@
         cols = lax.broadcasted_iota(jnp.int32, (count, count), 1)
         peer, part = rows % PEERS, rows // PEERS
         ahead = jnp.zeros_like(part)
-        for index, part_ahead in enumerate(AHEAD):
-            ahead = jnp.where(part == index, part_ahead, ahead)
+        upper = lax.axis_index("z") == 1
+        for index, (low_ahead, high_ahead) in enumerate(AHEAD):
+            ahead = jnp.where(part == index, jnp.where(upper, high_ahead, low_ahead), ahead)
         moved = moved_ref[...].reshape(count, moved_ref.shape[2])
         turned = picked(cols == peer * LINE + ahead, moved, ((1,), (0,)))
         for part, part_ref in enumerate(part_refs):
@@ -173,12 +174,12 @@
     return ahead if ahead < LINE // 2 else ahead - LINE
 
 
-def along_line(rows, ahead):
+def along_line(rows, index):
     line_total, ring = PEERS * LINE * 2, LINE * 2
     pairs = []
     for place in range(ring):
-        there = (place + step_of(place, ahead)) % ring
         for peer in range(PEERS):
+            there = (place + step_of(place, AHEAD[index][peer // (PEERS // 2)])) % ring
             source = ((place % LINE) * PEERS + peer) * 2 + place // LINE
             target = ((there % LINE) * PEERS + peer) * 2 + there // LINE
             pairs.append((source, line_total + target))
@@ -219,7 +220,7 @@
         out_specs=[vmem] * (2 + LINE),
         compiler_params=params,
     )(queries, step_rows, moved)
-    arrived = [along_line(part, ahead) for part, ahead in zip(parts, AHEAD)]
+    arrived = [along_line(part, index) for index, part in enumerate(parts)]
     first = pl.pallas_call(
         resident_kernel,
         out_shape=first_shape,

time: 35.9 us -> 34.9 us (0.972)
  waiting for transfers between devices: 24.8 us -> 23.8 us
    ppermute x4, waiting for transfers between devices: 24.8 us -> 23.8 us  [along_line(): return lax.ppermute(rows, ('group', 'pair', 'z', 'x', 'y', 'tp'), pairs)]
  transfers between devices with their start and end apart: 4 -> 4, of which waited for: 2 -> 1; matrix products, arithmetic and copies ran while one was open for 0% -> 0% of each run, Pallas kernels for 3% -> 3%
where the time goes in v7:
time: 34.9 us; the launch traced here: 34.7 us
  waiting for transfers between devices  23.8 us (68%)
  starting transfers between devices  5.17 us (15%)
  Pallas kernels  3.19 us (9%)
  local copies, waits for them, and re-layouts  1.7 us (5%)
  between operations  0.75 us (2%)
    ppermute x4, waiting for transfers between devices, along_line(): return lax.ppermute(rows, ('group', 'pair', 'z', 'x', 'y', 'tp'), pairs)  23.8 us
    ppermute x4, starting transfers between devices, along_line(): return lax.ppermute(rows, ('group', 'pair', 'z', 'x', 'y', 'tp'), pairs)  5.17 us
    unnamed x8, local copies, waits for them, and re-layouts  1.7 us
    pallas_call x1, Pallas kernels, shards(): pl.pallas_call(last_kernel, out_shape=jax.ShapeDtypeStruct((seq_count,) +...  1.59 us
    pallas_call x1, Pallas kernels, shards(): pl.pallas_call(resident_kernel, out_shape=first_shape, in_specs=[smem] +...  1.2 us
  transfers between devices with their start and end apart: 4, of which 1 were waited for; matrix products, arithmetic and copies ran while one was open for 0% of the time, Pallas kernels for 3%

profile of v7, /device:TPU:1, one launch (start us, length us, event | category | flops | bytes accessed | tf_op | source)
XLA Modules:
  0.0 34.7 jit_solution(8846917755284865634)
XLA Ops:
  0.0 0.0 copy-start.3
  0.0 0.6 %copy-done.3 = s32[256]{0:T(256)S(1)} copy-done((s32[256]{0:T(256)S(1)}, s32[256]{0:T(256)}, u32[]{:S(2)}) %copy-start.3) | copy-done | bytes 1048
  0.7 0.3 shard_map.64
  1.0 0.0 copy-start
  1.0 0.0 copy-start.2
  1.0 0.0 copy-start.1
  1.0 1.0 %copy-done = bf16[2,4,64,576]{3,2,1,0:T(8,128)(2,1)S(1)} copy-done((bf16[2,4,64,576]{3,2,1,0:T(8,128)(2,1)S(1)}, bf16[2,4,64,576]{3,2,1,0:T(8,128)(2,1)}, u32[]{:S(2)}) %copy-start) | copy-done | bytes 589848
  2.1 0.0 copy-done.2
  2.1 0.1 shard_map.65
  2.2 1.3 %collective-permute-start = (bf16[32,1152]{1,0:T(8,128)(2,1)S(1)}, bf16[32,1152]{1,0:T(8,128)(2,1)S(1)}, u32[]{:S(2)}, u32[]{:S(2)}) collective-permute-start(bf16[32,1152]{1,0:T(8,128)(2,1)S(1)} %get-tuple-element.18), channel_id=1, source_target_pairs={{0,320},{2,322},{4,324},{6,326},{8,328},{10,330},{12,332},{14,334}... | collective-permute-start | bytes 221192 | tf_op jit(solution)/shard_map/ppermute | solution.py:186
  3.5 1.3 %collective-permute-start.1 = (bf16[32,1152]{1,0:T(8,128)(2,1)S(1)}, bf16[32,1152]{1,0:T(8,128)(2,1)S(1)}, u32[]{:S(2)}, u32[]{:S(2)}) collective-permute-start(bf16[32,1152]{1,0:T(8,128)(2,1)S(1)} %get-tuple-element.19), channel_id=1, source_target_pairs={{0,384},{2,386},{4,388},{6,390},{8,392},{10,394},{12,396},{14,398}... | collective-permute-start | bytes 221192 | tf_op jit(solution)/shard_map/ppermute | solution.py:186
  4.8 1.3 %collective-permute-start.2 = (bf16[32,1152]{1,0:T(8,128)(2,1)S(1)}, bf16[32,1152]{1,0:T(8,128)(2,1)S(1)}, u32[]{:S(2)}, u32[]{:S(2)}) collective-permute-start(bf16[32,1152]{1,0:T(8,128)(2,1)S(1)} %get-tuple-element.20), channel_id=1, source_target_pairs={{0,449},{2,451},{4,453},{6,455},{8,457},{10,459},{12,461},{14,463}... | collective-permute-start | bytes 221192 | tf_op jit(solution)/shard_map/ppermute | solution.py:186
  6.1 1.3 %collective-permute-start.3 = (bf16[32,1152]{1,0:T(8,128)(2,1)S(1)}, bf16[32,1152]{1,0:T(8,128)(2,1)S(1)}, u32[]{:S(2)}, u32[]{:S(2)}) collective-permute-start(bf16[32,1152]{1,0:T(8,128)(2,1)S(1)} %get-tuple-element.21), channel_id=1, source_target_pairs={{0,256},{2,258},{4,260},{6,262},{8,264},{10,266},{12,268},{14,270}... | collective-permute-start | bytes 221192 | tf_op jit(solution)/shard_map/ppermute | solution.py:186
  8.1 0.0 copy-done.1
  8.1 1.2 %shard_map.66.first_ref = bf16[4,64,512]{2,1,0:T(8,128)(2,1)S(1)} custom-call(s32[1]{0:T(128)S(6)} %copy.9.length_ref, bf16[2,4,64,576]{3,2,1,0:T(8,128)(2,1)S(1)} %copy-done, bf16[2,4,576]{2,1,0:T(4,128)(2,1)S(1)} %copy-done.2, bf16[1,576,512]{2,1,0:T(8,128)(2,1)S(1)} %bitcast.4, bf16[16,576]{1,0:T(8,128)(2,1)S(1)} %get-tuple-element.16.after_ref.tail_ref), custom_call_target="tpu_custom_call" | custom-call | tf_op jit(solution)/shard_map/pallas_call | solution.py:224
  9.3 23.8 %collective-permute-done.refs_0_ = bf16[32,1152]{1,0:T(8,128)(2,1)S(1)} collective-permute-done((bf16[32,1152]{1,0:T(8,128)(2,1)S(1)}, bf16[32,1152]{1,0:T(8,128)(2,1)S(1)}, u32[]{:S(2)}, u32[]{:S(2)}) %collective-permute-start) | collective-permute-done | bytes 73760 | tf_op jit(solution)/shard_map/ppermute | solution.py:186
  33.1 0.0 collective-permute-done.1.refs_1_
  33.1 0.0 collective-permute-done.2.refs_2_
  33.1 0.0 collective-permute-done.3.refs_3_
  33.1 1.6 %shard_map.67 = bf16[2,4,64,512]{3,2,1,0:T(8,128)(2,1)} custom-call(bf16[2,4,64,576]{3,2,1,0:T(8,128)(2,1)S(1)} %copy-done, bf16[2,4,576]{2,1,0:T(4,128)(2,1)S(1)} %copy-done.2, bf16[4,64,512]{2,1,0:T(8,128)(2,1)S(1)} %shard_map.66.first_ref, bf16[576,256]{1,0:T(8,128)(2,1)S(1)} %get-tuple-element.17.query_t_ref, ...), custom_call_target="tpu_custom_call" | custom-call | tf_op jit(solution)/shard_map/pallas_call | solution.py:231
  (3 shorter events, 0.1 us)
Async XLA Ops:
  0.0 0.7 %copy-start.3 = (s32[256]{0:T(256)S(1)}, s32[256]{0:T(256)}, u32[]{:S(2)}) copy-start(s32[256]{0:T(256)} %param.13) | copy-start | bytes 3076
  1.0 1.1 %copy-start = (bf16[2,4,64,576]{3,2,1,0:T(8,128)(2,1)S(1)}, bf16[2,4,64,576]{3,2,1,0:T(8,128)(2,1)}, u32[]{:S(2)}) copy-start(bf16[2,4,64,576]{3,2,1,0:T(8,128)(2,1)} %query_ref.5) | copy-start | bytes 1769476
  1.0 1.1 %copy-start.2 = (bf16[2,4,576]{2,1,0:T(4,128)(2,1)S(1)}, bf16[2,4,576]{2,1,0:T(4,128)(2,1)}, u32[]{:S(2)}) copy-start(bf16[2,4,576]{2,1,0:T(4,128)(2,1)} %step_ref.5) | copy-start | bytes 27652
  1.0 7.0 %copy-start.1 = (bf16[1,512,576]{1,2,0:T(8,128)(2,1)S(1)}, bf16[1,512,576]{1,2,0:T(8,128)(2,1)}, u32[]{:S(2)}) copy-start(bf16[1,512,576]{1,2,0:T(8,128)(2,1)} %param.10) | copy-start | bytes 1769476
  2.2 30.9 %collective-permute-start = (bf16[32,1152]{1,0:T(8,128)(2,1)S(1)}, bf16[32,1152]{1,0:T(8,128)(2,1)S(1)}, u32[]{:S(2)}, u32[]{:S(2)}) collective-permute-start(bf16[32,1152]{1,0:T(8,128)(2,1)S(1)} %get-tuple-element.18), channel_id=1, source_target_pairs={{0,320},{2,322},{4,324},{6,326},{8,328},{10,330},{12,332},{14,334}... | collective-permute-start | bytes 221192 | tf_op jit(solution)/shard_map/ppermute | solution.py:186
  3.5 29.6 %collective-permute-start.1 = (bf16[32,1152]{1,0:T(8,128)(2,1)S(1)}, bf16[32,1152]{1,0:T(8,128)(2,1)S(1)}, u32[]{:S(2)}, u32[]{:S(2)}) collective-permute-start(bf16[32,1152]{1,0:T(8,128)(2,1)S(1)} %get-tuple-element.19), channel_id=1, source_target_pairs={{0,384},{2,386},{4,388},{6,390},{8,392},{10,394},{12,396},{14,398}... | collective-permute-start | bytes 221192 | tf_op jit(solution)/shard_map/ppermute | solution.py:186
  4.8 28.3 %collective-permute-start.2 = (bf16[32,1152]{1,0:T(8,128)(2,1)S(1)}, bf16[32,1152]{1,0:T(8,128)(2,1)S(1)}, u32[]{:S(2)}, u32[]{:S(2)}) collective-permute-start(bf16[32,1152]{1,0:T(8,128)(2,1)S(1)} %get-tuple-element.20), channel_id=1, source_target_pairs={{0,449},{2,451},{4,453},{6,455},{8,457},{10,459},{12,461},{14,463}... | collective-permute-start | bytes 221192 | tf_op jit(solution)/shard_map/ppermute | solution.py:186
  6.1 27.0 %collective-permute-start.3 = (bf16[32,1152]{1,0:T(8,128)(2,1)S(1)}, bf16[32,1152]{1,0:T(8,128)(2,1)S(1)}, u32[]{:S(2)}, u32[]{:S(2)}) collective-permute-start(bf16[32,1152]{1,0:T(8,128)(2,1)S(1)} %get-tuple-element.21), channel_id=1, source_target_pairs={{0,256},{2,258},{4,260},{6,262},{8,264},{10,266},{12,268},{14,270}... | collective-permute-start | bytes 221192 | tf_op jit(solution)/shard_map/ppermute | solution.py:186

commit v8 on v7

--- a/solution.py
+++ b/solution.py
@@ -97,8 +97,11 @@
         yield mixed.astype(jnp.bfloat16).reshape(-1, head_count, KV_RANK)
 
 
-def resident_kernel(length_ref, query_ref, step_ref, cache_ref, after_ref, first_ref):
-    first_ref[...] = resident(length_ref[0], flat_rows(query_ref, 0), step_ref[0], cache_ref[0])
+def resident_kernel(length_ref, query_ref, step_ref, cache_ref, after_ref, out_ref, result, sem):
+    result[...] = resident(length_ref[0], flat_rows(query_ref, 0), step_ref[0], cache_ref[0])
+    copy = pltpu.make_async_copy(result, out_ref.at[0], sem)
+    copy.start()
+    copy.wait()
 
 
 def middle_kernel(query_ref, step_ref, moved_ref, query_t_ref, tail_ref, *part_refs):
@@ -126,11 +129,9 @@
             part_ref[...] = turned[part * PEERS : (part + 1) * PEERS]
 
 
-def last_kernel(query_ref, step_ref, first_ref, query_t_ref, tail_ref, *refs):
-    part_refs, (out_ref, result, sems) = refs[:LINE], refs[LINE:]
+def last_kernel(query_ref, step_ref, query_t_ref, tail_ref, *refs):
+    part_refs, (out_ref, result, sems) = refs[:LINE], refs[LINE + 1 :]
     decode = lax.axis_index("group") == 1
-    before = pltpu.make_async_copy(first_ref, out_ref.at[0], sems.at[0])
-    before.start()
 
     @pl.when(decode)
     def _():
@@ -145,7 +146,7 @@
             steps = pl.ds(part * attended.shape[0], attended.shape[0])
             result[steps] = attended
             copies.append(
-                pltpu.make_async_copy(result.at[steps], out_ref.at[1, steps], sems.at[1 + part])
+                pltpu.make_async_copy(result.at[steps], out_ref.at[1, steps], sems.at[part])
             )
             copies[-1].start()
         for copy in copies:
@@ -154,11 +155,9 @@
     @pl.when(jnp.logical_not(decode))
     def _():
         result[...] = steps_only(flat_rows(query_ref, 1), step_ref[1])
-        after = pltpu.make_async_copy(result, out_ref.at[1], sems.at[1])
-        after.start()
-        after.wait()
-
-    before.wait()
+        copy = pltpu.make_async_copy(result, out_ref.at[1], sems.at[0])
+        copy.start()
+        copy.wait()
 
 
 vmem = pl.BlockSpec(memory_space=pltpu.VMEM)
@@ -189,7 +188,7 @@
 def shards(queries, step_rows, cache, lengths, outgoing, crossing):
     seq_count, steps_total, head_count, latent_width = queries.shape
     row_total = outgoing.shape[0]
-    first_shape = jax.ShapeDtypeStruct((steps_total, head_count, KV_RANK), jnp.bfloat16)
+    first_shape = (steps_total, head_count, KV_RANK)
     keys = cache.transpose(0, 2, 1)
 
     query_rows = steps_total * head_count
@@ -206,7 +205,7 @@
     moved = lax.cond(
         lax.axis_index("group") == 0,
         lambda rows: lax.all_to_all(rows, ("z", "x", "y"), 0, 0, tiled=True),
-        lambda rows: rows,
+        jnp.zeros_like,
         packed,
     )
     query_t, tail, *parts = pl.pallas_call(
@@ -221,24 +220,24 @@
         compiler_params=params,
     )(queries, step_rows, moved)
     arrived = [along_line(part, index) for index, part in enumerate(parts)]
-    first = pl.pallas_call(
+    out_shape = jax.ShapeDtypeStruct((seq_count,) + first_shape, jnp.bfloat16)
+    half_done = pl.pallas_call(
         resident_kernel,
-        out_shape=first_shape,
+        out_shape=out_shape,
         in_specs=[smem] + [vmem] * 3 + [anywhere],
-        out_specs=vmem,
+        out_specs=anywhere,
+        scratch_shapes=[pltpu.VMEM(first_shape, jnp.bfloat16), pltpu.SemaphoreType.DMA],
         compiler_params=params,
     )(lengths, queries, step_rows, keys, tail)
     return pl.pallas_call(
         last_kernel,
-        out_shape=jax.ShapeDtypeStruct((seq_count,) + first_shape.shape, jnp.bfloat16),
-        in_specs=[vmem] * (5 + LINE),
+        out_shape=out_shape,
+        in_specs=[vmem] * (4 + LINE) + [anywhere],
         out_specs=anywhere,
-        scratch_shapes=[
-            pltpu.VMEM(first_shape.shape, jnp.bfloat16),
-            pltpu.SemaphoreType.DMA((3,)),
-        ],
-        compiler_params=params,
-    )(queries, step_rows, first, query_t, tail, *arrived)
+        scratch_shapes=[pltpu.VMEM(first_shape, jnp.bfloat16), pltpu.SemaphoreType.DMA((2,))],
+        input_output_aliases={4 + LINE: 0},
+        compiler_params=params,
+    )(queries, step_rows, query_t, tail, *arrived, half_done)
 
 
 def solution(mesh):

time: 34.9 us -> 34.7 us (level)
  Pallas kernels: 3.19 us -> 3.9 us
  waiting for transfers between devices: 23.8 us -> 23.1 us
    pallas_call x2, Pallas kernels: 2.79 us -> 3.49 us  [the longest x1 1.91 us: shards(): pl.pallas_call(resident_kernel, out_shape=out_shape, in_specs=[smem] + [v...]
    ppermute x4, waiting for transfers between devices: 23.8 us -> 23.1 us  [along_line(): return lax.ppermute(rows, ('group', 'pair', 'z', 'x', 'y', 'tp'), pairs)]
    unnamed x8, local copies, waits for them, and re-layouts: 1.7 us -> 1.34 us
  transfers between devices with their start and end apart: 4 -> 4, of which waited for: 1 -> 1; matrix products, arithmetic and copies ran while one was open for 0% -> 0% of each run, Pallas kernels for 3% -> 6%
where the time goes in v8:
time: 34.7 us; the launch traced here: 34.4 us
  waiting for transfers between devices  23.1 us (67%)
  starting transfers between devices  5.17 us (15%)
  Pallas kernels  3.9 us (11%)
  local copies, waits for them, and re-layouts  1.41 us (4%)
  between operations  0.75 us (2%)
    ppermute x4, waiting for transfers between devices, along_line(): return lax.ppermute(rows, ('group', 'pair', 'z', 'x', 'y', 'tp'), pairs)  23.1 us
    ppermute x4, starting transfers between devices, along_line(): return lax.ppermute(rows, ('group', 'pair', 'z', 'x', 'y', 'tp'), pairs)  5.17 us
    pallas_call x1, Pallas kernels, shards(): pl.pallas_call(resident_kernel, out_shape=out_shape, in_specs=[smem] + [v...  1.91 us
    pallas_call x1, Pallas kernels, shards(): pl.pallas_call(last_kernel, out_shape=out_shape, in_specs=[vmem] * (4 + L...  1.58 us
    unnamed x8, local copies, waits for them, and re-layouts  1.34 us
  transfers between devices with their start and end apart: 4, of which 1 were waited for; matrix products, arithmetic and copies ran while one was open for 0% of the time, Pallas kernels for 6%

profile of v8, /device:TPU:1, one launch (start us, length us, event | category | flops | bytes accessed | tf_op | source)
XLA Modules:
  0.0 34.4 jit_solution(4379423396586542969)
XLA Ops:
  0.0 0.0 copy-start.3
  0.0 0.6 %copy-done.3 = s32[256]{0:T(256)S(1)} copy-done((s32[256]{0:T(256)S(1)}, s32[256]{0:T(256)}, u32[]{:S(2)}) %copy-start.3) | copy-done | bytes 1048
  0.7 0.0 copy-start
  0.7 0.3 shard_map.64
  1.0 0.0 copy-start.2
  1.0 0.1 conditional.1
  1.0 0.1 broadcast.21
  1.1 0.0 copy-start.1
  1.1 0.7 %copy-done = bf16[2,4,64,576]{3,2,1,0:T(8,128)(2,1)S(1)} copy-done((bf16[2,4,64,576]{3,2,1,0:T(8,128)(2,1)S(1)}, bf16[2,4,64,576]{3,2,1,0:T(8,128)(2,1)}, u32[]{:S(2)}) %copy-start) | copy-done | bytes 589848
  1.8 0.0 copy-done.2
  1.8 0.1 shard_map.65
  1.9 1.3 %collective-permute-start = (bf16[32,1152]{1,0:T(8,128)(2,1)S(1)}, bf16[32,1152]{1,0:T(8,128)(2,1)S(1)}, u32[]{:S(2)}, u32[]{:S(2)}) collective-permute-start(bf16[32,1152]{1,0:T(8,128)(2,1)S(1)} %get-tuple-element.17), channel_id=1, source_target_pairs={{0,320},{2,322},{4,324},{6,326},{8,328},{10,330},{12,332},{14,334}... | collective-permute-start | bytes 221192 | tf_op jit(solution)/shard_map/ppermute | solution.py:185
  3.2 1.3 %collective-permute-start.1 = (bf16[32,1152]{1,0:T(8,128)(2,1)S(1)}, bf16[32,1152]{1,0:T(8,128)(2,1)S(1)}, u32[]{:S(2)}, u32[]{:S(2)}) collective-permute-start(bf16[32,1152]{1,0:T(8,128)(2,1)S(1)} %get-tuple-element.18), channel_id=1, source_target_pairs={{0,384},{2,386},{4,388},{6,390},{8,392},{10,394},{12,396},{14,398}... | collective-permute-start | bytes 221192 | tf_op jit(solution)/shard_map/ppermute | solution.py:185
  4.5 1.3 %collective-permute-start.2 = (bf16[32,1152]{1,0:T(8,128)(2,1)S(1)}, bf16[32,1152]{1,0:T(8,128)(2,1)S(1)}, u32[]{:S(2)}, u32[]{:S(2)}) collective-permute-start(bf16[32,1152]{1,0:T(8,128)(2,1)S(1)} %get-tuple-element.19), channel_id=1, source_target_pairs={{0,449},{2,451},{4,453},{6,455},{8,457},{10,459},{12,461},{14,463}... | collective-permute-start | bytes 221192 | tf_op jit(solution)/shard_map/ppermute | solution.py:185
  5.8 1.3 %collective-permute-start.3 = (bf16[32,1152]{1,0:T(8,128)(2,1)S(1)}, bf16[32,1152]{1,0:T(8,128)(2,1)S(1)}, u32[]{:S(2)}, u32[]{:S(2)}) collective-permute-start(bf16[32,1152]{1,0:T(8,128)(2,1)S(1)} %get-tuple-element.20), channel_id=1, source_target_pairs={{0,256},{2,258},{4,260},{6,262},{8,264},{10,266},{12,268},{14,270}... | collective-permute-start | bytes 221192 | tf_op jit(solution)/shard_map/ppermute | solution.py:185
  7.8 0.0 copy-done.1
  7.8 1.9 %shard_map.66.refs_4_ = bf16[2,4,64,512]{3,2,1,0:T(8,128)(2,1)} custom-call(s32[1]{0:T(128)S(6)} %copy.11.length_ref, bf16[2,4,64,576]{3,2,1,0:T(8,128)(2,1)S(1)} %copy-done, bf16[2,4,576]{2,1,0:T(4,128)(2,1)S(1)} %copy-done.2, bf16[1,576,512]{2,1,0:T(8,128)(2,1)S(1)} %bitcast.4, bf16[16,576]{1,0:T(8,128)(2,1)S(1)} %get-tuple-element.16.after_ref.tail_ref), custom_call_target="tpu_custom_call" | custom-call | tf_op jit(solution)/shard_map/pallas_call | solution.py:224
  9.7 23.1 %collective-permute-done.refs_0_ = bf16[32,1152]{1,0:T(8,128)(2,1)S(1)} collective-permute-done((bf16[32,1152]{1,0:T(8,128)(2,1)S(1)}, bf16[32,1152]{1,0:T(8,128)(2,1)S(1)}, u32[]{:S(2)}, u32[]{:S(2)}) %collective-permute-start) | collective-permute-done | bytes 73760 | tf_op jit(solution)/shard_map/ppermute | solution.py:185
  32.8 0.0 collective-permute-done.1.refs_1_
  32.8 0.0 collective-permute-done.2.refs_2_
  32.8 0.0 collective-permute-done.3.refs_3_
  32.8 1.6 %shard_map.67 = bf16[2,4,64,512]{3,2,1,0:T(8,128)(2,1)} custom-call(bf16[2,4,64,576]{3,2,1,0:T(8,128)(2,1)S(1)} %copy-done, bf16[2,4,576]{2,1,0:T(4,128)(2,1)S(1)} %copy-done.2, bf16[576,256]{1,0:T(8,128)(2,1)S(1)} %get-tuple-element.15.query_t_ref, bf16[16,576]{1,0:T(8,128)(2,1)S(1)} %get-tuple-element.16.after_ref.tail_ref, ...), custom_call_target="tpu_custom_call", output_to_operand_aliasing={{}: (8, {})} | custom-call | tf_op jit(solution)/shard_map/pallas_call | solution.py:232
  (2 shorter events, 0.0 us)
Async XLA Ops:
  0.0 0.7 %copy-start.3 = (s32[256]{0:T(256)S(1)}, s32[256]{0:T(256)}, u32[]{:S(2)}) copy-start(s32[256]{0:T(256)} %param.13) | copy-start | bytes 3076
  0.7 1.1 %copy-start = (bf16[2,4,64,576]{3,2,1,0:T(8,128)(2,1)S(1)}, bf16[2,4,64,576]{3,2,1,0:T(8,128)(2,1)}, u32[]{:S(2)}) copy-start(bf16[2,4,64,576]{3,2,1,0:T(8,128)(2,1)} %query_ref.5) | copy-start | bytes 1769476
  1.0 0.8 %copy-start.2 = (bf16[2,4,576]{2,1,0:T(4,128)(2,1)S(1)}, bf16[2,4,576]{2,1,0:T(4,128)(2,1)}, u32[]{:S(2)}) copy-start(bf16[2,4,576]{2,1,0:T(4,128)(2,1)} %step_ref.5) | copy-start | bytes 27652
  1.1 6.7 %copy-start.1 = (bf16[1,512,576]{1,2,0:T(8,128)(2,1)S(1)}, bf16[1,512,576]{1,2,0:T(8,128)(2,1)}, u32[]{:S(2)}) copy-start(bf16[1,512,576]{1,2,0:T(8,128)(2,1)} %param.10) | copy-start | bytes 1769476
  1.9 30.9 %collective-permute-start = (bf16[32,1152]{1,0:T(8,128)(2,1)S(1)}, bf16[32,1152]{1,0:T(8,128)(2,1)S(1)}, u32[]{:S(2)}, u32[]{:S(2)}) collective-permute-start(bf16[32,1152]{1,0:T(8,128)(2,1)S(1)} %get-tuple-element.17), channel_id=1, source_target_pairs={{0,320},{2,322},{4,324},{6,326},{8,328},{10,330},{12,332},{14,334}... | collective-permute-start | bytes 221192 | tf_op jit(solution)/shard_map/ppermute | solution.py:185
  3.2 29.6 %collective-permute-start.1 = (bf16[32,1152]{1,0:T(8,128)(2,1)S(1)}, bf16[32,1152]{1,0:T(8,128)(2,1)S(1)}, u32[]{:S(2)}, u32[]{:S(2)}) collective-permute-start(bf16[32,1152]{1,0:T(8,128)(2,1)S(1)} %get-tuple-element.18), channel_id=1, source_target_pairs={{0,384},{2,386},{4,388},{6,390},{8,392},{10,394},{12,396},{14,398}... | collective-permute-start | bytes 221192 | tf_op jit(solution)/shard_map/ppermute | solution.py:185
  4.5 28.3 %collective-permute-start.2 = (bf16[32,1152]{1,0:T(8,128)(2,1)S(1)}, bf16[32,1152]{1,0:T(8,128)(2,1)S(1)}, u32[]{:S(2)}, u32[]{:S(2)}) collective-permute-start(bf16[32,1152]{1,0:T(8,128)(2,1)S(1)} %get-tuple-element.19), channel_id=1, source_target_pairs={{0,449},{2,451},{4,453},{6,455},{8,457},{10,459},{12,461},{14,463}... | collective-permute-start | bytes 221192 | tf_op jit(solution)/shard_map/ppermute | solution.py:185
  5.8 27.0 %collective-permute-start.3 = (bf16[32,1152]{1,0:T(8,128)(2,1)S(1)}, bf16[32,1152]{1,0:T(8,128)(2,1)S(1)}, u32[]{:S(2)}, u32[]{:S(2)}) collective-permute-start(bf16[32,1152]{1,0:T(8,128)(2,1)S(1)} %get-tuple-element.20), channel_id=1, source_target_pairs={{0,256},{2,258},{4,260},{6,262},{8,264},{10,266},{12,268},{14,270}... | collective-permute-start | bytes 221192 | tf_op jit(solution)/shard_map/ppermute | solution.py:185

commit v9 on v8

--- a/solution.py
+++ b/solution.py
@@ -193,7 +193,9 @@
 
     query_rows = steps_total * head_count
     ahead = (crossing // PEERS - lax.axis_index("pair") + LINE) % LINE
-    slots = (crossing % PEERS) * LINE + ahead
+    plane = PEERS // 2
+    peer = (crossing % plane) * 2 + (crossing // plane) % 2
+    slots = peer * LINE + ahead
     mine = jnp.where(lax.axis_index("group") == 0, outgoing.T, jnp.zeros((), outgoing.dtype))
     packed = pl.pallas_call(
         pack_kernel,
@@ -204,7 +206,7 @@
     )(slots.reshape(1, row_total), mine)
     moved = lax.cond(
         lax.axis_index("group") == 0,
-        lambda rows: lax.all_to_all(rows, ("z", "x", "y"), 0, 0, tiled=True),
+        lambda rows: lax.all_to_all(rows, ("x", "y", "z"), 0, 0, tiled=True),
         jnp.zeros_like,
         packed,
     )

time: 34.7 us -> 35.1 us (1.012)
  waiting for transfers between devices: 23.1 us -> 23.5 us
    ppermute x4, waiting for transfers between devices: 23.1 us -> 23.5 us  [along_line(): return lax.ppermute(rows, ('group', 'pair', 'z', 'x', 'y', 'tp'), pairs)]
where the time goes in v9:
time: 35.1 us; the launch traced here: 34.8 us
  waiting for transfers between devices  23.5 us (67%)
  starting transfers between devices  5.17 us (15%)
  Pallas kernels  3.9 us (11%)
  local copies, waits for them, and re-layouts  1.42 us (4%)
  between operations  0.75 us (2%)
    ppermute x4, waiting for transfers between devices, along_line(): return lax.ppermute(rows, ('group', 'pair', 'z', 'x', 'y', 'tp'), pairs)  23.5 us
    ppermute x4, starting transfers between devices, along_line(): return lax.ppermute(rows, ('group', 'pair', 'z', 'x', 'y', 'tp'), pairs)  5.17 us
    pallas_call x1, Pallas kernels, shards(): pl.pallas_call(resident_kernel, out_shape=out_shape, in_specs=[smem] + [v...  1.91 us
    pallas_call x1, Pallas kernels, shards(): pl.pallas_call(last_kernel, out_shape=out_shape, in_specs=[vmem] * (4 + L...  1.58 us
    unnamed x8, local copies, waits for them, and re-layouts  1.34 us
  transfers between devices with their start and end apart: 4, of which 1 were waited for; matrix products, arithmetic and copies ran while one was open for 0% of the time, Pallas kernels for 6%

profile of v9, /device:TPU:1, one launch (start us, length us, event | category | flops | bytes accessed | tf_op | source)
XLA Modules:
  0.0 34.8 jit_solution(8491149193703199429)
XLA Ops:
  0.0 0.0 copy-start.3
  0.0 0.6 %copy-done.3 = s32[256]{0:T(256)S(1)} copy-done((s32[256]{0:T(256)S(1)}, s32[256]{0:T(256)}, u32[]{:S(2)}) %copy-start.3) | copy-done | bytes 1048
  0.7 0.0 copy-start
  0.7 0.3 shard_map.64
  1.0 0.0 copy-start.2
  1.0 0.1 conditional.1
  1.0 0.1 broadcast.28
  1.1 0.0 copy-start.1
  1.1 0.7 %copy-done = bf16[2,4,64,576]{3,2,1,0:T(8,128)(2,1)S(1)} copy-done((bf16[2,4,64,576]{3,2,1,0:T(8,128)(2,1)S(1)}, bf16[2,4,64,576]{3,2,1,0:T(8,128)(2,1)}, u32[]{:S(2)}) %copy-start) | copy-done | bytes 589848
  1.8 0.0 copy-done.2
  1.8 0.1 shard_map.65
  1.9 1.3 %collective-permute-start = (bf16[32,1152]{1,0:T(8,128)(2,1)S(1)}, bf16[32,1152]{1,0:T(8,128)(2,1)S(1)}, u32[]{:S(2)}, u32[]{:S(2)}) collective-permute-start(bf16[32,1152]{1,0:T(8,128)(2,1)S(1)} %get-tuple-element.17), channel_id=1, source_target_pairs={{0,320},{2,322},{4,324},{6,326},{8,328},{10,330},{12,332},{14,334}... | collective-permute-start | bytes 221192 | tf_op jit(solution)/shard_map/ppermute | solution.py:185
  3.2 1.3 %collective-permute-start.1 = (bf16[32,1152]{1,0:T(8,128)(2,1)S(1)}, bf16[32,1152]{1,0:T(8,128)(2,1)S(1)}, u32[]{:S(2)}, u32[]{:S(2)}) collective-permute-start(bf16[32,1152]{1,0:T(8,128)(2,1)S(1)} %get-tuple-element.18), channel_id=1, source_target_pairs={{0,384},{2,386},{4,388},{6,390},{8,392},{10,394},{12,396},{14,398}... | collective-permute-start | bytes 221192 | tf_op jit(solution)/shard_map/ppermute | solution.py:185
  4.5 1.3 %collective-permute-start.2 = (bf16[32,1152]{1,0:T(8,128)(2,1)S(1)}, bf16[32,1152]{1,0:T(8,128)(2,1)S(1)}, u32[]{:S(2)}, u32[]{:S(2)}) collective-permute-start(bf16[32,1152]{1,0:T(8,128)(2,1)S(1)} %get-tuple-element.19), channel_id=1, source_target_pairs={{0,449},{2,451},{4,453},{6,455},{8,457},{10,459},{12,461},{14,463}... | collective-permute-start | bytes 221192 | tf_op jit(solution)/shard_map/ppermute | solution.py:185
  5.8 1.3 %collective-permute-start.3 = (bf16[32,1152]{1,0:T(8,128)(2,1)S(1)}, bf16[32,1152]{1,0:T(8,128)(2,1)S(1)}, u32[]{:S(2)}, u32[]{:S(2)}) collective-permute-start(bf16[32,1152]{1,0:T(8,128)(2,1)S(1)} %get-tuple-element.20), channel_id=1, source_target_pairs={{0,256},{2,258},{4,260},{6,262},{8,264},{10,266},{12,268},{14,270}... | collective-permute-start | bytes 221192 | tf_op jit(solution)/shard_map/ppermute | solution.py:185
  7.8 0.0 copy-done.1
  7.8 1.9 %shard_map.66.refs_4_ = bf16[2,4,64,512]{3,2,1,0:T(8,128)(2,1)} custom-call(s32[1]{0:T(128)S(6)} %copy.11.length_ref, bf16[2,4,64,576]{3,2,1,0:T(8,128)(2,1)S(1)} %copy-done, bf16[2,4,576]{2,1,0:T(4,128)(2,1)S(1)} %copy-done.2, bf16[1,576,512]{2,1,0:T(8,128)(2,1)S(1)} %bitcast.4, bf16[16,576]{1,0:T(8,128)(2,1)S(1)} %get-tuple-element.16.after_ref.tail_ref), custom_call_target="tpu_custom_call" | custom-call | tf_op jit(solution)/shard_map/pallas_call | solution.py:226
  9.7 23.5 %collective-permute-done.refs_0_ = bf16[32,1152]{1,0:T(8,128)(2,1)S(1)} collective-permute-done((bf16[32,1152]{1,0:T(8,128)(2,1)S(1)}, bf16[32,1152]{1,0:T(8,128)(2,1)S(1)}, u32[]{:S(2)}, u32[]{:S(2)}) %collective-permute-start) | collective-permute-done | bytes 73760 | tf_op jit(solution)/shard_map/ppermute | solution.py:185
  33.2 0.0 collective-permute-done.1.refs_1_
  33.2 0.0 collective-permute-done.2.refs_2_
  33.3 0.0 collective-permute-done.3.refs_3_
  33.3 1.6 %shard_map.67 = bf16[2,4,64,512]{3,2,1,0:T(8,128)(2,1)} custom-call(bf16[2,4,64,576]{3,2,1,0:T(8,128)(2,1)S(1)} %copy-done, bf16[2,4,576]{2,1,0:T(4,128)(2,1)S(1)} %copy-done.2, bf16[576,256]{1,0:T(8,128)(2,1)S(1)} %get-tuple-element.15.query_t_ref, bf16[16,576]{1,0:T(8,128)(2,1)S(1)} %get-tuple-element.16.after_ref.tail_ref, ...), custom_call_target="tpu_custom_call", output_to_operand_aliasing={{}: (8, {})} | custom-call | tf_op jit(solution)/shard_map/pallas_call | solution.py:234
  (2 shorter events, 0.0 us)
Async XLA Ops:
  0.0 0.7 %copy-start.3 = (s32[256]{0:T(256)S(1)}, s32[256]{0:T(256)}, u32[]{:S(2)}) copy-start(s32[256]{0:T(256)} %param.13) | copy-start | bytes 3076
  0.7 1.1 %copy-start = (bf16[2,4,64,576]{3,2,1,0:T(8,128)(2,1)S(1)}, bf16[2,4,64,576]{3,2,1,0:T(8,128)(2,1)}, u32[]{:S(2)}) copy-start(bf16[2,4,64,576]{3,2,1,0:T(8,128)(2,1)} %query_ref.5) | copy-start | bytes 1769476
  1.0 0.8 %copy-start.2 = (bf16[2,4,576]{2,1,0:T(4,128)(2,1)S(1)}, bf16[2,4,576]{2,1,0:T(4,128)(2,1)}, u32[]{:S(2)}) copy-start(bf16[2,4,576]{2,1,0:T(4,128)(2,1)} %step_ref.5) | copy-start | bytes 27652
  1.1 6.7 %copy-start.1 = (bf16[1,512,576]{1,2,0:T(8,128)(2,1)S(1)}, bf16[1,512,576]{1,2,0:T(8,128)(2,1)}, u32[]{:S(2)}) copy-start(bf16[1,512,576]{1,2,0:T(8,128)(2,1)} %param.10) | copy-start | bytes 1769476
  1.9 31.3 %collective-permute-start = (bf16[32,1152]{1,0:T(8,128)(2,1)S(1)}, bf16[32,1152]{1,0:T(8,128)(2,1)S(1)}, u32[]{:S(2)}, u32[]{:S(2)}) collective-permute-start(bf16[32,1152]{1,0:T(8,128)(2,1)S(1)} %get-tuple-element.17), channel_id=1, source_target_pairs={{0,320},{2,322},{4,324},{6,326},{8,328},{10,330},{12,332},{14,334}... | collective-permute-start | bytes 221192 | tf_op jit(solution)/shard_map/ppermute | solution.py:185
  3.2 30.0 %collective-permute-start.1 = (bf16[32,1152]{1,0:T(8,128)(2,1)S(1)}, bf16[32,1152]{1,0:T(8,128)(2,1)S(1)}, u32[]{:S(2)}, u32[]{:S(2)}) collective-permute-start(bf16[32,1152]{1,0:T(8,128)(2,1)S(1)} %get-tuple-element.18), channel_id=1, source_target_pairs={{0,384},{2,386},{4,388},{6,390},{8,392},{10,394},{12,396},{14,398}... | collective-permute-start | bytes 221192 | tf_op jit(solution)/shard_map/ppermute | solution.py:185
  4.5 28.7 %collective-permute-start.2 = (bf16[32,1152]{1,0:T(8,128)(2,1)S(1)}, bf16[32,1152]{1,0:T(8,128)(2,1)S(1)}, u32[]{:S(2)}, u32[]{:S(2)}) collective-permute-start(bf16[32,1152]{1,0:T(8,128)(2,1)S(1)} %get-tuple-element.19), channel_id=1, source_target_pairs={{0,449},{2,451},{4,453},{6,455},{8,457},{10,459},{12,461},{14,463}... | collective-permute-start | bytes 221192 | tf_op jit(solution)/shard_map/ppermute | solution.py:185
  5.8 27.4 %collective-permute-start.3 = (bf16[32,1152]{1,0:T(8,128)(2,1)S(1)}, bf16[32,1152]{1,0:T(8,128)(2,1)S(1)}, u32[]{:S(2)}, u32[]{:S(2)}) collective-permute-start(bf16[32,1152]{1,0:T(8,128)(2,1)S(1)} %get-tuple-element.20), channel_id=1, source_target_pairs={{0,256},{2,258},{4,260},{6,262},{8,264},{10,266},{12,268},{14,270}... | collective-permute-start | bytes 221192 | tf_op jit(solution)/shard_map/ppermute | solution.py:185

commit v10 on v8

--- a/solution.py
+++ b/solution.py
@@ -9,7 +9,7 @@
 PEERS = 32
 lap = 64
 LINE = 4
-AHEAD = ((1, 2), (2, 1), (3, 3), (0, 0))
+AHEAD = ((1, 2), (0, 1), (2, 3), (3, 0))
 
 score_scale = 192.0 ** (-0.5)
 masked_score = -1e30

time: 34.7 us -> 36.9 us (1.063)
  waiting for transfers between devices: 23.1 us -> 25.4 us
    ppermute x4, waiting for transfers between devices: 23.1 us -> 25.4 us  [along_line(): return lax.ppermute(rows, ('group', 'pair', 'z', 'x', 'y', 'tp'), pairs)]
  transfers between devices with their start and end apart: 4 -> 4, of which waited for: 1 -> 2; matrix products, arithmetic and copies ran while one was open for 0% -> 0% of each run, Pallas kernels for 6% -> 5%
where the time goes in v10:
time: 36.9 us; the launch traced here: 36.7 us
  waiting for transfers between devices  25.4 us (69%)
  starting transfers between devices  5.17 us (14%)
  Pallas kernels  3.88 us (11%)
  local copies, waits for them, and re-layouts  1.41 us (4%)
  between operations  0.75 us (2%)
    ppermute x4, waiting for transfers between devices, along_line(): return lax.ppermute(rows, ('group', 'pair', 'z', 'x', 'y', 'tp'), pairs)  25.4 us
    ppermute x4, starting transfers between devices, along_line(): return lax.ppermute(rows, ('group', 'pair', 'z', 'x', 'y', 'tp'), pairs)  5.17 us
    pallas_call x1, Pallas kernels, shards(): pl.pallas_call(resident_kernel, out_shape=out_shape, in_specs=[smem] + [v...  1.91 us
    pallas_call x1, Pallas kernels, shards(): pl.pallas_call(last_kernel, out_shape=out_shape, in_specs=[vmem] * (4 + L...  1.56 us
    unnamed x8, local copies, waits for them, and re-layouts  1.34 us
  transfers between devices with their start and end apart: 4, of which 2 were waited for; matrix products, arithmetic and copies ran while one was open for 0% of the time, Pallas kernels for 5%

profile of v10, /device:TPU:1, one launch (start us, length us, event | category | flops | bytes accessed | tf_op | source)
XLA Modules:
  0.0 36.7 jit_solution(15173273125928279343)
XLA Ops:
  0.0 0.0 copy-start.3
  0.0 0.6 %copy-done.3 = s32[256]{0:T(256)S(1)} copy-done((s32[256]{0:T(256)S(1)}, s32[256]{0:T(256)}, u32[]{:S(2)}) %copy-start.3) | copy-done | bytes 1048
  0.7 0.0 copy-start
  0.7 0.3 shard_map.64
  1.0 0.0 copy-start.2
  1.0 0.1 conditional.1
  1.0 0.1 broadcast.21
  1.1 0.0 copy-start.1
  1.1 0.7 %copy-done = bf16[2,4,64,576]{3,2,1,0:T(8,128)(2,1)S(1)} copy-done((bf16[2,4,64,576]{3,2,1,0:T(8,128)(2,1)S(1)}, bf16[2,4,64,576]{3,2,1,0:T(8,128)(2,1)}, u32[]{:S(2)}) %copy-start) | copy-done | bytes 589848
  1.8 0.0 copy-done.2
  1.8 0.1 shard_map.65
  1.9 1.3 %collective-permute-start = (bf16[32,1152]{1,0:T(8,128)(2,1)S(1)}, bf16[32,1152]{1,0:T(8,128)(2,1)S(1)}, u32[]{:S(2)}, u32[]{:S(2)}) collective-permute-start(bf16[32,1152]{1,0:T(8,128)(2,1)S(1)} %get-tuple-element.17), channel_id=1, source_target_pairs={{0,320},{2,322},{4,324},{6,326},{8,328},{10,330},{12,332},{14,334}... | collective-permute-start | bytes 221192 | tf_op jit(solution)/shard_map/ppermute | solution.py:185
  3.2 1.3 %collective-permute-start.1 = (bf16[32,1152]{1,0:T(8,128)(2,1)S(1)}, bf16[32,1152]{1,0:T(8,128)(2,1)S(1)}, u32[]{:S(2)}, u32[]{:S(2)}) collective-permute-start(bf16[32,1152]{1,0:T(8,128)(2,1)S(1)} %get-tuple-element.18), channel_id=1, source_target_pairs={{0,256},{2,258},{4,260},{6,262},{8,264},{10,266},{12,268},{14,270}... | collective-permute-start | bytes 221192 | tf_op jit(solution)/shard_map/ppermute | solution.py:185
  4.5 1.3 %collective-permute-start.2 = (bf16[32,1152]{1,0:T(8,128)(2,1)S(1)}, bf16[32,1152]{1,0:T(8,128)(2,1)S(1)}, u32[]{:S(2)}, u32[]{:S(2)}) collective-permute-start(bf16[32,1152]{1,0:T(8,128)(2,1)S(1)} %get-tuple-element.19), channel_id=1, source_target_pairs={{0,384},{2,386},{4,388},{6,390},{8,392},{10,394},{12,396},{14,398}... | collective-permute-start | bytes 221192 | tf_op jit(solution)/shard_map/ppermute | solution.py:185
  5.8 1.3 %collective-permute-start.3 = (bf16[32,1152]{1,0:T(8,128)(2,1)S(1)}, bf16[32,1152]{1,0:T(8,128)(2,1)S(1)}, u32[]{:S(2)}, u32[]{:S(2)}) collective-permute-start(bf16[32,1152]{1,0:T(8,128)(2,1)S(1)} %get-tuple-element.20), channel_id=1, source_target_pairs={{0,449},{2,451},{4,453},{6,455},{8,457},{10,459},{12,461},{14,463}... | collective-permute-start | bytes 221192 | tf_op jit(solution)/shard_map/ppermute | solution.py:185
  7.8 0.0 copy-done.1
  7.8 1.9 %shard_map.66.refs_4_ = bf16[2,4,64,512]{3,2,1,0:T(8,128)(2,1)} custom-call(s32[1]{0:T(128)S(6)} %copy.11.length_ref, bf16[2,4,64,576]{3,2,1,0:T(8,128)(2,1)S(1)} %copy-done, bf16[2,4,576]{2,1,0:T(4,128)(2,1)S(1)} %copy-done.2, bf16[1,576,512]{2,1,0:T(8,128)(2,1)S(1)} %bitcast.4, bf16[16,576]{1,0:T(8,128)(2,1)S(1)} %get-tuple-element.16.after_ref.tail_ref), custom_call_target="tpu_custom_call" | custom-call | tf_op jit(solution)/shard_map/pallas_call | solution.py:224
  9.7 23.1 %collective-permute-done.refs_0_ = bf16[32,1152]{1,0:T(8,128)(2,1)S(1)} collective-permute-done((bf16[32,1152]{1,0:T(8,128)(2,1)S(1)}, bf16[32,1152]{1,0:T(8,128)(2,1)S(1)}, u32[]{:S(2)}, u32[]{:S(2)}) %collective-permute-start) | collective-permute-done | bytes 73760 | tf_op jit(solution)/shard_map/ppermute | solution.py:185
  32.8 0.0 collective-permute-done.1.refs_1_
  32.8 2.3 %collective-permute-done.2.refs_2_ = bf16[32,1152]{1,0:T(8,128)(2,1)S(1)} collective-permute-done((bf16[32,1152]{1,0:T(8,128)(2,1)S(1)}, bf16[32,1152]{1,0:T(8,128)(2,1)S(1)}, u32[]{:S(2)}, u32[]{:S(2)}) %collective-permute-start.2) | collective-permute-done | bytes 73760 | tf_op jit(solution)/shard_map/ppermute | solution.py:185
  35.1 0.0 collective-permute-done.3.refs_3_
  35.1 1.6 %shard_map.67 = bf16[2,4,64,512]{3,2,1,0:T(8,128)(2,1)} custom-call(bf16[2,4,64,576]{3,2,1,0:T(8,128)(2,1)S(1)} %copy-done, bf16[2,4,576]{2,1,0:T(4,128)(2,1)S(1)} %copy-done.2, bf16[576,256]{1,0:T(8,128)(2,1)S(1)} %get-tuple-element.15.query_t_ref, bf16[16,576]{1,0:T(8,128)(2,1)S(1)} %get-tuple-element.16.after_ref.tail_ref, ...), custom_call_target="tpu_custom_call", output_to_operand_aliasing={{}: (8, {})} | custom-call | tf_op jit(solution)/shard_map/pallas_call | solution.py:232
  (2 shorter events, 0.0 us)
Async XLA Ops:
  0.0 0.7 %copy-start.3 = (s32[256]{0:T(256)S(1)}, s32[256]{0:T(256)}, u32[]{:S(2)}) copy-start(s32[256]{0:T(256)} %param.13) | copy-start | bytes 3076
  0.7 1.1 %copy-start = (bf16[2,4,64,576]{3,2,1,0:T(8,128)(2,1)S(1)}, bf16[2,4,64,576]{3,2,1,0:T(8,128)(2,1)}, u32[]{:S(2)}) copy-start(bf16[2,4,64,576]{3,2,1,0:T(8,128)(2,1)} %query_ref.5) | copy-start | bytes 1769476
  1.0 0.8 %copy-start.2 = (bf16[2,4,576]{2,1,0:T(4,128)(2,1)S(1)}, bf16[2,4,576]{2,1,0:T(4,128)(2,1)}, u32[]{:S(2)}) copy-start(bf16[2,4,576]{2,1,0:T(4,128)(2,1)} %step_ref.5) | copy-start | bytes 27652
  1.1 6.7 %copy-start.1 = (bf16[1,512,576]{1,2,0:T(8,128)(2,1)S(1)}, bf16[1,512,576]{1,2,0:T(8,128)(2,1)}, u32[]{:S(2)}) copy-start(bf16[1,512,576]{1,2,0:T(8,128)(2,1)} %param.10) | copy-start | bytes 1769476
  1.9 30.9 %collective-permute-start = (bf16[32,1152]{1,0:T(8,128)(2,1)S(1)}, bf16[32,1152]{1,0:T(8,128)(2,1)S(1)}, u32[]{:S(2)}, u32[]{:S(2)}) collective-permute-start(bf16[32,1152]{1,0:T(8,128)(2,1)S(1)} %get-tuple-element.17), channel_id=1, source_target_pairs={{0,320},{2,322},{4,324},{6,326},{8,328},{10,330},{12,332},{14,334}... | collective-permute-start | bytes 221192 | tf_op jit(solution)/shard_map/ppermute | solution.py:185
  3.2 29.6 %collective-permute-start.1 = (bf16[32,1152]{1,0:T(8,128)(2,1)S(1)}, bf16[32,1152]{1,0:T(8,128)(2,1)S(1)}, u32[]{:S(2)}, u32[]{:S(2)}) collective-permute-start(bf16[32,1152]{1,0:T(8,128)(2,1)S(1)} %get-tuple-element.18), channel_id=1, source_target_pairs={{0,256},{2,258},{4,260},{6,262},{8,264},{10,266},{12,268},{14,270}... | collective-permute-start | bytes 221192 | tf_op jit(solution)/shard_map/ppermute | solution.py:185
  4.5 30.6 %collective-permute-start.2 = (bf16[32,1152]{1,0:T(8,128)(2,1)S(1)}, bf16[32,1152]{1,0:T(8,128)(2,1)S(1)}, u32[]{:S(2)}, u32[]{:S(2)}) collective-permute-start(bf16[32,1152]{1,0:T(8,128)(2,1)S(1)} %get-tuple-element.19), channel_id=1, source_target_pairs={{0,384},{2,386},{4,388},{6,390},{8,392},{10,394},{12,396},{14,398}... | collective-permute-start | bytes 221192 | tf_op jit(solution)/shard_map/ppermute | solution.py:185
  5.8 29.3 %collective-permute-start.3 = (bf16[32,1152]{1,0:T(8,128)(2,1)S(1)}, bf16[32,1152]{1,0:T(8,128)(2,1)S(1)}, u32[]{:S(2)}, u32[]{:S(2)}) collective-permute-start(bf16[32,1152]{1,0:T(8,128)(2,1)S(1)} %get-tuple-element.20), channel_id=1, source_target_pairs={{0,449},{2,451},{4,453},{6,455},{8,457},{10,459},{12,461},{14,463}... | collective-permute-start | bytes 221192 | tf_op jit(solution)/shard_map/ppermute | solution.py:185

commit v11 on v8

--- a/solution.py
+++ b/solution.py
@@ -88,12 +88,20 @@
     scores = jnp.where(step <= query_step, scores, masked_score)
     expo = jnp.exp(scores - jnp.max(scores, axis=0, keepdims=True))
     total = jnp.sum(expo, axis=0, keepdims=True)
-    share = jnp.transpose(jnp.broadcast_to(1.0 / total, (8, total.shape[1])))[:, :1]
     weights = expo.astype(jnp.bfloat16)
+    step_count = query_t.shape[1] // head_count
+    step_weights = weights[base_count:].astype(jnp.float32)[: 8 - 1]
+    columns = jnp.transpose(jnp.concatenate([1.0 / total, step_weights], axis=0))
+    step_values = keys[base_count:, :KV_RANK].astype(jnp.float32)
     width = 2 * head_count
     for start in range(0, weights.shape[1], width):
-        mixed = product(weights[:, start : start + width], keys[:, :KV_RANK], ((0,), (0,)))
-        mixed = mixed * share[start : start + width]
+        own = columns[start : start + width]
+        mixed = product(
+            weights[:base_count, start : start + width], keys[:base_count, :KV_RANK], ((0,), (0,))
+        )
+        for index in range(step_count):
+            mixed = mixed + own[:, 1 + index : 2 + index] * step_values[index : index + 1]
+        mixed = mixed * own[:, :1]
         yield mixed.astype(jnp.bfloat16).reshape(-1, head_count, KV_RANK)
 
 

time: 34.7 us -> 34.6 us (level)
  no operation moved by 1% of the time
where the time goes in v11:
time: 34.6 us; the launch traced here: 34.4 us
  waiting for transfers between devices  23.1 us (67%)
  starting transfers between devices  5.17 us (15%)
  Pallas kernels  3.84 us (11%)
  local copies, waits for them, and re-layouts  1.41 us (4%)
  between operations  0.75 us (2%)
    ppermute x4, waiting for transfers between devices, along_line(): return lax.ppermute(rows, ('group', 'pair', 'z', 'x', 'y', 'tp'), pairs)  23.1 us
    ppermute x4, starting transfers between devices, along_line(): return lax.ppermute(rows, ('group', 'pair', 'z', 'x', 'y', 'tp'), pairs)  5.17 us
    pallas_call x1, Pallas kernels, shards(): pl.pallas_call(resident_kernel, out_shape=out_shape, in_specs=[smem] + [v...  1.91 us
    pallas_call x1, Pallas kernels, shards(): pl.pallas_call(last_kernel, out_shape=out_shape, in_specs=[vmem] * (4 + L...  1.53 us
    unnamed x8, local copies, waits for them, and re-layouts  1.34 us
  transfers between devices with their start and end apart: 4, of which 1 were waited for; matrix products, arithmetic and copies ran while one was open for 0% of the time, Pallas kernels for 6%

profile of v11, /device:TPU:1, one launch (start us, length us, event | category | flops | bytes accessed | tf_op | source)
XLA Modules:
  0.0 34.4 jit_solution(8785286379898446569)
XLA Ops:
  0.0 0.0 copy-start.3
  0.0 0.6 %copy-done.3 = s32[256]{0:T(256)S(1)} copy-done((s32[256]{0:T(256)S(1)}, s32[256]{0:T(256)}, u32[]{:S(2)}) %copy-start.3) | copy-done | bytes 1048
  0.7 0.0 copy-start
  0.7 0.3 shard_map.64
  1.0 0.0 copy-start.2
  1.0 0.1 conditional.1
  1.0 0.1 broadcast.21
  1.1 0.0 copy-start.1
  1.1 0.7 %copy-done = bf16[2,4,64,576]{3,2,1,0:T(8,128)(2,1)S(1)} copy-done((bf16[2,4,64,576]{3,2,1,0:T(8,128)(2,1)S(1)}, bf16[2,4,64,576]{3,2,1,0:T(8,128)(2,1)}, u32[]{:S(2)}) %copy-start) | copy-done | bytes 589848
  1.8 0.0 copy-done.2
  1.8 0.1 shard_map.65
  1.9 1.3 %collective-permute-start = (bf16[32,1152]{1,0:T(8,128)(2,1)S(1)}, bf16[32,1152]{1,0:T(8,128)(2,1)S(1)}, u32[]{:S(2)}, u32[]{:S(2)}) collective-permute-start(bf16[32,1152]{1,0:T(8,128)(2,1)S(1)} %get-tuple-element.17), channel_id=1, source_target_pairs={{0,320},{2,322},{4,324},{6,326},{8,328},{10,330},{12,332},{14,334}... | collective-permute-start | bytes 221192 | tf_op jit(solution)/shard_map/ppermute | solution.py:193
  3.2 1.3 %collective-permute-start.1 = (bf16[32,1152]{1,0:T(8,128)(2,1)S(1)}, bf16[32,1152]{1,0:T(8,128)(2,1)S(1)}, u32[]{:S(2)}, u32[]{:S(2)}) collective-permute-start(bf16[32,1152]{1,0:T(8,128)(2,1)S(1)} %get-tuple-element.18), channel_id=1, source_target_pairs={{0,384},{2,386},{4,388},{6,390},{8,392},{10,394},{12,396},{14,398}... | collective-permute-start | bytes 221192 | tf_op jit(solution)/shard_map/ppermute | solution.py:193
  4.5 1.3 %collective-permute-start.2 = (bf16[32,1152]{1,0:T(8,128)(2,1)S(1)}, bf16[32,1152]{1,0:T(8,128)(2,1)S(1)}, u32[]{:S(2)}, u32[]{:S(2)}) collective-permute-start(bf16[32,1152]{1,0:T(8,128)(2,1)S(1)} %get-tuple-element.19), channel_id=1, source_target_pairs={{0,449},{2,451},{4,453},{6,455},{8,457},{10,459},{12,461},{14,463}... | collective-permute-start | bytes 221192 | tf_op jit(solution)/shard_map/ppermute | solution.py:193
  5.8 1.3 %collective-permute-start.3 = (bf16[32,1152]{1,0:T(8,128)(2,1)S(1)}, bf16[32,1152]{1,0:T(8,128)(2,1)S(1)}, u32[]{:S(2)}, u32[]{:S(2)}) collective-permute-start(bf16[32,1152]{1,0:T(8,128)(2,1)S(1)} %get-tuple-element.20), channel_id=1, source_target_pairs={{0,256},{2,258},{4,260},{6,262},{8,264},{10,266},{12,268},{14,270}... | collective-permute-start | bytes 221192 | tf_op jit(solution)/shard_map/ppermute | solution.py:193
  7.8 0.0 copy-done.1
  7.8 1.9 %shard_map.66.refs_4_ = bf16[2,4,64,512]{3,2,1,0:T(8,128)(2,1)} custom-call(s32[1]{0:T(128)S(6)} %copy.11.length_ref, bf16[2,4,64,576]{3,2,1,0:T(8,128)(2,1)S(1)} %copy-done, bf16[2,4,576]{2,1,0:T(4,128)(2,1)S(1)} %copy-done.2, bf16[1,576,512]{2,1,0:T(8,128)(2,1)S(1)} %bitcast.4, bf16[16,576]{1,0:T(8,128)(2,1)S(1)} %get-tuple-element.16.after_ref.tail_ref), custom_call_target="tpu_custom_call" | custom-call | tf_op jit(solution)/shard_map/pallas_call | solution.py:232
  9.7 23.1 %collective-permute-done.refs_0_ = bf16[32,1152]{1,0:T(8,128)(2,1)S(1)} collective-permute-done((bf16[32,1152]{1,0:T(8,128)(2,1)S(1)}, bf16[32,1152]{1,0:T(8,128)(2,1)S(1)}, u32[]{:S(2)}, u32[]{:S(2)}) %collective-permute-start) | collective-permute-done | bytes 73760 | tf_op jit(solution)/shard_map/ppermute | solution.py:193
  32.8 0.0 collective-permute-done.1.refs_1_
  32.8 0.0 collective-permute-done.2.refs_2_
  32.8 0.0 collective-permute-done.3.refs_3_
  32.8 1.5 %shard_map.67 = bf16[2,4,64,512]{3,2,1,0:T(8,128)(2,1)} custom-call(bf16[2,4,64,576]{3,2,1,0:T(8,128)(2,1)S(1)} %copy-done, bf16[2,4,576]{2,1,0:T(4,128)(2,1)S(1)} %copy-done.2, bf16[576,256]{1,0:T(8,128)(2,1)S(1)} %get-tuple-element.15.query_t_ref, bf16[16,576]{1,0:T(8,128)(2,1)S(1)} %get-tuple-element.16.after_ref.tail_ref, ...), custom_call_target="tpu_custom_call", output_to_operand_aliasing={{}: (8, {})} | custom-call | tf_op jit(solution)/shard_map/pallas_call | solution.py:240
  (2 shorter events, 0.0 us)
Async XLA Ops:
  0.0 0.7 %copy-start.3 = (s32[256]{0:T(256)S(1)}, s32[256]{0:T(256)}, u32[]{:S(2)}) copy-start(s32[256]{0:T(256)} %param.13) | copy-start | bytes 3076
  0.7 1.1 %copy-start = (bf16[2,4,64,576]{3,2,1,0:T(8,128)(2,1)S(1)}, bf16[2,4,64,576]{3,2,1,0:T(8,128)(2,1)}, u32[]{:S(2)}) copy-start(bf16[2,4,64,576]{3,2,1,0:T(8,128)(2,1)} %query_ref.5) | copy-start | bytes 1769476
  1.0 0.8 %copy-start.2 = (bf16[2,4,576]{2,1,0:T(4,128)(2,1)S(1)}, bf16[2,4,576]{2,1,0:T(4,128)(2,1)}, u32[]{:S(2)}) copy-start(bf16[2,4,576]{2,1,0:T(4,128)(2,1)} %step_ref.5) | copy-start | bytes 27652
  1.1 6.7 %copy-start.1 = (bf16[1,512,576]{1,2,0:T(8,128)(2,1)S(1)}, bf16[1,512,576]{1,2,0:T(8,128)(2,1)}, u32[]{:S(2)}) copy-start(bf16[1,512,576]{1,2,0:T(8,128)(2,1)} %param.10) | copy-start | bytes 1769476
  1.9 30.9 %collective-permute-start = (bf16[32,1152]{1,0:T(8,128)(2,1)S(1)}, bf16[32,1152]{1,0:T(8,128)(2,1)S(1)}, u32[]{:S(2)}, u32[]{:S(2)}) collective-permute-start(bf16[32,1152]{1,0:T(8,128)(2,1)S(1)} %get-tuple-element.17), channel_id=1, source_target_pairs={{0,320},{2,322},{4,324},{6,326},{8,328},{10,330},{12,332},{14,334}... | collective-permute-start | bytes 221192 | tf_op jit(solution)/shard_map/ppermute | solution.py:193
  3.2 29.6 %collective-permute-start.1 = (bf16[32,1152]{1,0:T(8,128)(2,1)S(1)}, bf16[32,1152]{1,0:T(8,128)(2,1)S(1)}, u32[]{:S(2)}, u32[]{:S(2)}) collective-permute-start(bf16[32,1152]{1,0:T(8,128)(2,1)S(1)} %get-tuple-element.18), channel_id=1, source_target_pairs={{0,384},{2,386},{4,388},{6,390},{8,392},{10,394},{12,396},{14,398}... | collective-permute-start | bytes 221192 | tf_op jit(solution)/shard_map/ppermute | solution.py:193
  4.5 28.3 %collective-permute-start.2 = (bf16[32,1152]{1,0:T(8,128)(2,1)S(1)}, bf16[32,1152]{1,0:T(8,128)(2,1)S(1)}, u32[]{:S(2)}, u32[]{:S(2)}) collective-permute-start(bf16[32,1152]{1,0:T(8,128)(2,1)S(1)} %get-tuple-element.19), channel_id=1, source_target_pairs={{0,449},{2,451},{4,453},{6,455},{8,457},{10,459},{12,461},{14,463}... | collective-permute-start | bytes 221192 | tf_op jit(solution)/shard_map/ppermute | solution.py:193
  5.8 27.0 %collective-permute-start.3 = (bf16[32,1152]{1,0:T(8,128)(2,1)S(1)}, bf16[32,1152]{1,0:T(8,128)(2,1)S(1)}, u32[]{:S(2)}, u32[]{:S(2)}) collective-permute-start(bf16[32,1152]{1,0:T(8,128)(2,1)S(1)} %get-tuple-element.20), channel_id=1, source_target_pairs={{0,256},{2,258},{4,260},{6,262},{8,264},{10,266},{12,268},{14,270}... | collective-permute-start | bytes 221192 | tf_op jit(solution)/shard_map/ppermute | solution.py:193
